TPU v7x, 32 devices: a whole 2x2x4 slice. The times are simulated.
32 devices in a mesh: dp: 8 (over z, y), tensor: 4 (over x, core).
Axes of the slice: x: 2, y: 2, z: 4, core: 2. Of those that a mesh axis runs over, the one named last changes fastest.
Arguments:
- tokens: bfloat16 [16384, 1024], P(('dp', 'tensor')), may hold values from -6 to 6
- segments: int32 [16384], P('dp'), may hold values from 0 to 31, never falling along the last dimension, each value on 1 to 2048 neighbouring positions
- cotangent: bfloat16 [16384, 1024], P(('dp', 'tensor')), may hold values from -12 to 12
- qkv_weight: bfloat16 [1024, 2048], P(None, 'tensor'), may hold values from -0.1875 to 0.1875
- out_weight: bfloat16 [1024, 1024], P('tensor'), may hold values from -1.5 to 1.5
- gate_up_weight: bfloat16 [1024, 2, 4608], P(None, None, 'tensor'), may hold values from -0.1875 to 0.1875
- down_weight: bfloat16 [4608, 1024], P('tensor'), may hold values from -0.09375 to 0.09375
- qkv_master: float32 [1024, 2048], P('dp', 'tensor'), may hold values from -0.1875 to 0.1875
- out_master: float32 [1024, 1024], P('tensor', 'dp'), may hold values from -1.5 to 1.5
- gate_up_master: float32 [1024, 2, 4608], P('dp', None, 'tensor'), may hold values from -0.1875 to 0.1875
- down_master: float32 [4608, 1024], P('tensor', 'dp'), may hold values from -0.09375 to 0.09375
- qkv_mean: float32 [1024, 2048], P('dp', 'tensor'), may hold values from -0.00036621094 to 0.00036621094
- out_mean: float32 [1024, 1024], P('tensor', 'dp'), may hold values from -0.00015258789 to 0.00015258789
- gate_up_mean: float32 [1024, 2, 4608], P('dp', None, 'tensor'), may hold values from -0.00036621094 to 0.00036621094
- down_mean: float32 [4608, 1024], P('tensor', 'dp'), may hold values from -0.00036621094 to 0.00036621094
- qkv_square: float32 [1024, 2048], P('dp', 'tensor'), may hold values from 2.889922e-09 to 1.1559688e-08
- out_square: float32 [1024, 1024], P('tensor', 'dp'), may hold values from 3.4679065e-10 to 1.3871626e-09
- gate_up_square: float32 [1024, 2, 4608], P('dp', None, 'tensor'), may hold values from 2.889922e-09 to 1.1559688e-08
- down_square: float32 [4608, 1024], P('tensor', 'dp'), may hold values from 2.889922e-09 to 1.1559688e-08
- gains: float32 [2176], replicated, may hold values from 0.5 to 9
- gains_mean: float32 [2176], replicated, may hold values from -0.0014648438 to 0.0014648438
- gains_square: float32 [2176], replicated, may hold values from 4.6238753e-08 to 1.8495501e-07
Outputs:
- result: bfloat16 [16384, 1024], P(('dp', 'tensor'))
- input_grad: bfloat16 [16384, 1024], P(('dp', 'tensor'))
- grad_norm: float32 [], replicated
- qkv_new: float32 [1024, 2048], P('dp', 'tensor')
- qkv_copy: bfloat16 [1024, 2048], P('dp', 'tensor')
- qkv_mean_new: float32 [1024, 2048], P('dp', 'tensor')
- qkv_square_new: float32 [1024, 2048], P('dp', 'tensor')
- out_new: float32 [1024, 1024], P('tensor', 'dp')
- out_copy: bfloat16 [1024, 1024], P('tensor', 'dp')
- out_mean_new: float32 [1024, 1024], P('tensor', 'dp')
- out_square_new: float32 [1024, 1024], P('tensor', 'dp')
- gate_up_new: float32 [1024, 2, 4608], P('dp', None, 'tensor')
- gate_up_copy: bfloat16 [1024, 2, 4608], P('dp', None, 'tensor')
- gate_up_mean_new: float32 [1024, 2, 4608], P('dp', None, 'tensor')
- gate_up_square_new: float32 [1024, 2, 4608], P('dp', None, 'tensor')
- down_new: float32 [4608, 1024], P('tensor', 'dp')
- down_copy: bfloat16 [4608, 1024], P('tensor', 'dp')
- down_mean_new: float32 [4608, 1024], P('tensor', 'dp')
- down_square_new: float32 [4608, 1024], P('tensor', 'dp')
- gains_new: float32 [2176], replicated
- gains_mean_new: float32 [2176], replicated
- gains_square_new: float32 [2176], replicated
Inputs may be any that keep to these rules, and one draw needn't show every extreme that they name: `segments`: document numbers never fall along the tokens; a document holds 1 to 2048 tokens and one holds exactly 2048.
All inputs are finite; a program needn't handle non-finite values.
Results may differ from a plain program's by a relative error of at most 0.028.
Values may be sent and summed in bfloat16 or wider, within the bound.
No kernel may reach another device: no remote copies, remote signals or barrier semaphores. Data moves between devices by JAX's collectives and lax.ppermute only.
A program may use at most 192 MiB of HBM per device.

v0:
```python
import jax
import jax.numpy as jnp
from jax import lax
from jax.experimental import pallas as pl
from jax.experimental.pallas import tpu as pltpu
from jax.sharding import PartitionSpec as P

QH = 16
KVH = 8
HD = 64
STEP = 5


NORM_EPS = 1e-06
ROPE_BASE = 1000000.0
CLIP_NORM = 1.0
BETA_ONE = 0.9
BETA_TWO = 0.95
ADAM_EPS = 1e-08
DECAY = 0.1
RATE_WEIGHT = 0.02
RATE_GAIN = 1.5
MASKED = -1e30

KINDS = QH // KVH + 2
RATIO = QH // KVH
PARTS = 2
PIECES = 4
HALVES = 2
CORE = 1
ACROSS = 2
MIB = 1024 * 1024


def params(limit=60):
    return pltpu.CompilerParams(vmem_limit_bytes=limit * MIB)


def cost(flops, size):
    return pl.CostEstimate(flops=flops // 8, bytes_accessed=size // 8, transcendentals=0)


def starts_of(seg):
    index = jnp.arange(seg.shape[0], dtype=jnp.int32)
    flag = (index == 0) | (seg != jnp.roll(seg, 1))
    return lax.cummax(jnp.where(flag, index, 0), axis=0)


def rotary(position):
    half = HD // 2
    freq = ROPE_BASE ** (-(jnp.arange(half, dtype=jnp.float32) * 2.0 / HD))
    angle = freq[:, None] * position[None, :]
    return (jnp.cos(angle), jnp.sin(angle))


def dot_nn(left, right):
    return lax.dot_general(
        left, right, (((1,), (0,)), ((), ())), preferred_element_type=jnp.float32
    )


def dot_nt(left, right):
    return lax.dot_general(
        left, right, (((1,), (1,)), ((), ())), preferred_element_type=jnp.float32
    )


def contract_rows(left, right):
    return lax.dot_general(
        left, right, (((0,), (0,)), ((), ())), preferred_element_type=jnp.float32
    )


def rotate(value, cosine, sine):
    half = value.shape[0] // 2
    first, second = (value[:half], value[half:])
    return jnp.concatenate(
        [first * cosine - second * sine, second * cosine + first * sine], axis=0
    )


def rotate_back(grad, cosine, sine):
    half = grad.shape[0] // 2
    first, second = (grad[:half], grad[half:])
    return jnp.concatenate(
        [first * cosine + second * sine, second * cosine - first * sine], axis=0
    )


def row_scale(value):
    return lax.rsqrt(jnp.mean(value * value, axis=-1, keepdims=True) + NORM_EPS)


def head_scale(value):
    return lax.rsqrt(jnp.mean(value * value, axis=0, keepdims=True) + NORM_EPS)


def project_kernel(place_ref, *refs):
    pieces = refs[:2]
    pre_ref, weight_ref, gain_ref, cos_ref, sin_ref = refs[2:7]
    normed_ref, raw_ref, flip_ref, row_ref = refs[-4:]
    step = pl.program_id(0)
    for r in range(2):

        @pl.when(step // PARTS == r)
        def _(r=r):
            value = pieces[r][...].astype(jnp.float32)
            normed_ref[...] = (value * row_scale(value) * pre_ref[...]).astype(jnp.bfloat16)

    joint = dot_nt(weight_ref[...], normed_ref[...])
    cosine, sine = cos_ref[...], sin_ref[...]
    for slot in range(raw_ref.shape[0]):
        kind = slot % KINDS
        raw = joint[slot * HD : (slot + 1) * HD]
        raw_ref[slot] = raw
        value = raw
        if kind < KINDS - 1:
            gain = gain_ref[:, 1:2] if kind == KINDS - 2 else gain_ref[:, 0:1]
            value = rotate(raw * head_scale(raw) * gain, cosine, sine)
        if kind < KINDS - 2:
            value = value * HD ** (-0.5)
        low = value.astype(jnp.bfloat16)
        flip_ref[slot] = low
        row_ref[slot] = low.T


def project(far, earlier, place, pieces, pre_gain, weight_rows, head_gains, cos_table, sin_table):
    rows, width = pieces[0].shape
    length = rows * PIECES
    block = rows // PARTS
    slots = weight_rows.shape[0] // HD
    at = lambda i, p: PARTS * ((i // PARTS + 2 * far) ^ p[0]) + i % PARTS

    def piece(r):
        return pl.BlockSpec(
            (block, width), lambda i, p: (jnp.clip(i - PARTS * r, 0, PARTS - 1), 0)
        )

    return pl.pallas_call(
        project_kernel,
        grid_spec=pltpu.PrefetchScalarGridSpec(
            num_scalar_prefetch=1,
            grid=(2 * PARTS,),
            in_specs=[piece(0), piece(1)]
            + [
                pl.BlockSpec(pre_gain.shape, lambda i, p: (0, 0)),
                pl.BlockSpec(weight_rows.shape, lambda i, p: (0, 0)),
                pl.BlockSpec(head_gains.shape, lambda i, p: (0, 0)),
                pl.BlockSpec((HD // 2, block), lambda i, p: (0, at(i, p))),
                pl.BlockSpec((HD // 2, block), lambda i, p: (0, at(i, p))),
            ]
            + [pl.BlockSpec(memory_space=pl.ANY)] * len(earlier),
            out_specs=[
                pl.BlockSpec((block, width), lambda i, p: (at(i, p), 0)),
                pl.BlockSpec((slots, HD, block), lambda i, p: (0, 0, at(i, p))),
                pl.BlockSpec((slots, HD, block), lambda i, p: (0, 0, at(i, p))),
                pl.BlockSpec((slots, block, HD), lambda i, p: (0, at(i, p), 0)),
            ],
        ),
        out_shape=[
            jax.ShapeDtypeStruct((length, width), jnp.bfloat16),
            jax.ShapeDtypeStruct((slots, HD, length), jnp.float32),
            jax.ShapeDtypeStruct((slots, HD, length), jnp.bfloat16),
            jax.ShapeDtypeStruct((slots, length, HD), jnp.bfloat16),
        ],
        input_output_aliases={8 + k: k for k in range(len(earlier))},
        compiler_params=params(),
        cost_estimate=cost(length * width * slots * HD, 8 * MIB),
        name="project",
    )(place, *pieces, pre_gain, weight_rows, head_gains, cos_table, sin_table, *earlier)


def mask_of(start_row, first_key, first_query, keys):
    queries = start_row.shape[1]
    key = first_key + lax.broadcasted_iota(jnp.int32, (keys, 1), 0)
    query = first_query + lax.broadcasted_iota(jnp.int32, (1, queries), 1)
    return (key >= start_row) & (key <= query)


def over_keys(one, first, last, at_query, block):
    begin = first // block
    whole = jnp.maximum(begin, jnp.minimum((last + block - 1) // block, at_query))
    pairs = (at_query - whole) // 2
    lax.fori_loop(begin, whole, lambda j, carry: one(True, j * block, block), None)
    lax.fori_loop(
        0, pairs, lambda k, carry: one(False, (whole + 2 * k) * block, 2 * block), None
    )
    lax.fori_loop(
        whole + 2 * pairs, at_query, lambda j, carry: one(False, j * block, block), None
    )
    one(True, at_query * block, block)


def attend_kernel(half, first_ref, last_ref, place_ref, *refs):
    query_ref, key_ref, value_ref, start_ref, weight_ref = refs[:5]
    context_ref, flip_ref, log_ref, send_ref, keep_ref, top_ref, total_ref, sum_ref = refs[-8:]
    groups, ratio = query_ref.shape[:2]
    block = start_ref.shape[1]
    step = pl.program_id(0)
    at_query = HALVES * (step ^ place_ref[0]) + half
    start_row = start_ref[...]
    queries = [
        jnp.concatenate([query_ref[g, h] for h in range(ratio)], axis=1) for g in range(groups)
    ]
    top_ref[...] = jnp.full_like(top_ref, MASKED)
    total_ref[...] = jnp.zeros_like(total_ref)
    sum_ref[...] = jnp.zeros_like(sum_ref)

    def one(masked, at, size):
        at = pl.multiple_of(at, block)
        if masked:
            mask = mask_of(start_row, at, at_query * block, size)
            mask = jnp.concatenate([mask] * ratio, axis=1)
        for g in range(groups):
            scores = dot_nn(key_ref[g, pl.ds(at, size), :], queries[g])
            if masked:
                scores = jnp.where(mask, scores, MASKED)
            top_old = top_ref[g]
            top = jnp.maximum(top_old, jnp.max(scores, axis=0, keepdims=True))
            expo = jnp.exp(scores - top)
            fade = jnp.exp(top_old - top)
            top_ref[g] = top
            total_ref[g] = total_ref[g] * fade + jnp.sum(expo, axis=0, keepdims=True)
            part = dot_nn(value_ref[g, :, pl.ds(at, size)], expo.astype(jnp.bfloat16))
            sum_ref[g] = sum_ref[g] * fade + part

    over_keys(one, first_ref[at_query], last_ref[at_query], at_query, block)
    wide = ratio * HD
    for g in range(groups):
        total = total_ref[g]
        output = sum_ref[g] / total
        both = jnp.concatenate(
            [output[:, h * block : (h + 1) * block] for h in range(ratio)], axis=0
        )
        flip_ref[g * wide : (g + 1) * wide, :] = both.astype(jnp.bfloat16)
        context_ref[:, g * wide : (g + 1) * wide] = both.T.astype(jnp.bfloat16)
        log_total = top_ref[g] + jnp.log(total)
        for h in range(ratio):
            log_ref[g, h] = log_total[:, h * block : (h + 1) * block]
    part = dot_nn(context_ref[...], weight_ref[...]).astype(jnp.bfloat16)

    @pl.when(step % 2 == 1)
    def _():
        send_ref[...] = part

    @pl.when(step % 2 == 0)
    def _():
        keep_ref[...] = part


def attend(half, earlier, place, flipped, rows, starts, weight):
    slots, _, length = flipped.shape
    groups = slots // KINDS
    block = length // PIECES // HALVES
    width = weight.shape[1]
    wide = groups * RATIO * HD
    at = lambda i, p: HALVES * (i ^ p[0]) + half
    flip_four = flipped.reshape(groups, KINDS, HD, length)
    row_four = rows.reshape(groups, KINDS, length, HD)
    out = jax.ShapeDtypeStruct((PIECES // 2, block, width), jnp.bfloat16)
    outs = pl.pallas_call(
        lambda *refs: attend_kernel(half, *refs),
        grid_spec=pltpu.PrefetchScalarGridSpec(
            num_scalar_prefetch=3,
            grid=(PIECES,),
            in_specs=[
                pl.BlockSpec((groups, RATIO, HD, block), lambda i, f, l, p: (0, 0, 0, at(i, p))),
                pl.BlockSpec((groups, None, length, HD), lambda i, f, l, p: (0, RATIO, 0, 0)),
                pl.BlockSpec((groups, None, HD, length), lambda i, f, l, p: (0, RATIO + 1, 0, 0)),
                pl.BlockSpec((1, block), lambda i, f, l, p: (0, at(i, p))),
                pl.BlockSpec(weight.shape, lambda i, f, l, p: (0, 0)),
            ]
            + [pl.BlockSpec(memory_space=pl.ANY)] * len(earlier),
            out_specs=[
                pl.BlockSpec((block, wide), lambda i, f, l, p: (at(i, p), 0)),
                pl.BlockSpec((wide, block), lambda i, f, l, p: (0, at(i, p))),
                pl.BlockSpec((groups, RATIO, 1, block), lambda i, f, l, p: (0, 0, 0, at(i, p))),
                pl.BlockSpec((None, block, width), lambda i, f, l, p: (i // 2, 0, 0)),
                pl.BlockSpec((None, block, width), lambda i, f, l, p: (i // 2, 0, 0)),
            ],
            scratch_shapes=[
                pltpu.VMEM((groups, 1, RATIO * block), jnp.float32),
                pltpu.VMEM((groups, 1, RATIO * block), jnp.float32),
                pltpu.VMEM((groups, HD, RATIO * block), jnp.float32),
            ],
        ),
        out_shape=[
            jax.ShapeDtypeStruct((length, wide), jnp.bfloat16),
            jax.ShapeDtypeStruct((wide, length), jnp.bfloat16),
            jax.ShapeDtypeStruct((groups, RATIO, 1, length), jnp.float32),
            out,
            out,
        ],
        input_output_aliases={8 + k: k for k in range(len(earlier))},
        compiler_params=params(),
        cost_estimate=cost(8 * groups * length * length * 64, 6 * MIB),
        name="attend",
    )(
        starts[::block], starts[block - 1 :: block], place, flip_four, row_four, flip_four,
        starts[None, :], weight, *earlier,
    )
    return (outs[:3], outs[3], outs[4])


def attend_back_kernel(pieces, first_ref, last_ref, place_ref, *refs):
    (query_ref, query_row_ref, key_ref, key_row_ref, value_row_ref, context_ref, log_ref,
     start_ref, weight_ref, raw_ref, raw_key_ref, cos_ref, sin_ref, gain_ref) = refs[:14]
    dh_pieces = refs[14 : 14 + pieces]
    if pieces > 1:
        joint_ref, gain_grad_ref, dh_ref = refs[14 + pieces : 17 + pieces]
    else:
        joint_ref, gain_grad_ref = refs[14 + pieces : 16 + pieces]
        dh_ref = dh_pieces[0]
    query_sum, key_sum, value_sum, query_gain_sum = refs[-4:]
    block = start_ref.shape[1]
    step = pl.program_id(0)
    steps = pl.num_programs(0)
    ratio = query_ref.shape[0]
    wide = ratio * HD

    @pl.when(step == 0)
    def _():
        key_sum[...] = jnp.zeros_like(key_sum)
        value_sum[...] = jnp.zeros_like(value_sum)
        query_gain_sum[...] = jnp.zeros_like(query_gain_sum)

    if pieces > 1:
        source = HALVES * ((step // HALVES) ^ place_ref[0]) + step % HALVES
        for r, piece in enumerate(dh_pieces):

            @pl.when(source == r)
            def _(piece=piece):
                dh_ref[...] = piece[...]

    query = jnp.concatenate([query_ref[h] for h in range(ratio)], axis=1)
    query_row = jnp.concatenate([query_row_ref[h] for h in range(ratio)], axis=0)
    start_row = start_ref[...]
    grad_wide = dot_nt(weight_ref[...], dh_ref[...]).astype(jnp.bfloat16)
    grad_float = grad_wide.astype(jnp.float32)
    products = grad_float * context_ref[...].astype(jnp.float32)
    delta = jnp.concatenate(
        [
            jnp.sum(products[h * HD : (h + 1) * HD], axis=0, keepdims=True)
            for h in range(ratio)
        ],
        axis=1,
    )
    grad = jnp.concatenate([grad_wide[h * HD : (h + 1) * HD] for h in range(ratio)], axis=1)
    turned = grad_float.T.astype(jnp.bfloat16)
    grad_row = jnp.concatenate([turned[:, h * HD : (h + 1) * HD] for h in range(ratio)], axis=0)
    log_total = jnp.concatenate([log_ref[h] for h in range(ratio)], axis=1)
    query_sum[...] = jnp.zeros_like(query_sum)

    def one(masked, at, size):
        at = pl.multiple_of(at, block)
        here = pl.ds(at, size)
        probs = jnp.exp(dot_nn(key_row_ref[here, :], query) - log_total)
        if masked:
            mask = mask_of(start_row, at, step * block, size)
            probs = jnp.where(jnp.concatenate([mask] * ratio, axis=1), probs, 0.0)
        prob_grad = dot_nn(value_row_ref[here, :], grad)
        score_grad = (probs * (prob_grad - delta)).astype(jnp.bfloat16)
        value_sum[here, :] += dot_nn(probs.astype(jnp.bfloat16), grad_row)
        key_sum[here, :] += dot_nn(score_grad, query_row)
        query_sum[...] += dot_nn(key_ref[:, here], score_grad)

    over_keys(one, first_ref[step], last_ref[step], step, block)

    def unwind(part, raw, cosine, sine, gain):
        inverse = head_scale(raw)
        back = rotate_back(part, cosine, sine)
        scaled = back * gain
        lean = jnp.mean(scaled * raw, axis=0, keepdims=True)
        return (back * raw * inverse, inverse * scaled - raw * inverse**3 * lean)

    at = pl.multiple_of(step * block, block)
    here = pl.ds(at, block)
    outs = []
    for h in range(ratio):
        part = query_sum[:, h * block : (h + 1) * block] * HD ** (-0.5)
        gain_part, out = unwind(
            part, raw_ref[h], cos_ref[:, here], sin_ref[:, here], gain_ref[:, 0:1]
        )
        query_gain_sum[...] += gain_part
        outs.append(out)
    joint_ref[here, :wide] = jnp.concatenate(outs, axis=0).T.astype(jnp.bfloat16)

    @pl.when(step == steps - 1)
    def _():
        def one_key(j, total):
            at = pl.multiple_of(j * block, block)
            here = pl.ds(at, block)
            pair = jnp.concatenate([key_sum[here, :], value_sum[here, :]], axis=1).T
            gain_part, out = unwind(
                pair[:HD], raw_key_ref[:, here], cos_ref[:, here], sin_ref[:, here],
                gain_ref[:, 1:2],
            )
            both = jnp.concatenate([out, pair[HD:]], axis=0)
            joint_ref[here, wide:] = both.T.astype(jnp.bfloat16)
            return total + gain_part

        key_gain_sum = lax.fori_loop(
            0, steps, one_key, jnp.zeros(query_gain_sum.shape, jnp.float32)
        )
        both = jnp.concatenate([query_gain_sum[...], key_gain_sum], axis=0).T
        gain_grad_ref[...] = jnp.sum(both, axis=0, keepdims=True)


def attend_back(
    g, place, flipped, rows, context_flip, log_total, starts, dh, weight, raw, tables, head_gains
):
    slots, _, length = flipped.shape
    groups = slots // KINDS
    ratio = RATIO
    block = length // PIECES // HALVES
    wide = ratio * HD
    width = weight.shape[1]
    pieces = len(dh)
    flip_four = flipped.reshape(groups, KINDS, HD, length)
    row_four = rows.reshape(groups, KINDS, length, HD)
    raw_four = raw.reshape(groups, KINDS, HD, length)
    by_step = pl.BlockSpec((block, width), lambda i, f, l, p: (i, 0))
    whole = pl.BlockSpec((block, width), lambda i, f, l, p: (0, 0))
    outs = pl.pallas_call(
        lambda *refs: attend_back_kernel(pieces, *refs),
        grid_spec=pltpu.PrefetchScalarGridSpec(
            num_scalar_prefetch=3,
            grid=(length // block,),
            in_specs=[
                pl.BlockSpec((None, ratio, HD, block), lambda i, f, l, p: (g, 0, 0, i)),
                pl.BlockSpec((None, ratio, block, HD), lambda i, f, l, p: (g, 0, i, 0)),
                pl.BlockSpec((None, None, HD, length), lambda i, f, l, p: (g, ratio, 0, 0)),
                pl.BlockSpec((None, None, length, HD), lambda i, f, l, p: (g, ratio, 0, 0)),
                pl.BlockSpec((None, None, length, HD), lambda i, f, l, p: (g, ratio + 1, 0, 0)),
                pl.BlockSpec((wide, block), lambda i, f, l, p: (g, i)),
                pl.BlockSpec((None, ratio, 1, block), lambda i, f, l, p: (g, 0, 0, i)),
                pl.BlockSpec((1, block), lambda i, f, l, p: (0, i)),
                pl.BlockSpec((wide, width), lambda i, f, l, p: (g, 0)),
                pl.BlockSpec((None, ratio, HD, block), lambda i, f, l, p: (g, 0, 0, i)),
                pl.BlockSpec((None, None, HD, length), lambda i, f, l, p: (g, ratio, 0, 0)),
                pl.BlockSpec((HD // 2, length), lambda i, f, l, p: (0, 0)),
                pl.BlockSpec((HD // 2, length), lambda i, f, l, p: (0, 0)),
                pl.BlockSpec(head_gains.shape, lambda i, f, l, p: (0, 0)),
            ]
            + [whole if pieces > 1 else by_step] * pieces,
            out_specs=[
                pl.BlockSpec((length, wide + 2 * HD), lambda i, f, l, p: (0, 0)),
                pl.BlockSpec((1, 2 * HD), lambda i, f, l, p: (0, 0)),
            ]
            + [by_step] * (pieces > 1),
            scratch_shapes=[
                pltpu.VMEM((HD, ratio * block), jnp.float32),
                pltpu.VMEM((length, HD), jnp.float32),
                pltpu.VMEM((length, HD), jnp.float32),
                pltpu.VMEM((HD, block), jnp.float32),
            ],
        ),
        out_shape=[
            jax.ShapeDtypeStruct((length, wide + 2 * HD), jnp.bfloat16),
            jax.ShapeDtypeStruct((1, 2 * HD), jnp.float32),
        ]
        + [jax.ShapeDtypeStruct((length, width), jnp.bfloat16)] * (pieces > 1),
        compiler_params=params(),
        cost_estimate=cost(20 * length * length * 128, 12 * MIB),
        name="attend_back",
    )(
        starts[::block], starts[block - 1 :: block], place, flip_four, row_four, flip_four, row_four, row_four, context_flip,
        log_total, starts[None, :], weight, raw_four, raw_four, tables[0], tables[1],
        head_gains, *dh,
    )
    return outs


def spread_kernel(groups, place_ref, *refs):
    send_rows, keep_rows = refs[:groups], refs[groups : 2 * groups]
    weight_ref, send_out, keep_out = refs[2 * groups :]
    depth = weight_ref.shape[0] // groups
    for rows, out in ((send_rows, send_out), (keep_rows, keep_out)):
        joined = jnp.concatenate([row[...] for row in rows], axis=1)
        out[...] = dot_nn(joined, weight_ref[...]).astype(jnp.bfloat16)


def spread(place, rows, weight):
    groups = len(rows)
    length, depth = rows[0].shape
    width = weight.shape[1]
    block = length // PIECES
    out = jax.ShapeDtypeStruct((PIECES // 2, block, width), jnp.bfloat16)
    return pl.pallas_call(
        lambda *refs: spread_kernel(groups, *refs),
        grid_spec=pltpu.PrefetchScalarGridSpec(
            num_scalar_prefetch=1,
            grid=(PIECES // 2,),
            in_specs=[pl.BlockSpec((block, depth), lambda i, p: ((2 * i + 1) ^ p[0], 0))] * groups
            + [pl.BlockSpec((block, depth), lambda i, p: ((2 * i) ^ p[0], 0))] * groups
            + [pl.BlockSpec(weight.shape, lambda i, p: (0, 0))],
            out_specs=[pl.BlockSpec((None, block, width), lambda i, p: (i, 0, 0))] * 2,
        ),
        out_shape=[out, out],
        compiler_params=params(),
        cost_estimate=cost(2 * length * width * depth * groups, 6 * MIB),
        name="spread",
    )(place, *rows, *rows, weight)


def feed_kernel(*refs):
    xs, grads, joint_ref, down_ref = refs[:2], refs[2:4], refs[4], refs[5]
    x_ref, grad_ref, hidden_ref, low_ref, out_keep, out_send, back_keep, back_send = refs[-8:]
    hidden_width = down_ref.shape[0]
    block = xs[0].shape[0]
    for r in range(2):
        x_ref[r * block : (r + 1) * block, :] = xs[r][...]
        grad_ref[r * block : (r + 1) * block, :] = grads[r][...]
    both = dot_nn(x_ref[...], joint_ref[...])
    gate, up = (both[:, :hidden_width], both[:, hidden_width:])
    sigmoid = 1.0 / (1.0 + jnp.exp(-gate))
    swish = gate * sigmoid
    hidden = (swish * up).astype(jnp.bfloat16)
    hidden_ref[...] = hidden
    hidden_grad = dot_nt(grad_ref[...], down_ref[...])
    low_ref[:, :hidden_width] = (
        hidden_grad * up * sigmoid * (1.0 + gate * (1.0 - sigmoid))
    ).astype(jnp.bfloat16)
    low_ref[:, hidden_width:] = (hidden_grad * swish).astype(jnp.bfloat16)
    out = dot_nn(hidden, down_ref[...]).astype(jnp.bfloat16)
    out_keep[...] = out[:block]
    out_send[...] = out[block:]
    back = dot_nt(low_ref[...], joint_ref[...]).astype(jnp.bfloat16)
    back_keep[...] = back[:block]
    back_send[...] = back[block:]


def feed(call, half, earlier, normed, grads, joint_weight, down_weight):
    block, width = normed[0].shape
    hidden_width = down_weight.shape[0]
    length = block * PIECES * HALVES
    once = pl.Buffered(1)
    row = lambda columns: pl.BlockSpec((2 * block, columns), lambda i: (call, 0))
    whole = lambda value: pl.BlockSpec(value.shape, lambda i: (0, 0), pipeline_mode=once)
    pair = pl.BlockSpec((block, width), lambda i: (0, 0))
    full = lambda columns: jax.ShapeDtypeStruct((length, columns), jnp.bfloat16)
    outs = pl.pallas_call(
        feed_kernel,
        grid=(1,),
        in_specs=[pl.BlockSpec((block, width), lambda i: (0, 0), pipeline_mode=once)] * 2
        + [pl.BlockSpec((block, width), lambda i: (half, 0), pipeline_mode=once)] * 2
        + [whole(joint_weight), whole(down_weight)]
        + [pl.BlockSpec(memory_space=pl.ANY)] * len(earlier),
        out_specs=[row(width), row(width), row(hidden_width), row(2 * hidden_width)] + [pair] * 4,
        out_shape=[full(width), full(width), full(hidden_width), full(2 * hidden_width)]
        + [jax.ShapeDtypeStruct((block, width), jnp.bfloat16)] * 4,
        input_output_aliases={6 + k: k for k in range(len(earlier))},
        compiler_params=params(),
        cost_estimate=cost(3 * length * width * hidden_width, 16 * MIB),
        name="feed",
    )(*normed, *grads, joint_weight, down_weight, *earlier)
    return (outs[:4], outs[4:6], outs[6:8])


def norm_kernel(x_ref, keep_ref, near_ref, far_ref, gain_ref, middle_ref, normed_ref):
    f32 = jnp.float32
    middle = x_ref[...].astype(f32) + (
        keep_ref[...].astype(f32) + near_ref[...].astype(f32) + far_ref[...].astype(f32)
    )
    middle_ref[...] = middle
    normed_ref[...] = (middle * row_scale(middle) * gain_ref[...]).astype(jnp.bfloat16)


def first_of(value, rows, width):
    if value.ndim == 3:
        return pl.BlockSpec((None, rows, width), lambda i: (0, i, 0))
    return pl.BlockSpec((rows, width), lambda i: (i, 0))


def norm(half, tokens, keep, near, far, gain):
    length, width = far.shape
    steps = 2
    rows = length // steps
    flat = pl.BlockSpec((rows, width), lambda i: (i, 0))
    return pl.pallas_call(
        norm_kernel,
        grid=(steps,),
        in_specs=[
            pl.BlockSpec((rows, width), lambda i: (half * steps + i, 0)),
            first_of(keep, rows, width),
            first_of(near, rows, width),
            flat,
            pl.BlockSpec(gain.shape, lambda i: (0, 0)),
        ],
        out_specs=[flat, flat],
        out_shape=[
            jax.ShapeDtypeStruct((length, width), jnp.float32),
            jax.ShapeDtypeStruct((length, width), jnp.bfloat16),
        ],
        compiler_params=params(),
        cost_estimate=cost(0, 4 * MIB),
        name="norm",
    )(tokens, keep, near, far, gain)


def norm_back_of(value, skip, grad, gain):
    inverse = row_scale(value)
    scaled = grad * gain
    lean = jnp.mean(scaled * value, axis=-1, keepdims=True)
    total = skip + (inverse * scaled - value * (inverse**3 * lean))
    return total, jnp.sum(grad * value * inverse, axis=0, keepdims=True)


def norm_back_kernel(
    value_ref, skip_ref, keep_ref, near_ref, far_ref, gain_ref, low_ref, part_ref
):
    f32 = jnp.float32
    grad = keep_ref[...].astype(f32) + near_ref[...].astype(f32) + far_ref[...].astype(f32)
    total, part = norm_back_of(value_ref[...], skip_ref[...].astype(f32), grad, gain_ref[...])
    low_ref[...] = total.astype(jnp.bfloat16)

    @pl.when(pl.program_id(0) == 0)
    def _():
        part_ref[...] = jnp.zeros_like(part_ref)

    part_ref[...] += part


def norm_back(half, value, skip, keep, near, far, gain):
    length, width = far.shape
    steps = 2
    rows = length // steps
    flat = pl.BlockSpec((rows, width), lambda i: (i, 0))
    return pl.pallas_call(
        norm_back_kernel,
        grid=(steps,),
        in_specs=[
            flat,
            pl.BlockSpec((rows, width), lambda i: (half * steps + i, 0)),
            first_of(keep, rows, width),
            first_of(near, rows, width),
            flat,
            pl.BlockSpec(gain.shape, lambda i: (0, 0)),
        ],
        out_specs=[flat, pl.BlockSpec((1, width), lambda i: (0, 0))],
        out_shape=[
            jax.ShapeDtypeStruct((length, width), jnp.bfloat16),
            jax.ShapeDtypeStruct((1, width), jnp.float32),
        ],
        compiler_params=params(),
        cost_estimate=cost(0, 6 * MIB),
        name="norm_back",
    )(value, skip, keep, near, far, gain)


def row_kernel(counts, *refs):
    scatter_ref, row_ref, turned_ref = refs[-3:]
    parts, heads, squares = refs[: counts[0]], refs[counts[0] : counts[1]], refs[counts[1] : -3]
    width = parts[0].shape[1]
    total = lambda items: sum([item[...] for item in items[1:]], items[0][...])
    row_ref[:, :width] = jnp.zeros((1, width), jnp.float32)
    row_ref[:, width : 2 * width] = total(parts)
    row_ref[:, 2 * width : 2 * width + 2 * HD] = total(heads)
    scattered = scatter_ref[...].astype(jnp.float32)
    turned_ref[...] = scattered.T
    over = jnp.sum(scattered * scattered, axis=0, keepdims=True)
    square = jnp.sum(over, axis=1, keepdims=True) + total(squares)
    lane = lax.broadcasted_iota(jnp.int32, (1, 2 * HD), 1)
    row_ref[:, 2 * width + 2 * HD :] = jnp.where(lane == 0, square, 0.0)


def row_of(parts, heads, squares, scattered):
    counts = (len(parts), len(parts) + len(heads))
    return pl.pallas_call(
        lambda *refs: row_kernel(counts, *refs),
        out_shape=[
            jax.ShapeDtypeStruct((1, 2 * parts[0].shape[1] + 4 * HD), jnp.float32),
            jax.ShapeDtypeStruct(scattered.shape[::-1], jnp.float32),
        ],
        compiler_params=params(24),
        cost_estimate=cost(0, MIB),
        name="row",
    )(*parts, *heads, *squares, scattered)


def finish_kernel(
    x_ref, near_skip, far_skip, keep_ref, near_ref, far_ref, gain_ref, begin_ref, square_ref,
    input_grad_ref, row_ref,
):
    f32 = jnp.float32
    step = pl.program_id(0)
    width = x_ref.shape[1]
    grad = keep_ref[...].astype(f32) + near_ref[...].astype(f32) + far_ref[...].astype(f32)
    skip = jnp.where(step < pl.num_programs(0) // HALVES, near_skip[...], far_skip[...])
    total, part = norm_back_of(
        x_ref[...].astype(f32), skip.astype(f32), grad, gain_ref[...]
    )
    input_grad_ref[...] = total.astype(jnp.bfloat16)

    @pl.when(step == 0)
    def _():
        lane = lax.broadcasted_iota(jnp.int32, row_ref.shape, 1)
        last = jnp.where(lane == 2 * width + 2 * HD, square_ref[...], 0.0)
        row_ref[...] = begin_ref[...] + last

    row_ref[:, :width] += part


def finish(tokens, skips, keep, near, far, gain, row, square):
    length, width = far.shape
    each = 1
    rows = length // HALVES // each
    flat = pl.BlockSpec((rows, width), lambda i: (i, 0))
    whole = lambda value: pl.BlockSpec(value.shape, lambda i: (0, 0))
    return pl.pallas_call(
        finish_kernel,
        grid=(HALVES * each,),
        in_specs=[
            flat,
            pl.BlockSpec((rows, width), lambda i: (jnp.minimum(i, each - 1), 0)),
            pl.BlockSpec((rows, width), lambda i: (jnp.maximum(i - each, 0), 0)),
            first_of(keep, rows, width),
            first_of(near, rows, width),
            flat,
            whole(gain),
            whole(row),
            whole(square),
        ],
        out_specs=[flat, whole(row)],
        out_shape=[
            jax.ShapeDtypeStruct((length, width), jnp.bfloat16),
            jax.ShapeDtypeStruct(row.shape, jnp.float32),
        ],
        compiler_params=params(),
        cost_estimate=cost(0, 6 * MIB),
        name="finish",
    )(tokens, *skips, keep, near, far, gain, row, square)


def exchange(value, axis, bit):
    size = lax.axis_size(axis)
    return lax.ppermute(value, axis, [(i, i ^ bit) for i in range(size)])


def after(value, *others):
    return lax.optimization_barrier((value, *others))[0]


def power_of_two(count):
    return count & (count - 1) == 0


class ScatterSum:
    def __init__(self, grads, flipped, second_first=False):
        size = lax.axis_size("dp")
        rows = grads[0].shape[0] // size
        self.left = [1 << k for k in reversed(range(size.bit_length() - 1))]
        self.order = self.left[::-1]
        if second_first:
            self.order[:2] = self.order[1::-1]
        self.flipped = flipped
        self.sources = [grad.reshape(size, rows, grad.shape[1]) for grad in grads]
        self.columns = sum(grad.shape[1] for grad in grads)
        self.joined = True
        self.total = None


def advance_kernel(plans, here_ref, *refs):
    count = sum(plan[0] for plan in plans)
    ins, outs = refs[:count], refs[count:]
    squares = jnp.zeros((1, 1), jnp.float32)
    for sources, joined, stride, shift, flipped in plans:
        parts, ins = ins[:sources], ins[sources:]

        def value(at, parts=parts, joined=joined):
            if joined:
                return jnp.concatenate([part[at] for part in parts], axis=1)
            return parts[0][at].astype(jnp.float32) + parts[1][at].astype(jnp.float32)

        if stride is None:
            total = value(0).astype(jnp.float32)
            over = jnp.sum(total * total, axis=0, keepdims=True)
            squares += jnp.sum(over, axis=1, keepdims=True)
            at = 0
            for columns, turned in flipped:
                part = total[:, at : at + columns]
                outs[0][...] = part.T if turned else part
                at, outs = at + columns, outs[1:]
            continue
        sent, kept, outs = outs[0], outs[1], outs[2:]
        own = (here_ref[0] >> shift) & 1
        for k in range(sent.shape[0]):
            base = k // stride * 2 * stride + k % stride
            sent[k] = value(base + (1 - own) * stride).astype(sent.dtype)
            kept[k] = value(base + own * stride).astype(kept.dtype)
    outs[0][...] = squares


def advance(here, items, *gates):
    plans, ins, shapes = [], [], []
    for item in items:
        rows, columns = item.sources[0].shape[1], item.columns
        if item.order:
            bit = item.order[0]
            at = item.left.index(bit)
            stride = 1 << (len(item.left) - 1 - at)
            plans.append((len(item.sources), item.joined, stride, bit.bit_length() - 1, ()))
            half = (item.sources[0].shape[0] // 2, rows, columns)
            shapes += [jax.ShapeDtypeStruct(half, jnp.bfloat16)] * 2
        else:
            plans.append((len(item.sources), item.joined, None, 0, item.flipped))
            for part, turned in item.flipped:
                shape = (part, rows) if turned else (rows, part)
                shapes.append(jax.ShapeDtypeStruct(shape, jnp.float32))
        ins += item.sources
    shapes.append(jax.ShapeDtypeStruct((1, 1), jnp.float32))
    if gates:
        ins[-1] = after(ins[-1], *gates)
    vmem = pl.BlockSpec(memory_space=pltpu.VMEM)
    outs = list(pl.pallas_call(
        lambda *refs: advance_kernel(plans, *refs),
        in_specs=[pl.BlockSpec(memory_space=pltpu.SMEM)] + [vmem] * len(ins),
        out_specs=[vmem] * len(shapes),
        out_shape=shapes,
        compiler_params=params(24),
        cost_estimate=cost(0, 6 * MIB),
        name="advance",
    )(here, *ins))
    sent_all = []
    for item in items:
        if item.order:
            bit = item.order.pop(0)
            item.left.remove(bit)
            sent, kept = outs.pop(0), outs.pop(0)
            item.sources, item.joined = [kept, exchange(sent, "dp", bit)], False
            sent_all.append(sent)
        else:
            item.total = [outs.pop(0) for _ in item.flipped]
    return sent_all, outs[0]


def sum_all(value):
    for axis in ("tensor", "dp"):
        size = lax.axis_size(axis)
        if not power_of_two(size):
            value = lax.psum(value, axis)
            continue
        bit = 1
        while bit < size:
            if 2 * bit < size:
                one, two, three = [exchange(value, axis, bit * k) for k in (1, 2, 3)]
                value = (value + one) + (two + three)
                bit *= 4
            else:
                value = value + exchange(value, axis, bit)
                bit *= 2
    return value


def adam(master, mean, square, grad, factor, rate, decay):
    scaled = grad * factor
    mean_new = BETA_ONE * mean + (1.0 - BETA_ONE) * scaled
    square_new = BETA_TWO * square + (1.0 - BETA_TWO) * scaled * scaled
    mean_hat = mean_new / (1.0 - BETA_ONE**STEP)
    square_hat = square_new / (1.0 - BETA_TWO**STEP)
    new = master - rate * (mean_hat / (jnp.sqrt(square_hat) + ADAM_EPS) + decay * master)
    return (new, mean_new, square_new)


def adam_kernel(
    out_rate, entries, sum_ref, out_sum, early_ref, late_ref, gate_ref, up_ref, down_sum, *refs
):
    gain_sum = sum_ref[:, :entries]
    squares = sum_ref[:, entries : entries + 1]
    norm = jnp.sqrt(squares + jnp.sum(gain_sum * gain_sum, axis=1, keepdims=True))
    factor = CLIP_NORM / jnp.maximum(norm, CLIP_NORM)
    states = [refs[3 * k : 3 * k + 3] for k in range(4)]
    results = [refs[12 + 4 * k : 16 + 4 * k] for k in range(4)]
    refs[28][...] = norm

    def update(state, result, at, grad, rate):
        new, mean, square = adam(
            state[0][at], state[1][at], state[2][at], grad.astype(jnp.float32), factor, rate,
            DECAY,
        )
        result[0][at] = new
        result[1][at] = new.astype(jnp.bfloat16)
        result[2][at] = mean
        result[3][at] = square

    rows = slice(None)
    early = early_ref.shape[1]
    update(states[1], results[1], (rows, rows), out_sum[...], out_rate)
    update(states[0], results[0], (rows, slice(0, early)), early_ref[...], RATE_WEIGHT)
    update(states[0], results[0], (rows, slice(early, None)), late_ref[...], RATE_WEIGHT)
    update(states[2], results[2], (rows, 0, rows), gate_ref[...], RATE_WEIGHT)
    update(states[2], results[2], (rows, 1, rows), up_ref[...], RATE_WEIGHT)
    update(states[3], results[3], (rows, rows), down_sum[...], RATE_WEIGHT)


def adam_all(entries, summed, sums, states, out_rate):
    steps = max(1, states[0][0].shape[0] // 32)

    def block(array):
        rows = array.shape[0] // steps
        rest = array.shape[1:]
        return pl.BlockSpec((rows,) + rest, lambda i: (i,) + (0,) * len(rest))

    shapes = []
    for state in states:
        shapes += [
            jax.ShapeDtypeStruct(state[0].shape, dtype)
            for dtype in (jnp.float32, jnp.bfloat16, jnp.float32, jnp.float32)
        ]
    arrays = [*sums]
    for state in states:
        arrays += state
    small = lambda shape: pl.BlockSpec(shape, lambda i: (0, 0))
    return pl.pallas_call(
        lambda *refs: adam_kernel(out_rate, entries, *refs),
        grid=(steps,),
        in_specs=[small(summed.shape)] + [block(array) for array in arrays],
        out_specs=[block(shape) for shape in shapes] + [small((1, 1))],
        out_shape=shapes + [jax.ShapeDtypeStruct((1, 1), jnp.float32)],
        compiler_params=params(),
        cost_estimate=cost(0, 16 * MIB),
        name="adam",
    )(summed, *arrays)


def shards(
    tokens,
    segments,
    cotangent,
    qkv_weight,
    out_weight,
    gate_up_weight,
    down_weight,
    qkv_master,
    out_master,
    gate_up_master,
    down_master,
    qkv_mean,
    out_mean,
    gate_up_mean,
    down_mean,
    qkv_square,
    out_square,
    gate_up_square,
    down_square,
    gains,
    gains_mean,
    gains_square,
):
    width = tokens.shape[1]
    length = segments.shape[0]
    groups = qkv_weight.shape[1] // (KINDS * HD)
    hidden_width = down_weight.shape[0]
    block = length // PIECES // HALVES
    attn_gain = gains[None, :width]
    ffn_gain = gains[None, width : 2 * width]
    head_gains = jnp.stack([gains[2 * width : 2 * width + HD], gains[2 * width + HD :]], axis=1)
    place = lax.axis_index("tensor").astype(jnp.int32).reshape(1)
    here = lax.axis_index("dp").astype(jnp.int32).reshape(1)

    across = exchange(tokens, "tensor", ACROSS)
    beside = exchange(tokens, "tensor", CORE)
    starts = starts_of(segments)
    tables = rotary((jnp.arange(length, dtype=jnp.int32) - starts).astype(jnp.float32))
    weight_rows = qkv_weight.T
    inner = (attn_gain, weight_rows, head_gains, *tables)
    near_part = project(0, [], place, [tokens, beside], *inner)
    flat_weight = after(gate_up_weight, near_part[2]).reshape(width, 2 * hidden_width)
    across = after(across, near_part[2], flat_weight)
    corner = exchange(across, "tensor", CORE)
    normed_one, raw, flipped, rows = project(1, near_part, place, [across, corner], *inner)

    grad_across = exchange(after(cotangent, across), "tensor", ACROSS)
    grad_pieces = [
        cotangent,
        exchange(after(cotangent, across), "tensor", CORE),
        grad_across,
        exchange(grad_across, "tensor", CORE),
    ]

    def added(left, right):
        return (left.astype(jnp.float32) + right.astype(jnp.float32)).astype(jnp.bfloat16)

    def halfway(send, keep):
        near = exchange(send, "tensor", CORE)
        return (keep, near, added(keep[1], near[1]))

    def across_of(passed):
        keep, near, passed = passed
        return (keep, near, exchange(passed, "tensor", ACROSS))

    attended, send, keep = attend(0, [], place, flipped, rows, starts, out_weight)
    passed = halfway(after(send, grad_across), keep)
    shares = across_of(passed)
    flipped_late = after(flipped, passed[2])
    attended, send, keep = attend(1, attended, place, flipped_late, rows, starts, out_weight)
    context, context_flip, log_total = attended

    weights = (flat_weight, down_weight)
    middle, normed = norm(0, tokens, *shares, ffn_gain)
    middles = [middle]
    beside, across = exchange(normed, "tensor", CORE), exchange(normed, "tensor", ACROSS)
    passed = halfway(after(send, shares[2]), keep)
    shares = across_of(passed)
    full, out_near, back_near = feed(
        0, 0, [], [after(normed, passed[2]), beside], grad_pieces[:2], *weights
    )
    across = after(across, out_near[0])
    corner = exchange(across, "tensor", CORE)
    full, out_far, back_far = feed(1, 0, full, [across, corner], grad_pieces[2:], *weights)
    outs, backs = [(*out_near, *out_far)], [(*back_near, *back_far)]

    keep, near, far = shares
    middle, normed = norm(1, tokens, keep, near, after(far, out_far[0]), ffn_gain)
    middles.append(middle)
    beside, across = exchange(normed, "tensor", CORE), exchange(normed, "tensor", ACROSS)
    full, out_near, back_near = feed(2, 1, full, [normed, beside], grad_pieces[:2], *weights)

    def share_of(pieces, *gates):
        third = exchange(pieces[3], "tensor", CORE)
        third = after(third, *gates) if gates else third
        return (pieces[0], exchange(pieces[1], "tensor", CORE), added(pieces[2], third))

    passed = share_of(backs[0], out_near[0])
    sums = [across_of(passed)]
    across = after(across, out_near[0])
    corner = exchange(across, "tensor", CORE)
    across = after(across, passed[2])
    full, out_far, back_far = feed(3, 1, full, [across, corner], grad_pieces[2:], *weights)
    outs.append((*out_near, *out_far))
    backs.append((*back_near, *back_far))
    normed_two, grad_full, hidden, flat_low = full

    def dh_of(half, keep, near, far):
        low, part = norm_back(half, middles[half], cotangent, keep, near, far, ffn_gain)
        across = exchange(low, "tensor", ACROSS)
        pieces = [low, exchange(low, "tensor", CORE), across, exchange(across, "tensor", CORE)]
        return pieces, part

    keep, near, far = sums[0]
    first_dh = dh_of(0, keep, near, after(far, out_far[0]))
    passed = share_of(after(tuple(backs[1]), far))
    sums.append(across_of(passed))
    sent = after(grad_full, passed[2], first_dh[0][0])
    down_grad = contract_rows(sent, hidden).astype(jnp.bfloat16)
    gate_grad = contract_rows(after(normed_two, down_grad), flat_low[:, :hidden_width])
    gate = ScatterSum([gate_grad.astype(jnp.bfloat16)], [(hidden_width, False)])
    sent, square = advance(here, [gate])
    squares = [square]
    out_sums = [share_of(after(tuple(out), passed[2])) for out in outs]
    keep, near, far = sums[1]
    far_late = after(far, sent[0], first_dh[0][2])
    second_dh = dh_of(1, keep, near, far_late)
    pieces_dh, ffn_parts = zip(first_dh, second_dh)
    down_sum = lax.psum_scatter(
        after(down_grad, far_late), "dp", scatter_dimension=0, tiled=True
    )
    normed_two = after(normed_two, pieces_dh[1][0])
    up_grad = contract_rows(normed_two, flat_low[:, hidden_width:])
    up = ScatterSum([up_grad.astype(jnp.bfloat16)], [(hidden_width, False)], True)
    advance(here, [up], pieces_dh[1][2])
    sent, _ = advance(here, [gate], up.sources[0])

    dh = [pieces_dh[half][r] for r in range(PIECES) for half in range(HALVES)]
    dh[0] = after(dh[0], *sent, *[item[2] for item in out_sums])
    out_fars = [
        exchange(after(item[2], pieces_dh[1][2]), "tensor", ACROSS) for item in out_sums
    ]

    joints, head_parts, mixed, early = [], [], [], []
    for g in range(groups):
        outs_back = attend_back(
            g, place, flipped, rows, context_flip, log_total, starts, dh, out_weight, raw, tables,
            head_gains,
        )
        joints.append(outs_back[0])
        head_parts.append(outs_back[1])
        if g == 0:
            dh_full = outs_back[2]
            early = ScatterSum(
                [
                    contract_rows(dh_full, context).astype(jnp.bfloat16),
                    contract_rows(normed_one, outs_back[0]).astype(jnp.bfloat16),
                ],
                [(context.shape[1], True), (joints[0].shape[1], False)],
            )
            sent, _ = advance(here, [gate, up, early], outs_back[1])
            dh = [after(dh_full, *sent, *out_fars)]
        else:
            dh = [dh_full]
    sent, square = advance(here, [gate, up, early], joints[-1], down_sum)
    squares.append(square)
    joints[0] = after(joints[0], *sent)
    send, keep = spread(place, joints, weight_rows)
    late = [
        contract_rows(normed_one, after(joints[g], keep)).astype(jnp.bfloat16)
        for g in range(1, groups)
    ]
    near = exchange(send, "tensor", CORE)
    passed = (keep, near, added(keep[1], near[1]))
    keep, near, far = across_of(passed)
    late = ScatterSum(late, [(joints[0].shape[1] * (groups - 1), False)])
    pending = [gate, up, early, late]
    gates = [passed[2]]
    while pending:
        pending = [item for item in pending if item.total is None]
        _, square = advance(here, pending, *gates)
        squares.append(square)
        pending = [item for item in pending if item.total is None]
        gates = []

    results = []
    for half in range(HALVES):
        keep_out, near_out, _ = out_sums[half]
        total = keep_out.astype(jnp.float32) + near_out.astype(jnp.float32)
        results.append(middles[half] + (total + out_fars[half].astype(jnp.float32)))
    result = jnp.concatenate(results, axis=0).astype(jnp.bfloat16)

    ffn_parts = [after(ffn_parts[0], result), *ffn_parts[1:]]
    row, down_total = row_of(ffn_parts, head_parts, squares[1:-1], down_sum)
    skips = [pieces[0] for pieces in pieces_dh]
    input_grad, row = finish(tokens, skips, keep, near, far, attn_gain, row, squares[-1])
    summed = sum_all(row)
    entries = gains.shape[0]
    out_fan = max(QH * HD * 16 // length, 16)
    out_rate = RATE_WEIGHT * (QH * HD / out_fan) ** 0.5
    updated = adam_all(
        entries, summed, [*early.total, *late.total, *gate.total, *up.total, down_total],
        [
            (qkv_master, qkv_mean, qkv_square),
            (out_master, out_mean, out_square),
            (gate_up_master, gate_up_mean, gate_up_square),
            (down_master, down_mean, down_square),
        ],
        out_rate,
    )
    grad_norm = updated[16][0, 0]
    factor = CLIP_NORM / jnp.maximum(grad_norm, CLIP_NORM)
    gain_results = adam(
        gains, gains_mean, gains_square, summed[0, :entries], factor, RATE_GAIN, 0.0
    )
    return (result, input_grad, grad_norm, *updated[:16], *gain_results)


def solution(mesh):
    in_specs = (
        P(("dp", "tensor"), None),
        P("dp"),
        P(("dp", "tensor"), None),
        P(None, "tensor"),
        P("tensor", None),
        P(None, None, "tensor"),
        P("tensor", None),
        P("dp", "tensor"),
        P("tensor", "dp"),
        P("dp", None, "tensor"),
        P("tensor", "dp"),
        P("dp", "tensor"),
        P("tensor", "dp"),
        P("dp", None, "tensor"),
        P("tensor", "dp"),
        P("dp", "tensor"),
        P("tensor", "dp"),
        P("dp", None, "tensor"),
        P("tensor", "dp"),
        P(),
        P(),
        P(),
    )
    out_specs = (
        P(("dp", "tensor"), None),
        P(("dp", "tensor"), None),
        P(),
        P("dp", "tensor"),
        P("dp", "tensor"),
        P("dp", "tensor"),
        P("dp", "tensor"),
        P("tensor", "dp"),
        P("tensor", "dp"),
        P("tensor", "dp"),
        P("tensor", "dp"),
        P("dp", None, "tensor"),
        P("dp", None, "tensor"),
        P("dp", None, "tensor"),
        P("dp", None, "tensor"),
        P("tensor", "dp"),
        P("tensor", "dp"),
        P("tensor", "dp"),
        P("tensor", "dp"),
        P(),
        P(),
        P(),
    )
    return jax.shard_map(shards, mesh=mesh, in_specs=in_specs, out_specs=out_specs, check_vma=False)
```

profile of v0, /device:TPU:0, one launch (start us, length us, event | category | flops | bytes accessed | tf_op | source)
XLA Modules:
  0.0 407.0 jit_solution(8622876508050697377)
XLA Ops:
  7.8 2.6 collective-permute-start
  10.3 1.3 slice.66
  12.4 1.5 select_bitcast_fusion
  15.0 2.3 copy.69
  17.4 1.3 fusion.17
  18.8 1.8 multiply_sine_fusion
  21.6 7.1 %project.2 = (bf16[2048,1024]{1,0:T(8,128)(2,1)}, f32[8,64,2048]{2,1,0:T(8,128)}, bf16[8,64,2048]{2,1,0:T(8,128)(2,1)}, bf16[8,2048,64]{2,1,0:T(8,128)(2,1)}) custom-call(s32[1]{0:T(128)} %bitcast.2.place_ref.refs_2_.refs_0_, bf16[512,1024]{1,0:T(8,128)(2,1)} %x_ref.5, bf16[512,1024]{1,0:T(8,128)(2,1)} %copy-done.30, f32[1,1024]{1,0:T(1,128)} %bitcast.86, ...), custom_call_target="tpu_custom_call" | custom-call | flops 134217728 | bytes 1048576 | tf_op jit(solution)/shard_map/project/pallas_call | solution.py:139
  28.7 5.4 %copy.74 = bf16[128,8,2,1152]{3,1,2,0:T(8,128)(2,1)} copy(bf16[128,8,2,1152]{3,2,1,0:T(2,128)(2,1)} %bitcast.75) | data formatting | bytes 9437184
  34.3 1.8 collective-permute-start.3
  37.3 7.1 %project.3 = (bf16[2048,1024]{1,0:T(8,128)(2,1)}, f32[8,64,2048]{2,1,0:T(8,128)}, bf16[8,64,2048]{2,1,0:T(8,128)(2,1)}, bf16[8,2048,64]{2,1,0:T(8,128)(2,1)}) custom-call(s32[1]{0:T(128)} %bitcast.2.place_ref.refs_2_.refs_0_, bf16[512,1024]{1,0:T(8,128)(2,1)} %copy-done.29, ...), custom_call_target="tpu_custom_call", output_to_operand_aliasing={{0}: (8, {}), {1}: (9, {}), {2}: (10, {}), {3}: (11, {})} | custom-call | flops 134217728 | bytes 1048576 | tf_op jit(solution)/shard_map/project/pallas_call | solution.py:139
  44.4 14.2 %attend.2 = (bf16[2048,256]{1,0:T(8,128)(2,1)}, bf16[256,2048]{1,0:T(8,128)(2,1)}, f32[2,2,1,2048]{3,2,1,0:T(1,128)}, bf16[2,256,1024]{2,1,0:T(8,128)(2,1)}, bf16[2,256,1024]{2,1,0:T(8,128)(2,1)}) custom-call(s32[8]{0:T(128)} %slice.70.refs_0_, s32[8]{0:T(128)} %slice.71.refs_1_, s32[1]{0:T(128)} %bitcast.2.place_ref.refs_2_.refs_0_, ...), custom_call_target="tpu_custom_call" | custom-call | flops 536870912 | bytes 786432 | tf_op jit(solution)/shard_map/attend/pallas_call | solution.py:261
  58.6 1.2 collective-permute-done.3.refs_2_
  59.9 2.9 collective-permute-done.4.near_ref
  62.8 1.6 fusion.11
  64.3 1.8 collective-permute-start.5
  66.2 17.3 %attend.3 = (bf16[2048,256]{1,0:T(8,128)(2,1)}, bf16[256,2048]{1,0:T(8,128)(2,1)}, f32[2,2,1,2048]{3,2,1,0:T(1,128)}, bf16[2,256,1024]{2,1,0:T(8,128)(2,1)}, bf16[2,256,1024]{2,1,0:T(8,128)(2,1)}) custom-call(s32[8]{0:T(128)} %slice.70.refs_0_, s32[8]{0:T(128)} %slice.71.refs_1_, ...), custom_call_target="tpu_custom_call", output_to_operand_aliasing={{0}: (8, {}), {1}: (9, {}), {2}: (10, {})} | custom-call | flops 536870912 | bytes 786432 | tf_op jit(solution)/shard_map/attend/pallas_call | solution.py:261
  84.0 2.8 norm.2
  87.4 2.2 fusion.12
  89.6 12.8 %feed.4 = (bf16[2048,1024]{1,0:T(8,128)(2,1)}, bf16[2048,1024]{1,0:T(8,128)(2,1)}, bf16[2048,1152]{1,0:T(8,128)(2,1)}, bf16[2048,2304]{1,0:T(8,128)(2,1)}, bf16[...) custom-call(bf16[256,1024]{1,0:T(8,128)(2,1)} %get-tuple-element.205.re, ...), custom_call_target="tpu_custom_call" | custom-call | flops 905969664 | bytes 2097152 | tf_op jit(solution)/shard_map/feed/pallas_call | solution.py:542
  102.8 1.8 collective-permute-start.12
  105.7 22.3 %feed.5 = (bf16[2048,1024]{1,0:T(8,128)(2,1)}, bf16[2048,1024]{1,0:T(8,128)(2,1)}, bf16[2048,1152]{1,0:T(8,128)(2,1)}, bf16[2048,2304]{1,0:T(8,128)(2,1)}, bf16[...) custom-call(bf16[256,1024]{1,0:T(8,128)(2,1)} %copy-done.37, ...), custom_call_target="tpu_custom_call", output_to_operand_aliasing={{0}: (6, {}), {1}: (7, {}), {2}: (8, {}), {3}: (9, {})} | custom-call | flops 905969664 | bytes 2097152 | tf_op jit(solution)/shard_map/feed/pallas_call | solution.py:542
  128.0 2.6 norm.3
  130.5 1.6 collective-permute-start.14
  133.4 12.8 %feed.6 = (bf16[2048,1024]{1,0:T(8,128)(2,1)}, bf16[2048,1024]{1,0:T(8,128)(2,1)}, bf16[2048,1152]{1,0:T(8,128)(2,1)}, bf16[2048,2304]{1,0:T(8,128)(2,1)}, bf16[...) custom-call(bf16[256,1024]{1,0:T(8,128)(2,1)} %get-tuple-element.216, ...), custom_call_target="tpu_custom_call", output_to_operand_aliasing={{0}: (6, {}), {1}: (7, {}), {2}: (8, {}), {3}: (9, {})} | custom-call | flops 905969664 | bytes 2097152 | tf_op jit(solution)/shard_map/feed/pallas_call | solution.py:542
  146.6 1.5 collective-permute-start.17
  149.0 13.1 %feed.7 = (bf16[2048,1024]{1,0:T(8,128)(2,1)}, bf16[2048,1024]{1,0:T(8,128)(2,1)}, bf16[2048,1152]{1,0:T(8,128)(2,1)}, bf16[2048,2304]{1,0:T(8,128)(2,1)}, bf16[...) custom-call(bf16[256,1024]{1,0:T(8,128)(2,1)} %copy-done.36, ...), custom_call_target="tpu_custom_call", output_to_operand_aliasing={{0}: (6, {}), {1}: (7, {}), {2}: (8, {}), {3}: (9, {})} | custom-call | flops 905969664 | bytes 2097152 | tf_op jit(solution)/shard_map/feed/pallas_call | solution.py:542
  163.4 2.9 norm_back.2
  169.7 9.9 %convolution_convert_fusion = bf16[1024,1152]{1,0:T(8,128)(2,1)} fusion(bf16[2048,1024]{1,0:T(8,128)(2,1)} %get-tuple-element.251, bf16[2048,1152]{1,0:T(8,128)(2,1)} %get-tuple-element.252), kind=kOutput, calls=%fused_computation.6 | convolution fusion | flops 4833017856 | bytes 11272192 | tf_op jit(solution)/shard_map/dot_general | solution.py:69
  179.6 8.9 %fusion.4 = bf16[1024,1152]{1,0:T(8,128)(2,1)S(1)} fusion(bf16[2048,1024]{1,0:T(8,128)(2,1)} %get-tuple-element.270, bf16[2048,2304]{1,0:T(8,128)(2,1)} %get-tuple-element.254), kind=kOutput, calls=%fused_computation.4 | convolution fusion | flops 4833017856 | bytes 11272192 | tf_op jit(solution)/shard_map/dot_general | solution.py:69
  190.0 1.7 collective-permute-done.22.far_ref
  194.0 2.9 norm_back.3
  197.0 1.3 collective-permute-start.25
  198.2 9.0 %fusion.7 = bf16[1024,1152]{1,0:T(8,128)(2,1)S(1)} fusion(bf16[2048,1024]{1,0:T(8,128)(2,1)} %get-tuple-element.270, bf16[2048,2304]{1,0:T(8,128)(2,1)} %get-tuple-element.254), kind=kOutput, calls=%fused_computation.5 | convolution fusion | flops 4833017856 | bytes 11272192 | tf_op jit(solution)/shard_map/dot_general | solution.py:69
  207.9 3.3 collective-permute-done.25.refs_22_
  213.4 13.3 %collective-permute-done.30.refs_2_ = bf16[4,128,1152]{2,1,0:T(8,128)(2,1)S(1)} collective-permute-done((bf16[4,128,1152]{2,1,0:T(8,128)(2,1)}, bf16[4,128,1152]{2,1,0:T(8,128)(2,1)S(1)}, u32[]{:S(2)}, u32[]{:S(2)}) %collective-permute-start.30) | collective-permute-done | bytes 1179680 | tf_op jit(solution)/shard_map/ppermute | solution.py:737
  227.8 6.2 %collective-permute-start.36 = (bf16[4,128,1152]{2,1,0:T(8,128)(2,1)}, bf16[4,128,1152]{2,1,0:T(8,128)(2,1)S(1)}, u32[]{:S(2)}, u32[]{:S(2)}) collective-permute-start(bf16[4,128,1152]{2,1,0:T(8,128)(2,1)} %get-tuple-element.278), channel_id=1, source_target_pairs={{0,8},{4,12},{8,0},{12,4},{16,24},{20,28},{24,16},{28,20},{1,9},{5... | collective-permute-start | bytes 3538952 | tf_op jit(solution)/shard_map/ppermute | solution.py:737
  235.0 1.3 copy-done.1
  240.3 26.5 %attend_back.2 = (bf16[2048,256]{1,0:T(8,128)(2,1)}, f32[1,128]{1,0:T(1,128)}, bf16[2048,1024]{1,0:T(8,128)(2,1)}) custom-call(s32[8]{0:T(128)} %slice.70.refs_0_, s32[8]{0:T(128)} %slice.71.refs_1_, s32[1]{0:T(128)} %bitcast.2.place_ref.refs_2_.refs_0_, bf16[2,4,64,2048]{3,2,1,0:T(8,128)(2,1)} %bitcast.60, bf16[2,4,2048,64]{3,2,1,0:T(8,128)(2,1)} %bitcast.50, ...), custom_call_target="tpu_custom_call" | custom-call | flops 1342177280 | bytes 1572864 | tf_op jit(solution)/shard_map/attend_back/pallas_call | solution.py:424
  266.9 4.0 convolution_convert_fusion.3
  270.9 1.3 convolution_convert_fusion.2
  272.2 8.5 %collective-permute-done.35.refs_2_ = bf16[2,128,1152]{2,1,0:T(8,128)(2,1)S(1)} collective-permute-done((bf16[2,128,1152]{2,1,0:T(8,128)(2,1)}, bf16[2,128,1152]{2,1,0:T(8,128)(2,1)S(1)}, u32[]{:S(2)}, u32[]{:S(2)}) %collective-permute-start.35) | collective-permute-done | bytes 589856 | tf_op jit(solution)/shard_map/ppermute | solution.py:737
  280.7 1.3 advance.12
  283.5 1.9 collective-permute-start.38
  285.6 24.6 %attend_back.3 = (bf16[2048,256]{1,0:T(8,128)(2,1)}, f32[1,128]{1,0:T(1,128)}) custom-call(s32[8]{0:T(128)} %slice.70.refs_0_, s32[8]{0:T(128)} %slice.71.refs_1_, s32[1]{0:T(128)} %bitcast.2.place_ref.refs_2_.refs_0_, bf16[2,4,64,2048]{3,2,1,0:T(8,128)(2,1)} %bitcast.62, bf16[2,4,2048,64]{3,2,1,0:T(8,128)(2,1)} %bitcast.53, ...), custom_call_target="tpu_custom_call" | custom-call | flops 1342177280 | bytes 1572864 | tf_op jit(solution)/shard_map/attend_back/pallas_call | solution.py:424
  312.2 5.4 %spread.1 = (bf16[2,512,1024]{2,1,0:T(8,128)(2,1)}, bf16[2,512,1024]{2,1,0:T(8,128)(2,1)}) custom-call(s32[1]{0:T(128)} %bitcast.2.place_ref.refs_2_.refs_0_, bf16[2048,256]{1,0:T(8,128)(2,1)} %get-tuple-element.296.refs_1_.refs_3_, bf16[2048,256]{1,0:T(8,128)(2,1)} %get-tuple-element.306.refs_2_.refs_4_, ...), custom_call_target="tpu_custom_call" | custom-call | flops 268435456 | bytes 786432 | tf_op jit(solution)/shard_map/spread/pallas_call | solution.py:489
  318.2 1.3 collective-permute-start.42
  319.5 2.5 collective-permute-done.40.near_ref
  322.0 2.4 fusion.10
  325.4 3.8 convolution_convert_fusion.1
  329.3 1.3 collective-permute-done.43.refs_4_
  330.6 4.3 %collective-permute-done.42.refs_2_ = bf16[1,128,1152]{2,1,0:T(8,128)(2,1)S(1)} collective-permute-done((bf16[1,128,1152]{2,1,0:T(8,128)(2,1)S(1)}, bf16[1,128,1152]{2,1,0:T(8,128)(2,1)S(1)}, u32[]{:S(2)}, u32[]{:S(2)}) %collective-permute-start.42) | collective-permute-done | bytes 294944 | tf_op jit(solution)/shard_map/ppermute | solution.py:737
  335.7 8.9 %collective-permute-start.45 = (bf16[4,128,256]{2,1,0:T(8,128)(2,1)S(1)}, bf16[4,128,256]{2,1,0:T(8,128)(2,1)S(1)}, u32[]{:S(2)}, u32[]{:S(2)}) collective-permute-start(bf16[4,128,256]{2,1,0:T(8,128)(2,1)S(1)} %get-tuple-element.312), channel_id=1, source_target_pairs={{0,4},{4,0},{8,12},{12,8},{16,20},{20,16},{24,28},{28,24},{1,5},{5... | collective-permute-start | bytes 786440 | tf_op jit(solution)/shard_map/ppermute | solution.py:737
  344.6 1.4 add_convert_fusion.3
  346.0 4.8 %collective-permute-done.45.refs_4_ = bf16[4,128,256]{2,1,0:T(8,128)(2,1)S(1)} collective-permute-done((bf16[4,128,256]{2,1,0:T(8,128)(2,1)S(1)}, bf16[4,128,256]{2,1,0:T(8,128)(2,1)S(1)}, u32[]{:S(2)}, u32[]{:S(2)}) %collective-permute-start.45) | collective-permute-done | bytes 262176 | tf_op jit(solution)/shard_map/ppermute | solution.py:737
  351.4 1.5 add_convert_fusion.1
  352.9 3.5 collective-permute-done.46.refs_2_
  356.9 2.9 collective-permute-start.47
  360.9 2.8 row.1
  366.8 4.9 %finish.1 = (bf16[512,1024]{1,0:T(8,128)(2,1)}, f32[1,2304]{1,0:T(1,128)}) custom-call(bf16[512,1024]{1,0:T(8,128)(2,1)} %x_ref.5, bf16[256,1024]{1,0:T(8,128)(2,1)} %get-tuple-element.275.refs_17_.near_skip, bf16[256,1024]{1,0:T(8,128)(2,1)} %get-tuple-element.257.refs_18_.far_skip, bf16[2,512,1024]{2,1,0:T(8,128)(2,1)} %get-tuple-element.297.keep_ref, ...), custom_call_target="tpu_custom_call" | custom-call | bytes 786432 | tf_op jit(solution)/shard_map/finish/pallas_call | solution.py:710
  373.6 1.4 collective-permute-done.50
  377.5 2.5 collective-permute-start.52
  381.7 1.9 collective-permute-done.51
  384.2 4.2 %collective-permute-done.54 = f32[1,2304]{1,0:T(1,128)S(1)} collective-permute-done((f32[1,2304]{1,0:T(1,128)S(1)}, f32[1,2304]{1,0:T(1,128)S(1)}, u32[]{:S(2)}, u32[]{:S(2)}) %collective-permute-start.54) | collective-permute-done | bytes 9248 | tf_op jit(solution)/shard_map/ppermute | solution.py:737
  388.9 9.6 %adam.1 = (f32[128,512]{1,0:T(8,128)}, bf16[128,512]{1,0:T(8,128)(2,1)}, f32[128,512]{1,0:T(8,128)}, f32[128,512]{1,0:T(8,128)}, f32[256,128]{1,0:T(8,128)}, /*i...) custom-call(f32[1,2304]{1,0:T(1,128)} %add.99.refs_0_, ...), custom_call_target="tpu_custom_call" | custom-call | bytes 2097152 | tf_op jit(solution)/shard_map/adam/pallas_call | solution.py:914
  (226 shorter events, 47.2 us)
Async XLA Ops:
  7.2 303.0 %reduce-scatter.2.cloned.1.call-start = ((), (), s32[]{:S(2)}) async-start(), calls=%async_computation.1 | async-start | bytes 2654208 | tf_op jit(solution)/shard_map/reduce_scatter | solution.py:1055
  7.2 13.4 %collective-permute-start.1 = (bf16[512,1024]{1,0:T(8,128)(2,1)}, bf16[512,1024]{1,0:T(8,128)(2,1)S(1)}, u32[]{:S(2)}, u32[]{:S(2)}) collective-permute-start(bf16[512,1024]{1,0:T(8,128)(2,1)} %x_ref.5), channel_id=1, source_target_pairs={{0,1},{1,0},{2,3},{3,2},{4,5},{5,4},{6,7},{7,6},{8,9},{9,8},{10,11... | collective-permute-start | bytes 3145736 | tf_op jit(solution)/shard_map/ppermute | solution.py:737
  7.8 26.5 %collective-permute-start = (bf16[512,1024]{1,0:T(8,128)(2,1)}, bf16[512,1024]{1,0:T(8,128)(2,1)S(1)}, u32[]{:S(2)}, u32[]{:S(2)}) collective-permute-start(bf16[512,1024]{1,0:T(8,128)(2,1)} %x_ref.5), channel_id=1, source_target_pairs={{0,2},{1,3},{2,0},{3,1},{4,6},{5,7},{6,4},{7,5},{8,10},{9,11},{10,... | collective-permute-start | bytes 3145736 | tf_op jit(solution)/shard_map/ppermute | solution.py:737
  34.3 3.0 collective-permute-start.2
  34.3 25.6 %collective-permute-start.3 = (bf16[512,1024]{1,0:T(8,128)(2,1)S(1)}, bf16[512,1024]{1,0:T(8,128)(2,1)S(1)}, u32[]{:S(2)}, u32[]{:S(2)}) collective-permute-start(bf16[512,1024]{1,0:T(8,128)(2,1)S(1)} %copy-done.19), channel_id=1, source_target_pairs={{0,2},{1,3},{2,0},{3,1},{4,6},{5,7},{6,4},{7,5},{8,10},{9,11},{10,... | collective-permute-start | bytes 3145736 | tf_op jit(solution)/shard_map/ppermute | solution.py:737
  59.9 27.4 %copy-start.21 = (bf16[512,1024]{1,0:T(8,128)(2,1)}, bf16[512,1024]{1,0:T(8,128)(2,1)S(1)}, u32[]{:S(2)}) copy-start(bf16[512,1024]{1,0:T(8,128)(2,1)S(1)} %collective-permute-done.3.refs_2_) | copy-start | bytes 3145732
  59.9 2.9 collective-permute-start.4
  64.3 19.1 %collective-permute-start.5 = (bf16[256,1024]{1,0:T(8,128)(2,1)S(1)}, bf16[256,1024]{1,0:T(8,128)(2,1)}, u32[]{:S(2)}, u32[]{:S(2)}) collective-permute-start(bf16[256,1024]{1,0:T(8,128)(2,1)S(1)} %fusion.11), channel_id=1, source_target_pairs={{0,2},{1,3},{2,0},{3,1},{4,6},{5,7},{6,4},{7,5},{8,10},{9,11},{10,... | collective-permute-start | bytes 1572872 | tf_op jit(solution)/shard_map/ppermute | solution.py:737
  83.5 4.0 collective-permute-start.6
  83.5 6.1 %collective-permute-start.8 = (bf16[512,1024]{1,0:T(8,128)(2,1)S(1)}, bf16[512,1024]{1,0:T(8,128)(2,1)}, u32[]{:S(2)}, u32[]{:S(2)}) collective-permute-start(bf16[512,1024]{1,0:T(8,128)(2,1)S(1)} %copy-done.19), channel_id=1, source_target_pairs={{0,1},{1,0},{2,3},{3,2},{4,5},{5,4},{6,7},{7,6},{8,9},{9,8},{10,11... | collective-permute-start | bytes 3145736 | tf_op jit(solution)/shard_map/ppermute | solution.py:737
  86.8 2.8 collective-permute-start.7
  87.0 15.4 %collective-permute-start.9 = (bf16[256,1024]{1,0:T(8,128)(2,1)}, bf16[256,1024]{1,0:T(8,128)(2,1)S(1)}, u32[]{:S(2)}, u32[]{:S(2)}) collective-permute-start(bf16[256,1024]{1,0:T(8,128)(2,1)} %get-tuple-element.205.refs_0_), channel_id=1, source_target_pairs={{0,2},{1,3},{2,0},{3,1},{4,6},{5,7},{6,4},{7,5},{8,10},{9,11},{10,... | collective-permute-start | bytes 1572872 | tf_op jit(solution)/shard_map/ppermute | solution.py:737
  87.3 17.3 %collective-permute-start.11 = (bf16[512,1024]{1,0:T(8,128)(2,1)S(1)}, bf16[512,1024]{1,0:T(8,128)(2,1)S(1)}, u32[]{:S(2)}, u32[]{:S(2)}) collective-permute-start(bf16[512,1024]{1,0:T(8,128)(2,1)S(1)} %collective-permute-done.3.refs_2_), channel_id=1, source_target_pairs={{0,1},{1,0},{2,3},{3,2},{4,5},{5,4},{6,7},{7,6},{8,9},{9,8},{10,11... | collective-permute-start | bytes 3145736 | tf_op jit(solution)/shard_map/ppermute | solution.py:737
  102.4 2.2 collective-permute-start.10
  102.8 25.2 %collective-permute-start.12 = (bf16[256,1024]{1,0:T(8,128)(2,1)S(1)}, bf16[256,1024]{1,0:T(8,128)(2,1)}, u32[]{:S(2)}, u32[]{:S(2)}) collective-permute-start(bf16[256,1024]{1,0:T(8,128)(2,1)S(1)} %copy-done.44), channel_id=1, source_target_pairs={{0,2},{1,3},{2,0},{3,1},{4,6},{5,7},{6,4},{7,5},{8,10},{9,11},{10,... | collective-permute-start | bytes 1572872 | tf_op jit(solution)/shard_map/ppermute | solution.py:737
  130.5 2.1 collective-permute-start.13
  130.5 15.7 %collective-permute-start.14 = (bf16[256,1024]{1,0:T(8,128)(2,1)}, bf16[256,1024]{1,0:T(8,128)(2,1)S(1)}, u32[]{:S(2)}, u32[]{:S(2)}) collective-permute-start(bf16[256,1024]{1,0:T(8,128)(2,1)} %get-tuple-element.216.refs_0_), channel_id=1, source_target_pairs={{0,2},{1,3},{2,0},{3,1},{4,6},{5,7},{6,4},{7,5},{8,10},{9,11},{10,... | collective-permute-start | bytes 1572872 | tf_op jit(solution)/shard_map/ppermute | solution.py:737
  132.1 14.4 %collective-permute-start.15 = (bf16[256,1024]{1,0:T(8,128)(2,1)}, bf16[256,1024]{1,0:T(8,128)(2,1)S(1)}, u32[]{:S(2)}, u32[]{:S(2)}) collective-permute-start(bf16[256,1024]{1,0:T(8,128)(2,1)} %get-tuple-element.226), channel_id=1, source_target_pairs={{0,1},{1,0},{2,3},{3,2},{4,5},{5,4},{6,7},{7,6},{8,9},{9,8},{10,11... | collective-permute-start | bytes 1572872 | tf_op jit(solution)/shard_map/ppermute | solution.py:737
  146.2 2.0 collective-permute-start.16
  146.6 15.5 %collective-permute-start.17 = (bf16[256,1024]{1,0:T(8,128)(2,1)S(1)}, bf16[256,1024]{1,0:T(8,128)(2,1)S(1)}, u32[]{:S(2)}, u32[]{:S(2)}) collective-permute-start(bf16[256,1024]{1,0:T(8,128)(2,1)S(1)} %add_convert_fusion.6), channel_id=1, source_target_pairs={{0,2},{1,3},{2,0},{3,1},{4,6},{5,7},{6,4},{7,5},{8,10},{9,11},{10,... | collective-permute-start | bytes 1572872 | tf_op jit(solution)/shard_map/ppermute | solution.py:737
  148.1 14.5 %collective-permute-start.23 = (bf16[256,1024]{1,0:T(8,128)(2,1)S(1)}, bf16[256,1024]{1,0:T(8,128)(2,1)S(1)}, u32[]{:S(2)}, u32[]{:S(2)}) collective-permute-start(bf16[256,1024]{1,0:T(8,128)(2,1)S(1)} %copy-done.55), channel_id=1, source_target_pairs={{0,1},{1,0},{2,3},{3,2},{4,5},{5,4},{6,7},{7,6},{8,9},{9,8},{10,11... | collective-permute-start | bytes 1572872 | tf_op jit(solution)/shard_map/ppermute | solution.py:737
  162.1 5.3 %collective-permute-start.18 = (bf16[256,1024]{1,0:T(8,128)(2,1)}, bf16[256,1024]{1,0:T(8,128)(2,1)S(1)}, u32[]{:S(2)}, u32[]{:S(2)}) collective-permute-start(bf16[256,1024]{1,0:T(8,128)(2,1)} %get-tuple-element.236), channel_id=1, source_target_pairs={{0,1},{1,0},{2,3},{3,2},{4,5},{5,4},{6,7},{7,6},{8,9},{9,8},{10,11... | collective-permute-start | bytes 1572872 | tf_op jit(solution)/shard_map/ppermute | solution.py:737
  166.3 23.7 %collective-permute-start.24 = (bf16[256,1024]{1,0:T(8,128)(2,1)}, bf16[256,1024]{1,0:T(8,128)(2,1)}, u32[]{:S(2)}, u32[]{:S(2)}) collective-permute-start(bf16[256,1024]{1,0:T(8,128)(2,1)} %get-tuple-element.275.refs_17_.near_skip), channel_id=1, source_target_pairs={{0,2},{1,3},{2,0},{3,1},{4,6},{5,7},{6,4},{7,5},{8,10},{9,11},{10,... | collective-permute-start | bytes 1572872 | tf_op jit(solution)/shard_map/ppermute | solution.py:737
  168.7 23.0 %collective-permute-start.22 = (bf16[256,1024]{1,0:T(8,128)(2,1)S(1)}, bf16[256,1024]{1,0:T(8,128)(2,1)S(1)}, u32[]{:S(2)}, u32[]{:S(2)}) collective-permute-start(bf16[256,1024]{1,0:T(8,128)(2,1)S(1)} %add_convert_fusion.5), channel_id=1, source_target_pairs={{0,2},{1,3},{2,0},{3,1},{4,6},{5,7},{6,4},{7,5},{8,10},{9,11},{10,... | collective-permute-start | bytes 1572872 | tf_op jit(solution)/shard_map/ppermute | solution.py:737
  191.7 2.3 collective-permute-start.21
  191.8 45.5 %collective-permute-start.31 = (bf16[256,1024]{1,0:T(8,128)(2,1)}, bf16[256,1024]{1,0:T(8,128)(2,1)}, u32[]{:S(2)}, u32[]{:S(2)}) collective-permute-start(bf16[256,1024]{1,0:T(8,128)(2,1)} %get-tuple-element.275.refs_17_.near_skip), channel_id=1, source_target_pairs={{0,1},{1,0},{2,3},{3,2},{4,5},{5,4},{6,7},{7,6},{8,9},{9,8},{10,11... | collective-permute-start | bytes 1572872 | tf_op jit(solution)/shard_map/ppermute | solution.py:737
  192.3 34.5 %collective-permute-start.30 = (bf16[4,128,1152]{2,1,0:T(8,128)(2,1)}, bf16[4,128,1152]{2,1,0:T(8,128)(2,1)S(1)}, u32[]{:S(2)}, u32[]{:S(2)}) collective-permute-start(bf16[4,128,1152]{2,1,0:T(8,128)(2,1)} %copy-done.18), channel_id=1, source_target_pairs={{0,4},{4,0},{8,12},{12,8},{16,20},{20,16},{24,28},{28,24},{1,5},{5... | collective-permute-start | bytes 3538952 | tf_op jit(solution)/shard_map/ppermute | solution.py:737
  192.3 15.0 %collective-permute-start.20 = (bf16[256,1024]{1,0:T(8,128)(2,1)}, bf16[256,1024]{1,0:T(8,128)(2,1)S(1)}, u32[]{:S(2)}, u32[]{:S(2)}) collective-permute-start(bf16[256,1024]{1,0:T(8,128)(2,1)} %get-tuple-element.240), channel_id=1, source_target_pairs={{0,1},{1,0},{2,3},{3,2},{4,5},{5,4},{6,7},{7,6},{8,9},{9,8},{10,11... | collective-permute-start | bytes 1572872 | tf_op jit(solution)/shard_map/ppermute | solution.py:737
  192.4 15.0 %collective-permute-start.28 = (bf16[256,1024]{1,0:T(8,128)(2,1)}, bf16[256,1024]{1,0:T(8,128)(2,1)S(1)}, u32[]{:S(2)}, u32[]{:S(2)}) collective-permute-start(bf16[256,1024]{1,0:T(8,128)(2,1)} %get-tuple-element.264), channel_id=1, source_target_pairs={{0,1},{1,0},{2,3},{3,2},{4,5},{5,4},{6,7},{7,6},{8,9},{9,8},{10,11... | collective-permute-start | bytes 1572872 | tf_op jit(solution)/shard_map/ppermute | solution.py:737
  197.0 14.2 %collective-permute-start.25 = (bf16[256,1024]{1,0:T(8,128)(2,1)}, bf16[256,1024]{1,0:T(8,128)(2,1)S(1)}, u32[]{:S(2)}, u32[]{:S(2)}) collective-permute-start(bf16[256,1024]{1,0:T(8,128)(2,1)} %get-tuple-element.257.refs_18_.far_skip), channel_id=1, source_target_pairs={{0,2},{1,3},{2,0},{3,1},{4,6},{5,7},{6,4},{7,5},{8,10},{9,11},{10,... | collective-permute-start | bytes 1572872 | tf_op jit(solution)/shard_map/ppermute | solution.py:737
  207.3 26.7 %copy-start.42 = (bf16[256,1024]{1,0:T(8,128)(2,1)S(1)}, bf16[256,1024]{1,0:T(8,128)(2,1)}, u32[]{:S(2)}) copy-start(bf16[256,1024]{1,0:T(8,128)(2,1)} %get-tuple-element.263) | copy-start | bytes 1572868
  207.3 30.9 %collective-permute-start.33 = (bf16[256,1024]{1,0:T(8,128)(2,1)}, bf16[256,1024]{1,0:T(8,128)(2,1)S(1)}, u32[]{:S(2)}, u32[]{:S(2)}) collective-permute-start(bf16[256,1024]{1,0:T(8,128)(2,1)} %collective-permute-done.24.refs_21_), channel_id=1, source_target_pairs={{0,1},{1,0},{2,3},{3,2},{4,5},{5,4},{6,7},{7,6},{8,9},{9,8},{10,11... | collective-permute-start | bytes 1572872 | tf_op jit(solution)/shard_map/ppermute | solution.py:737
  207.4 32.0 %collective-permute-start.32 = (bf16[256,1024]{1,0:T(8,128)(2,1)S(1)}, bf16[256,1024]{1,0:T(8,128)(2,1)S(1)}, u32[]{:S(2)}, u32[]{:S(2)}) collective-permute-start(bf16[256,1024]{1,0:T(8,128)(2,1)S(1)} %copy-done.28), channel_id=1, source_target_pairs={{0,1},{1,0},{2,3},{3,2},{4,5},{5,4},{6,7},{7,6},{8,9},{9,8},{10,11... | collective-permute-start | bytes 1572872 | tf_op jit(solution)/shard_map/ppermute | solution.py:737
  211.2 28.1 %copy-start.32 = (bf16[256,1024]{1,0:T(8,128)(2,1)}, bf16[256,1024]{1,0:T(8,128)(2,1)S(1)}, u32[]{:S(2)}) copy-start(bf16[256,1024]{1,0:T(8,128)(2,1)S(1)} %collective-permute-done.25.refs_22_) | copy-start | bytes 1572868
  211.2 28.2 %collective-permute-start.34 = (bf16[256,1024]{1,0:T(8,128)(2,1)S(1)}, bf16[256,1024]{1,0:T(8,128)(2,1)S(1)}, u32[]{:S(2)}, u32[]{:S(2)}) collective-permute-start(bf16[256,1024]{1,0:T(8,128)(2,1)S(1)} %collective-permute-done.25.refs_22_), channel_id=1, source_target_pairs={{0,1},{1,0},{2,3},{3,2},{4,5},{5,4},{6,7},{7,6},{8,9},{9,8},{10,11... | collective-permute-start | bytes 1572872 | tf_op jit(solution)/shard_map/ppermute | solution.py:737
  227.8 52.9 %collective-permute-start.36 = (bf16[4,128,1152]{2,1,0:T(8,128)(2,1)}, bf16[4,128,1152]{2,1,0:T(8,128)(2,1)S(1)}, u32[]{:S(2)}, u32[]{:S(2)}) collective-permute-start(bf16[4,128,1152]{2,1,0:T(8,128)(2,1)} %get-tuple-element.278), channel_id=1, source_target_pairs={{0,8},{4,12},{8,0},{12,4},{16,24},{20,28},{24,16},{28,20},{1,9},{5... | collective-permute-start | bytes 3538952 | tf_op jit(solution)/shard_map/ppermute | solution.py:737
  237.3 48.3 %collective-permute-start.26 = (bf16[256,1024]{1,0:T(8,128)(2,1)}, bf16[256,1024]{1,0:T(8,128)(2,1)}, u32[]{:S(2)}, u32[]{:S(2)}) collective-permute-start(bf16[256,1024]{1,0:T(8,128)(2,1)} %add_convert_fusion.4), channel_id=1, source_target_pairs={{0,2},{1,3},{2,0},{3,1},{4,6},{5,7},{6,4},{7,5},{8,10},{9,11},{10,... | collective-permute-start | bytes 1572872 | tf_op jit(solution)/shard_map/ppermute | solution.py:737
  238.2 47.4 %collective-permute-start.29 = (bf16[256,1024]{1,0:T(8,128)(2,1)}, bf16[256,1024]{1,0:T(8,128)(2,1)}, u32[]{:S(2)}, u32[]{:S(2)}) collective-permute-start(bf16[256,1024]{1,0:T(8,128)(2,1)} %add_convert_fusion.2), channel_id=1, source_target_pairs={{0,2},{1,3},{2,0},{3,1},{4,6},{5,7},{6,4},{7,5},{8,10},{9,11},{10,... | collective-permute-start | bytes 1572872 | tf_op jit(solution)/shard_map/ppermute | solution.py:737
  239.3 41.4 %collective-permute-start.35 = (bf16[2,128,1152]{2,1,0:T(8,128)(2,1)}, bf16[2,128,1152]{2,1,0:T(8,128)(2,1)S(1)}, u32[]{:S(2)}, u32[]{:S(2)}) collective-permute-start(bf16[2,128,1152]{2,1,0:T(8,128)(2,1)} %get-tuple-element.274), channel_id=1, source_target_pairs={{0,8},{4,12},{8,0},{12,4},{16,24},{20,28},{24,16},{28,20},{1,9},{5... | collective-permute-start | bytes 1769480 | tf_op jit(solution)/shard_map/ppermute | solution.py:737
  283.5 26.7 %collective-permute-start.38 = (bf16[2,128,1152]{2,1,0:T(8,128)(2,1)}, bf16[2,128,1152]{2,1,0:T(8,128)(2,1)S(1)}, u32[]{:S(2)}, u32[]{:S(2)}) collective-permute-start(bf16[2,128,1152]{2,1,0:T(8,128)(2,1)} %get-tuple-element.287), channel_id=1, source_target_pairs={{0,4},{4,0},{8,12},{12,8},{16,20},{20,16},{24,28},{28,24},{1,5},{5... | collective-permute-start | bytes 1769480 | tf_op jit(solution)/shard_map/ppermute | solution.py:737
  285.4 24.8 %collective-permute-start.39 = (bf16[4,128,512]{2,1,0:T(8,128)(2,1)}, bf16[4,128,512]{2,1,0:T(8,128)(2,1)S(1)}, u32[]{:S(2)}, u32[]{:S(2)}) collective-permute-start(bf16[4,128,512]{2,1,0:T(8,128)(2,1)} %get-tuple-element.289), channel_id=1, source_target_pairs={{0,4},{4,0},{8,12},{12,8},{16,20},{20,16},{24,28},{28,24},{1,5},{5... | collective-permute-start | bytes 1572872 | tf_op jit(solution)/shard_map/ppermute | solution.py:737
  285.6 24.7 %collective-permute-start.37 = (bf16[1,128,1152]{2,1,0:T(8,128)(2,1)}, bf16[1,128,1152]{2,1,0:T(8,128)(2,1)S(1)}, u32[]{:S(2)}, u32[]{:S(2)}) collective-permute-start(bf16[1,128,1152]{2,1,0:T(8,128)(2,1)} %get-tuple-element.285), channel_id=1, source_target_pairs={{0,16},{4,20},{8,24},{12,28},{16,0},{20,4},{24,8},{28,12},{1,17},{... | collective-permute-start | bytes 884744 | tf_op jit(solution)/shard_map/ppermute | solution.py:737
  317.6 4.4 %collective-permute-start.40 = (bf16[2,512,1024]{2,1,0:T(8,128)(2,1)}, bf16[2,512,1024]{2,1,0:T(8,128)(2,1)S(1)}, u32[]{:S(2)}, u32[]{:S(2)}) collective-permute-start(bf16[2,512,1024]{2,1,0:T(8,128)(2,1)} %get-tuple-element.298), channel_id=1, source_target_pairs={{0,1},{1,0},{2,3},{3,2},{4,5},{5,4},{6,7},{7,6},{8,9},{9,8},{10,11... | collective-permute-start | bytes 6291464 | tf_op jit(solution)/shard_map/ppermute | solution.py:737
  317.6 26.9 %collective-permute-start.19 = (bf16[256,1024]{1,0:T(8,128)(2,1)}, bf16[256,1024]{1,0:T(8,128)(2,1)S(1)}, u32[]{:S(2)}, u32[]{:S(2)}) collective-permute-start(bf16[256,1024]{1,0:T(8,128)(2,1)} %get-tuple-element.238), channel_id=1, source_target_pairs={{0,1},{1,0},{2,3},{3,2},{4,5},{5,4},{6,7},{7,6},{8,9},{9,8},{10,11... | collective-permute-start | bytes 1572872 | tf_op jit(solution)/shard_map/ppermute | solution.py:737
  318.1 33.3 %collective-permute-start.27 = (bf16[256,1024]{1,0:T(8,128)(2,1)}, bf16[256,1024]{1,0:T(8,128)(2,1)S(1)}, u32[]{:S(2)}, u32[]{:S(2)}) collective-permute-start(bf16[256,1024]{1,0:T(8,128)(2,1)} %get-tuple-element.262), channel_id=1, source_target_pairs={{0,1},{1,0},{2,3},{3,2},{4,5},{5,4},{6,7},{7,6},{8,9},{9,8},{10,11... | collective-permute-start | bytes 1572872 | tf_op jit(solution)/shard_map/ppermute | solution.py:737
  318.2 12.4 %collective-permute-start.43 = (bf16[2,128,512]{2,1,0:T(8,128)(2,1)S(1)}, bf16[2,128,512]{2,1,0:T(8,128)(2,1)S(1)}, u32[]{:S(2)}, u32[]{:S(2)}) collective-permute-start(bf16[2,128,512]{2,1,0:T(8,128)(2,1)S(1)} %get-tuple-element.295), channel_id=1, source_target_pairs={{0,8},{4,12},{8,0},{12,4},{16,24},{20,28},{24,16},{28,20},{1,9},{5... | collective-permute-start | bytes 786440 | tf_op jit(solution)/shard_map/ppermute | solution.py:737
  318.2 16.6 %collective-permute-start.42 = (bf16[1,128,1152]{2,1,0:T(8,128)(2,1)S(1)}, bf16[1,128,1152]{2,1,0:T(8,128)(2,1)S(1)}, u32[]{:S(2)}, u32[]{:S(2)}) collective-permute-start(bf16[1,128,1152]{2,1,0:T(8,128)(2,1)S(1)} %get-tuple-element.294), channel_id=1, source_target_pairs={{0,16},{4,20},{8,24},{12,28},{16,0},{20,4},{24,8},{28,12},{1,17},{... | collective-permute-start | bytes 884744 | tf_op jit(solution)/shard_map/ppermute | solution.py:737
  324.4 41.4 %collective-permute-start.41 = (bf16[512,1024]{1,0:T(8,128)(2,1)S(1)}, bf16[512,1024]{1,0:T(8,128)(2,1)S(1)}, u32[]{:S(2)}, u32[]{:S(2)}) collective-permute-start(bf16[512,1024]{1,0:T(8,128)(2,1)S(1)} %fusion.10), channel_id=1, source_target_pairs={{0,2},{1,3},{2,0},{3,1},{4,6},{5,7},{6,4},{7,5},{8,10},{9,11},{10,... | collective-permute-start | bytes 3145736 | tf_op jit(solution)/shard_map/ppermute | solution.py:737
  335.6 10.3 %collective-permute-start.44 = (bf16[1,128,512]{2,1,0:T(8,128)(2,1)S(1)}, bf16[1,128,512]{2,1,0:T(8,128)(2,1)S(1)}, u32[]{:S(2)}, u32[]{:S(2)}) collective-permute-start(bf16[1,128,512]{2,1,0:T(8,128)(2,1)S(1)} %get-tuple-element.310), channel_id=1, source_target_pairs={{0,16},{4,20},{8,24},{12,28},{16,0},{20,4},{24,8},{28,12},{1,17},{... | collective-permute-start | bytes 393224 | tf_op jit(solution)/shard_map/ppermute | solution.py:737
  335.6 25.2 %copy-start.9 = (bf16[128,1152]{1,0:T(8,128)(2,1)S(1)}, bf16[128,1152]{1,0:T(8,128)(2,1)}, u32[]{:S(2)}) copy-start(bf16[128,1152]{1,0:T(8,128)(2,1)} %reduce-scatter.2.cloned.1.call-done.refs_8_) | copy-start | bytes 884740
  335.6 25.2 %copy-start.14 = (f32[1,1024]{1,0:T(1,128)S(1)}, f32[1,1024]{1,0:T(1,128)}, u32[]{:S(2)}) copy-start(f32[1,1024]{1,0:T(1,128)} %get-tuple-element.300.refs_0_) | copy-start | bytes 12292
  335.7 25.2 %copy-start.15 = (f32[1,1024]{1,0:T(1,128)S(1)}, f32[1,1024]{1,0:T(1,128)}, u32[]{:S(2)}) copy-start(f32[1,1024]{1,0:T(1,128)} %get-tuple-element.301.refs_1_) | copy-start | bytes 12292
  335.7 25.2 %copy-start.16 = (f32[1,128]{1,0:T(1,128)S(1)}, f32[1,128]{1,0:T(1,128)}, u32[]{:S(2)}) copy-start(f32[1,128]{1,0:T(1,128)} %get-tuple-element.282.refs_2_) | copy-start | bytes 1540
  335.7 25.2 %copy-start.17 = (f32[1,128]{1,0:T(1,128)S(1)}, f32[1,128]{1,0:T(1,128)}, u32[]{:S(2)}) copy-start(f32[1,128]{1,0:T(1,128)} %get-tuple-element.302.refs_3_) | copy-start | bytes 1540
  335.7 15.1 %collective-permute-start.45 = (bf16[4,128,256]{2,1,0:T(8,128)(2,1)S(1)}, bf16[4,128,256]{2,1,0:T(8,128)(2,1)S(1)}, u32[]{:S(2)}, u32[]{:S(2)}) collective-permute-start(bf16[4,128,256]{2,1,0:T(8,128)(2,1)S(1)} %get-tuple-element.312), channel_id=1, source_target_pairs={{0,4},{4,0},{8,12},{12,8},{16,20},{20,16},{24,28},{28,24},{1,5},{5... | collective-permute-start | bytes 786440 | tf_op jit(solution)/shard_map/ppermute | solution.py:737
  351.4 5.0 %collective-permute-start.46 = (bf16[2,128,256]{2,1,0:T(8,128)(2,1)S(1)}, bf16[2,128,256]{2,1,0:T(8,128)(2,1)S(1)}, u32[]{:S(2)}, u32[]{:S(2)}) collective-permute-start(bf16[2,128,256]{2,1,0:T(8,128)(2,1)S(1)} %get-tuple-element.315), channel_id=1, source_target_pairs={{0,8},{4,12},{8,0},{12,4},{16,24},{20,28},{24,16},{28,20},{1,9},{5... | collective-permute-start | bytes 393224 | tf_op jit(solution)/shard_map/ppermute | solution.py:737
  356.9 7.7 %collective-permute-start.47 = (bf16[1,128,256]{2,1,0:T(8,128)(2,1)S(1)}, bf16[1,128,256]{2,1,0:T(8,128)(2,1)S(1)}, u32[]{:S(2)}, u32[]{:S(2)}) collective-permute-start(bf16[1,128,256]{2,1,0:T(8,128)(2,1)S(1)} %get-tuple-element.319), channel_id=1, source_target_pairs={{0,16},{4,20},{8,24},{12,28},{16,0},{20,4},{24,8},{28,12},{1,17},{... | collective-permute-start | bytes 196616 | tf_op jit(solution)/shard_map/ppermute | solution.py:737
  371.7 3.3 collective-permute-start.50
  371.8 3.9 collective-permute-start.49
  372.9 2.8 collective-permute-start.48
  376.4 4.6 %collective-permute-start.53 = (f32[1,2304]{1,0:T(1,128)S(1)}, f32[1,2304]{1,0:T(1,128)S(1)}, u32[]{:S(2)}, u32[]{:S(2)}) collective-permute-start(f32[1,2304]{1,0:T(1,128)S(1)} %add_add_fusion.1), channel_id=1, source_target_pairs={{0,12},{4,8},{8,4},{12,0},{16,28},{20,24},{24,20},{28,16},{1,13},{... | collective-permute-start | bytes 27656 | tf_op jit(solution)/shard_map/ppermute | solution.py:737
  377.5 4.2 %collective-permute-start.52 = (f32[1,2304]{1,0:T(1,128)S(1)}, f32[1,2304]{1,0:T(1,128)S(1)}, u32[]{:S(2)}, u32[]{:S(2)}) collective-permute-start(f32[1,2304]{1,0:T(1,128)S(1)} %add_add_fusion.1), channel_id=1, source_target_pairs={{0,8},{4,12},{8,0},{12,4},{16,24},{20,28},{24,16},{28,20},{1,9},{5... | collective-permute-start | bytes 27656 | tf_op jit(solution)/shard_map/ppermute | solution.py:737
  380.0 3.7 collective-permute-start.51
  383.7 4.6 %collective-permute-start.54 = (f32[1,2304]{1,0:T(1,128)S(1)}, f32[1,2304]{1,0:T(1,128)S(1)}, u32[]{:S(2)}, u32[]{:S(2)}) collective-permute-start(f32[1,2304]{1,0:T(1,128)S(1)} %add_add_fusion), channel_id=1, source_target_pairs={{0,16},{4,20},{8,24},{12,28},{16,0},{20,4},{24,8},{28,12},{1,17},{... | collective-permute-start | bytes 27656 | tf_op jit(solution)/shard_map/ppermute | solution.py:737
  (48 other events, 372.0 us)
Sparse Core Ops, SparseCore 0:
  191.8 81.3 reduce-scatter.1
where the time goes:
time: 406 us; the launch traced here: 407 us
  Pallas kernels  199 us (49%)
  waiting for transfers between devices  59.4 us (15%)
  starting transfers between devices  49.8 us (12%)
  matrix products  36.9 us (9%)
  local copies, waits for them, and re-layouts  26.9 us (7%)
  other arithmetic  19.2 us (5%)
  between operations  15.6 us (4%)
    pallas_call x4, Pallas kernels, feed(): pl.pallas_call(feed_kernel, grid=(1,), in_specs=[pl.BlockSpec((block, wid...  60.9 us
    ppermute x55, waiting for transfers between devices, exchange(): return lax.ppermute(value, axis, [(i, i ^ bit) for i in range(size)])  59.3 us
    pallas_call x2, Pallas kernels, attend_back(): pl.pallas_call(lambda *refs: attend_back_kernel(pieces, *refs), grid_spec...  51.1 us
    ppermute x55, starting transfers between devices, exchange(): return lax.ppermute(value, axis, [(i, i ^ bit) for i in range(size)])  49.8 us
    dot_general x6, matrix products, contract_rows(): lax.dot_general(left, right, (((0,), (0,)), ((), ())), preferred_element_...  36.9 us
    pallas_call x2, Pallas kernels, attend(): pl.pallas_call(lambda *refs: attend_kernel(half, *refs), grid_spec=pltpu....  31.5 us
    unnamed x114, local copies, waits for them, and re-layouts  21.4 us
    pallas_call x2, Pallas kernels, project(): pl.pallas_call(project_kernel, grid_spec=pltpu.PrefetchScalarGridSpec(num...  14.2 us
  transfers between devices with their start and end apart: 56, of which 21 were waited for; matrix products, arithmetic and copies ran while one was open for 16% of the time, Pallas kernels for 43%

commit v1 on v0

--- a/solution.py
+++ b/solution.py
@@ -503,31 +503,52 @@
     )(place, *rows, *rows, weight)
 
 
-def feed_kernel(*refs):
-    xs, grads, joint_ref, down_ref = refs[:2], refs[2:4], refs[4], refs[5]
-    x_ref, grad_ref, hidden_ref, low_ref, out_keep, out_send, back_keep, back_send = refs[-8:]
+def feed_kernel(call, *refs):
+    xs, grads, joint_hbm, down_hbm = refs[:2], refs[2:4], refs[4], refs[5]
+    (x_full, grad_full, hidden_full, low_full, out_keep, out_send, back_keep, back_send,
+     x_ref, grad_ref, hidden_ref, low_ref, joint_ref, down_ref, sems) = refs[-15:]
     hidden_width = down_ref.shape[0]
     block = xs[0].shape[0]
+    cut = (hidden_width + 255) // 256 * 256
+    rows = pl.ds(call * 2 * block, 2 * block)
+
+    def copy(source, target, k):
+        item = pltpu.make_async_copy(source, target, sems.at[k])
+        item.start()
+        return item
+
+    first = copy(joint_hbm.at[:, :cut], joint_ref.at[:, :cut], 0)
+    second = copy(joint_hbm.at[:, cut:], joint_ref.at[:, cut:], 1)
+    third = copy(down_hbm, down_ref, 2)
     for r in range(2):
         x_ref[r * block : (r + 1) * block, :] = xs[r][...]
         grad_ref[r * block : (r + 1) * block, :] = grads[r][...]
-    both = dot_nn(x_ref[...], joint_ref[...])
-    gate, up = (both[:, :hidden_width], both[:, hidden_width:])
+    stores = [copy(x_ref, x_full.at[rows, :], 3), copy(grad_ref, grad_full.at[rows, :], 4)]
+    first.wait()
+    left = dot_nn(x_ref[...], joint_ref[:, :cut])
+    second.wait()
+    right = dot_nn(x_ref[...], joint_ref[:, cut:])
+    gate = left[:, :hidden_width]
+    up = jnp.concatenate([left[:, hidden_width:], right], axis=1)
     sigmoid = 1.0 / (1.0 + jnp.exp(-gate))
     swish = gate * sigmoid
-    hidden = (swish * up).astype(jnp.bfloat16)
-    hidden_ref[...] = hidden
+    hidden_ref[...] = (swish * up).astype(jnp.bfloat16)
+    stores.append(copy(hidden_ref, hidden_full.at[rows, :], 5))
+    third.wait()
     hidden_grad = dot_nt(grad_ref[...], down_ref[...])
     low_ref[:, :hidden_width] = (
         hidden_grad * up * sigmoid * (1.0 + gate * (1.0 - sigmoid))
     ).astype(jnp.bfloat16)
     low_ref[:, hidden_width:] = (hidden_grad * swish).astype(jnp.bfloat16)
-    out = dot_nn(hidden, down_ref[...]).astype(jnp.bfloat16)
+    stores.append(copy(low_ref, low_full.at[rows, :], 6))
+    out = dot_nn(hidden_ref[...], down_ref[...]).astype(jnp.bfloat16)
     out_keep[...] = out[:block]
     out_send[...] = out[block:]
     back = dot_nt(low_ref[...], joint_ref[...]).astype(jnp.bfloat16)
     back_keep[...] = back[:block]
     back_send[...] = back[block:]
+    for item in stores:
+        item.wait()
 
 
 def feed(call, half, earlier, normed, grads, joint_weight, down_weight):
@@ -535,20 +556,25 @@
     hidden_width = down_weight.shape[0]
     length = block * PIECES * HALVES
     once = pl.Buffered(1)
-    row = lambda columns: pl.BlockSpec((2 * block, columns), lambda i: (call, 0))
-    whole = lambda value: pl.BlockSpec(value.shape, lambda i: (0, 0), pipeline_mode=once)
     pair = pl.BlockSpec((block, width), lambda i: (0, 0))
     full = lambda columns: jax.ShapeDtypeStruct((length, columns), jnp.bfloat16)
+    any_space = pl.BlockSpec(memory_space=pl.ANY)
+    rows = lambda columns: pltpu.VMEM((2 * block, columns), jnp.bfloat16)
     outs = pl.pallas_call(
-        feed_kernel,
+        lambda *refs: feed_kernel(call, *refs),
         grid=(1,),
         in_specs=[pl.BlockSpec((block, width), lambda i: (0, 0), pipeline_mode=once)] * 2
         + [pl.BlockSpec((block, width), lambda i: (half, 0), pipeline_mode=once)] * 2
-        + [whole(joint_weight), whole(down_weight)]
-        + [pl.BlockSpec(memory_space=pl.ANY)] * len(earlier),
-        out_specs=[row(width), row(width), row(hidden_width), row(2 * hidden_width)] + [pair] * 4,
+        + [any_space] * (2 + len(earlier)),
+        out_specs=[any_space] * 4 + [pair] * 4,
         out_shape=[full(width), full(width), full(hidden_width), full(2 * hidden_width)]
         + [jax.ShapeDtypeStruct((block, width), jnp.bfloat16)] * 4,
+        scratch_shapes=[
+            rows(width), rows(width), rows(hidden_width), rows(2 * hidden_width),
+            pltpu.VMEM(joint_weight.shape, jnp.bfloat16),
+            pltpu.VMEM(down_weight.shape, jnp.bfloat16),
+            pltpu.SemaphoreType.DMA((7,)),
+        ],
         input_output_aliases={6 + k: k for k in range(len(earlier))},
         compiler_params=params(),
         cost_estimate=cost(3 * length * width * hidden_width, 16 * MIB),
@@ -1058,8 +1084,7 @@
     normed_two = after(normed_two, pieces_dh[1][0])
     up_grad = contract_rows(normed_two, flat_low[:, hidden_width:])
     up = ScatterSum([up_grad.astype(jnp.bfloat16)], [(hidden_width, False)], True)
-    advance(here, [up], pieces_dh[1][2])
-    sent, _ = advance(here, [gate], up.sources[0])
+    sent, _ = advance(here, [up], pieces_dh[1][2])
 
     dh = [pieces_dh[half][r] for r in range(PIECES) for half in range(HALVES)]
     dh[0] = after(dh[0], *sent, *[item[2] for item in out_sums])
@@ -1100,14 +1125,12 @@
     passed = (keep, near, added(keep[1], near[1]))
     keep, near, far = across_of(passed)
     late = ScatterSum(late, [(joints[0].shape[1] * (groups - 1), False)])
-    pending = [gate, up, early, late]
-    gates = [passed[2]]
-    while pending:
-        pending = [item for item in pending if item.total is None]
-        _, square = advance(here, pending, *gates)
+    advance(here, [late], passed[2])
+    pending = [early, late]
+    while pending != [late]:
+        _, square = advance(here, pending)
         squares.append(square)
-        pending = [item for item in pending if item.total is None]
-        gates = []
+        pending = [item for item in (gate, up, early, late) if item.total is None]
 
     results = []
     for half in range(HALVES):
@@ -1117,9 +1140,13 @@
     result = jnp.concatenate(results, axis=0).astype(jnp.bfloat16)
 
     ffn_parts = [after(ffn_parts[0], result), *ffn_parts[1:]]
-    row, down_total = row_of(ffn_parts, head_parts, squares[1:-1], down_sum)
+    row, down_total = row_of(ffn_parts, head_parts, squares, down_sum)
+    gates = [row]
+    while late.total is None:
+        _, square = advance(here, [late], *gates)
+        gates = []
     skips = [pieces[0] for pieces in pieces_dh]
-    input_grad, row = finish(tokens, skips, keep, near, far, attn_gain, row, squares[-1])
+    input_grad, row = finish(tokens, skips, keep, near, far, attn_gain, row, square)
     summed = sum_all(row)
     entries = gains.shape[0]
     out_fan = max(QH * HD * 16 // length, 16)

time: 406 us -> 397 us (0.978); the launches traced: 407 us -> 390 us
  waiting for transfers between devices: 59.4 us -> 49.2 us
  starting transfers between devices: 49.8 us -> 41.2 us
    ppermute x55, waiting for transfers between devices: 59.3 us -> 49.2 us  [exchange(): return lax.ppermute(value, axis, [(i, i ^ bit) for i in range(size)])]
    ppermute x55, starting transfers between devices: 49.8 us -> 41.1 us  [exchange(): return lax.ppermute(value, axis, [(i, i ^ bit) for i in range(size)])]
    unnamed x114 -> x132, local copies, waits for them, and re-layouts: 21.4 us -> 23.3 us
    pallas_call x9 -> x8, Pallas kernels: 7.68 us -> 8.34 us  [advance(): pl.pallas_call(lambda *refs: advance_kernel(plans, *refs), in_specs=[pl.B...]
  transfers between devices with their start and end apart: 56 -> 56, of which waited for: 21 -> 20; matrix products, arithmetic and copies ran while one was open for 16% -> 17% of each run, Pallas kernels for 43% -> 45%
where the time goes in v1:
time: 397 us; the launch traced here: 390 us
  Pallas kernels  198 us (50%)
  waiting for transfers between devices  49.2 us (12%)
  starting transfers between devices  41.2 us (10%)
  matrix products  36.8 us (9%)
  local copies, waits for them, and re-layouts  28.8 us (7%)
  other arithmetic  20.1 us (5%)
  between operations  15.6 us (4%)
    pallas_call x4, Pallas kernels, feed(): pl.pallas_call(lambda *refs: feed_kernel(call, *refs), grid=(1,), in_spec...  58.6 us
    pallas_call x2, Pallas kernels, attend_back(): pl.pallas_call(lambda *refs: attend_back_kernel(pieces, *refs), grid_spec...  51.4 us
    ppermute x55, waiting for transfers between devices, exchange(): return lax.ppermute(value, axis, [(i, i ^ bit) for i in range(size)])  49.2 us
    ppermute x55, starting transfers between devices, exchange(): return lax.ppermute(value, axis, [(i, i ^ bit) for i in range(size)])  41.1 us
    dot_general x6, matrix products, contract_rows(): lax.dot_general(left, right, (((0,), (0,)), ((), ())), preferred_element_...  36.8 us
    pallas_call x2, Pallas kernels, attend(): pl.pallas_call(lambda *refs: attend_kernel(half, *refs), grid_spec=pltpu....  31.5 us
    unnamed x132, local copies, waits for them, and re-layouts  23.3 us
    pallas_call x2, Pallas kernels, project(): pl.pallas_call(project_kernel, grid_spec=pltpu.PrefetchScalarGridSpec(num...  14.2 us
  transfers between devices with their start and end apart: 56, of which 20 were waited for; matrix products, arithmetic and copies ran while one was open for 17% of the time, Pallas kernels for 45%

profile of v1, /device:TPU:0, one launch (start us, length us, event | category | flops | bytes accessed | tf_op | source)
XLA Modules:
  0.0 389.6 jit_solution(17636727989987258436)
XLA Ops:
  7.8 2.6 collective-permute-start
  10.3 1.3 slice.66
  12.4 1.5 select_bitcast_fusion
  15.0 2.3 copy.69
  17.4 1.3 fusion.17
  18.8 1.8 multiply_sine_fusion
  21.6 7.1 %project.2 = (bf16[2048,1024]{1,0:T(8,128)(2,1)}, f32[8,64,2048]{2,1,0:T(8,128)}, bf16[8,64,2048]{2,1,0:T(8,128)(2,1)}, bf16[8,2048,64]{2,1,0:T(8,128)(2,1)}) custom-call(s32[1]{0:T(128)} %bitcast.2.place_ref.refs_2_.refs_0_, bf16[512,1024]{1,0:T(8,128)(2,1)} %x_ref.5, bf16[512,1024]{1,0:T(8,128)(2,1)} %copy-done.39, f32[1,1024]{1,0:T(1,128)} %bitcast.86, ...), custom_call_target="tpu_custom_call" | custom-call | flops 134217728 | bytes 1048576 | tf_op jit(solution)/shard_map/project/pallas_call | solution.py:139
  28.7 5.4 %copy.74 = bf16[128,8,2,1152]{3,1,2,0:T(8,128)(2,1)} copy(bf16[128,8,2,1152]{3,2,1,0:T(2,128)(2,1)} %bitcast.75) | data formatting | bytes 9437184
  34.3 1.8 collective-permute-start.3
  37.3 7.1 %project.3 = (bf16[2048,1024]{1,0:T(8,128)(2,1)}, f32[8,64,2048]{2,1,0:T(8,128)}, bf16[8,64,2048]{2,1,0:T(8,128)(2,1)}, bf16[8,2048,64]{2,1,0:T(8,128)(2,1)}) custom-call(s32[1]{0:T(128)} %bitcast.2.place_ref.refs_2_.refs_0_, bf16[512,1024]{1,0:T(8,128)(2,1)} %copy-done.38, ...), custom_call_target="tpu_custom_call", output_to_operand_aliasing={{0}: (8, {}), {1}: (9, {}), {2}: (10, {}), {3}: (11, {})} | custom-call | flops 134217728 | bytes 1048576 | tf_op jit(solution)/shard_map/project/pallas_call | solution.py:139
  44.4 14.2 %attend.2 = (bf16[2048,256]{1,0:T(8,128)(2,1)}, bf16[256,2048]{1,0:T(8,128)(2,1)}, f32[2,2,1,2048]{3,2,1,0:T(1,128)}, bf16[2,256,1024]{2,1,0:T(8,128)(2,1)}, bf16[2,256,1024]{2,1,0:T(8,128)(2,1)}) custom-call(s32[8]{0:T(128)} %slice.70.refs_0_, s32[8]{0:T(128)} %slice.71.refs_1_, s32[1]{0:T(128)} %bitcast.2.place_ref.refs_2_.refs_0_, ...), custom_call_target="tpu_custom_call" | custom-call | flops 536870912 | bytes 786432 | tf_op jit(solution)/shard_map/attend/pallas_call | solution.py:261
  58.6 1.2 collective-permute-done.3.refs_2_
  59.9 2.9 collective-permute-done.4.near_ref
  62.8 1.6 fusion.11
  64.3 1.8 collective-permute-start.5
  66.2 17.3 %attend.3 = (bf16[2048,256]{1,0:T(8,128)(2,1)}, bf16[256,2048]{1,0:T(8,128)(2,1)}, f32[2,2,1,2048]{3,2,1,0:T(1,128)}, bf16[2,256,1024]{2,1,0:T(8,128)(2,1)}, bf16[2,256,1024]{2,1,0:T(8,128)(2,1)}) custom-call(s32[8]{0:T(128)} %slice.70.refs_0_, s32[8]{0:T(128)} %slice.71.refs_1_, ...), custom_call_target="tpu_custom_call", output_to_operand_aliasing={{0}: (8, {}), {1}: (9, {}), {2}: (10, {})} | custom-call | flops 536870912 | bytes 786432 | tf_op jit(solution)/shard_map/attend/pallas_call | solution.py:261
  84.0 3.0 norm.2
  87.6 2.2 fusion.12
  89.8 14.6 %feed.4 = (bf16[2048,1024]{1,0:T(8,128)(2,1)}, bf16[2048,1024]{1,0:T(8,128)(2,1)}, bf16[2048,1152]{1,0:T(8,128)(2,1)}, bf16[2048,2304]{1,0:T(8,128)(2,1)}, bf16[...) custom-call(bf16[256,1024]{1,0:T(8,128)(2,1)} %get-tuple-element.205.re, ...), custom_call_target="tpu_custom_call" | custom-call | flops 905969664 | bytes 2097152 | tf_op jit(solution)/shard_map/feed/pallas_call | solution.py:563
  104.8 1.8 collective-permute-start.12
  107.7 14.7 %feed.5 = (bf16[2048,1024]{1,0:T(8,128)(2,1)}, bf16[2048,1024]{1,0:T(8,128)(2,1)}, bf16[2048,1152]{1,0:T(8,128)(2,1)}, bf16[2048,2304]{1,0:T(8,128)(2,1)}, bf16[...) custom-call(bf16[256,1024]{1,0:T(8,128)(2,1)} %copy-done.45, ...), custom_call_target="tpu_custom_call", output_to_operand_aliasing={{0}: (6, {}), {1}: (7, {}), {2}: (8, {}), {3}: (9, {})} | custom-call | flops 905969664 | bytes 2097152 | tf_op jit(solution)/shard_map/feed/pallas_call | solution.py:563
  122.4 2.6 norm.3
  125.0 1.6 collective-permute-start.14
  127.9 14.6 %feed.6 = (bf16[2048,1024]{1,0:T(8,128)(2,1)}, bf16[2048,1024]{1,0:T(8,128)(2,1)}, bf16[2048,1152]{1,0:T(8,128)(2,1)}, bf16[2048,2304]{1,0:T(8,128)(2,1)}, bf16[...) custom-call(bf16[256,1024]{1,0:T(8,128)(2,1)} %get-tuple-element.216, ...), custom_call_target="tpu_custom_call", output_to_operand_aliasing={{0}: (6, {}), {1}: (7, {}), {2}: (8, {}), {3}: (9, {})} | custom-call | flops 905969664 | bytes 2097152 | tf_op jit(solution)/shard_map/feed/pallas_call | solution.py:563
  143.0 1.5 collective-permute-start.17
  145.3 14.8 %feed.7 = (bf16[2048,1024]{1,0:T(8,128)(2,1)}, bf16[2048,1024]{1,0:T(8,128)(2,1)}, bf16[2048,1152]{1,0:T(8,128)(2,1)}, bf16[2048,2304]{1,0:T(8,128)(2,1)}, bf16[...) custom-call(bf16[256,1024]{1,0:T(8,128)(2,1)} %copy-done.42, ...), custom_call_target="tpu_custom_call", output_to_operand_aliasing={{0}: (6, {}), {1}: (7, {}), {2}: (8, {}), {3}: (9, {})} | custom-call | flops 905969664 | bytes 2097152 | tf_op jit(solution)/shard_map/feed/pallas_call | solution.py:563
  161.4 2.9 norm_back.2
  165.5 1.2 add_convert_fusion.5
  167.7 9.9 %convolution_convert_fusion = bf16[1024,1152]{1,0:T(8,128)(2,1)} fusion(bf16[2048,1024]{1,0:T(8,128)(2,1)} %get-tuple-element.251, bf16[2048,1152]{1,0:T(8,128)(2,1)} %get-tuple-element.252), kind=kOutput, calls=%fused_computation.6 | convolution fusion | flops 4833017856 | bytes 11272192 | tf_op jit(solution)/shard_map/dot_general | solution.py:69
  177.6 8.9 %fusion.4 = bf16[1024,1152]{1,0:T(8,128)(2,1)S(1)} fusion(bf16[2048,1024]{1,0:T(8,128)(2,1)} %get-tuple-element.269, bf16[2048,2304]{1,0:T(8,128)(2,1)} %get-tuple-element.254), kind=kOutput, calls=%fused_computation.4 | convolution fusion | flops 4833017856 | bytes 11272192 | tf_op jit(solution)/shard_map/dot_general | solution.py:69
  187.7 2.0 collective-permute-done.22.far_ref
  192.7 2.9 norm_back.3
  195.6 1.3 collective-permute-start.25
  196.9 9.3 %fusion.7 = bf16[1024,1152]{1,0:T(8,128)(2,1)S(1)} fusion(bf16[2048,1024]{1,0:T(8,128)(2,1)} %get-tuple-element.269, bf16[2048,2304]{1,0:T(8,128)(2,1)} %get-tuple-element.254), kind=kOutput, calls=%fused_computation.5 | convolution fusion | flops 4833017856 | bytes 11272192 | tf_op jit(solution)/shard_map/dot_general | solution.py:69
  206.3 3.6 collective-permute-done.25.refs_22_
  212.1 1.7 collective-permute-start.35
  213.8 2.1 add_convert_fusion.2
  218.8 26.6 %attend_back.2 = (bf16[2048,256]{1,0:T(8,128)(2,1)}, f32[1,128]{1,0:T(1,128)}, bf16[2048,1024]{1,0:T(8,128)(2,1)}) custom-call(s32[8]{0:T(128)} %slice.70.refs_0_, s32[8]{0:T(128)} %slice.71.refs_1_, s32[1]{0:T(128)} %bitcast.2.place_ref.refs_2_.refs_0_, bf16[2,4,64,2048]{3,2,1,0:T(8,128)(2,1)} %bitcast.60, bf16[2,4,2048,64]{3,2,1,0:T(8,128)(2,1)} %bitcast.50, ...), custom_call_target="tpu_custom_call" | custom-call | flops 1342177280 | bytes 1572864 | tf_op jit(solution)/shard_map/attend_back/pallas_call | solution.py:424
  245.4 3.9 %convolution_convert_fusion.3 = bf16[1024,256]{1,0:T(8,128)(2,1)S(1)} fusion(bf16[2048,1024]{1,0:T(8,128)(2,1)} %get-tuple-element.287.refs_17_, bf16[2048,256]{1,0:T(8,128)(2,1)} %get-tuple-element.277), kind=kOutput, calls=%fused_computation.10 | convolution fusion | flops 1074003968 | bytes 5767168 | tf_op jit(solution)/shard_map/dot_general | solution.py:69
  249.4 1.3 convolution_convert_fusion.2
  250.8 2.7 advance.10
  255.8 2.3 collective-permute-start.37
  258.2 24.8 %attend_back.3 = (bf16[2048,256]{1,0:T(8,128)(2,1)}, f32[1,128]{1,0:T(1,128)}) custom-call(s32[8]{0:T(128)} %slice.70.refs_0_, s32[8]{0:T(128)} %slice.71.refs_1_, s32[1]{0:T(128)} %bitcast.2.place_ref.refs_2_.refs_0_, bf16[2,4,64,2048]{3,2,1,0:T(8,128)(2,1)} %bitcast.62, bf16[2,4,2048,64]{3,2,1,0:T(8,128)(2,1)} %bitcast.53, ...), custom_call_target="tpu_custom_call" | custom-call | flops 1342177280 | bytes 1572864 | tf_op jit(solution)/shard_map/attend_back/pallas_call | solution.py:424
  286.6 5.3 %spread.1 = (bf16[2,512,1024]{2,1,0:T(8,128)(2,1)}, bf16[2,512,1024]{2,1,0:T(8,128)(2,1)}) custom-call(s32[1]{0:T(128)} %bitcast.2.place_ref.refs_2_.refs_0_, bf16[2048,256]{1,0:T(8,128)(2,1)} %get-tuple-element.294.refs_1_.refs_3_, bf16[2048,256]{1,0:T(8,128)(2,1)} %get-tuple-element.304.refs_2_.refs_4_, ...), custom_call_target="tpu_custom_call" | custom-call | flops 268435456 | bytes 786432 | tf_op jit(solution)/shard_map/spread/pallas_call | solution.py:489
  293.4 2.9 collective-permute-done.39.near_ref
  296.3 2.4 fusion.10
  298.7 1.2 collective-permute-start.40
  300.0 3.5 convolution_convert_fusion.1
  304.9 1.4 add_convert_fusion.3
  307.5 1.9 collective-permute-start.44
  309.4 2.7 collective-permute-done.42.refs_4_
  312.6 1.6 collective-permute-start.45
  314.7 1.4 add_convert_fusion.1
  316.0 15.9 %collective-permute-done.43.refs_2_ = bf16[1,128,1152]{2,1,0:T(8,128)(2,1)S(1)} collective-permute-done((bf16[1,128,1152]{2,1,0:T(8,128)(2,1)S(1)}, bf16[1,128,1152]{2,1,0:T(8,128)(2,1)S(1)}, u32[]{:S(2)}, u32[]{:S(2)}) %collective-permute-start.43) | collective-permute-done | bytes 294944 | tf_op jit(solution)/shard_map/ppermute | solution.py:763
  331.9 6.3 %collective-permute-done.44.refs_4_ = bf16[1,128,1152]{2,1,0:T(8,128)(2,1)S(1)} collective-permute-done((bf16[1,128,1152]{2,1,0:T(8,128)(2,1)S(1)}, bf16[1,128,1152]{2,1,0:T(8,128)(2,1)S(1)}, u32[]{:S(2)}, u32[]{:S(2)}) %collective-permute-start.44) | collective-permute-done | bytes 294944 | tf_op jit(solution)/shard_map/ppermute | solution.py:763
  338.2 2.1 collective-permute-done.45.refs_6_
  344.1 2.8 row.1
  350.4 4.9 %finish.1 = (bf16[512,1024]{1,0:T(8,128)(2,1)}, f32[1,2304]{1,0:T(1,128)}) custom-call(bf16[512,1024]{1,0:T(8,128)(2,1)} %x_ref.5, bf16[256,1024]{1,0:T(8,128)(2,1)} %get-tuple-element.272.refs_17_.near_skip, bf16[256,1024]{1,0:T(8,128)(2,1)} %get-tuple-element.257.refs_18_.far_skip, bf16[2,512,1024]{2,1,0:T(8,128)(2,1)} %get-tuple-element.295.keep_ref, ...), custom_call_target="tpu_custom_call" | custom-call | bytes 786432 | tf_op jit(solution)/shard_map/finish/pallas_call | solution.py:736
  357.2 1.4 collective-permute-done.50
  360.0 2.3 collective-permute-start.53
  364.6 1.3 collective-permute-done.52
  366.4 2.5 collective-permute-start.54
  368.9 2.1 collective-permute-done.54
  371.6 9.5 %adam.1 = (f32[128,512]{1,0:T(8,128)}, bf16[128,512]{1,0:T(8,128)(2,1)}, f32[128,512]{1,0:T(8,128)}, f32[128,512]{1,0:T(8,128)}, f32[256,128]{1,0:T(8,128)}, /*i...) custom-call(f32[1,2304]{1,0:T(1,128)} %add.99.refs_0_, ...), custom_call_target="tpu_custom_call" | custom-call | bytes 2097152 | tf_op jit(solution)/shard_map/adam/pallas_call | solution.py:940
  (243 shorter events, 48.9 us)
Async XLA Ops:
  7.2 275.9 %reduce-scatter.2.cloned.1.call-start = ((), (), s32[]{:S(2)}) async-start(), calls=%async_computation.1 | async-start | bytes 2654208 | tf_op jit(solution)/shard_map/reduce_scatter | solution.py:1081
  7.2 13.4 %collective-permute-start.1 = (bf16[512,1024]{1,0:T(8,128)(2,1)}, bf16[512,1024]{1,0:T(8,128)(2,1)S(1)}, u32[]{:S(2)}, u32[]{:S(2)}) collective-permute-start(bf16[512,1024]{1,0:T(8,128)(2,1)} %x_ref.5), channel_id=1, source_target_pairs={{0,1},{1,0},{2,3},{3,2},{4,5},{5,4},{6,7},{7,6},{8,9},{9,8},{10,11... | collective-permute-start | bytes 3145736 | tf_op jit(solution)/shard_map/ppermute | solution.py:763
  7.8 26.5 %collective-permute-start = (bf16[512,1024]{1,0:T(8,128)(2,1)}, bf16[512,1024]{1,0:T(8,128)(2,1)S(1)}, u32[]{:S(2)}, u32[]{:S(2)}) collective-permute-start(bf16[512,1024]{1,0:T(8,128)(2,1)} %x_ref.5), channel_id=1, source_target_pairs={{0,2},{1,3},{2,0},{3,1},{4,6},{5,7},{6,4},{7,5},{8,10},{9,11},{10,... | collective-permute-start | bytes 3145736 | tf_op jit(solution)/shard_map/ppermute | solution.py:763
  34.3 3.0 collective-permute-start.2
  34.3 25.6 %collective-permute-start.3 = (bf16[512,1024]{1,0:T(8,128)(2,1)S(1)}, bf16[512,1024]{1,0:T(8,128)(2,1)S(1)}, u32[]{:S(2)}, u32[]{:S(2)}) collective-permute-start(bf16[512,1024]{1,0:T(8,128)(2,1)S(1)} %copy-done.26), channel_id=1, source_target_pairs={{0,2},{1,3},{2,0},{3,1},{4,6},{5,7},{6,4},{7,5},{8,10},{9,11},{10,... | collective-permute-start | bytes 3145736 | tf_op jit(solution)/shard_map/ppermute | solution.py:763
  59.9 27.6 %copy-start.28 = (bf16[512,1024]{1,0:T(8,128)(2,1)}, bf16[512,1024]{1,0:T(8,128)(2,1)S(1)}, u32[]{:S(2)}) copy-start(bf16[512,1024]{1,0:T(8,128)(2,1)S(1)} %collective-permute-done.3.refs_2_) | copy-start | bytes 3145732
  59.9 2.9 collective-permute-start.4
  64.3 19.1 %collective-permute-start.5 = (bf16[256,1024]{1,0:T(8,128)(2,1)S(1)}, bf16[256,1024]{1,0:T(8,128)(2,1)}, u32[]{:S(2)}, u32[]{:S(2)}) collective-permute-start(bf16[256,1024]{1,0:T(8,128)(2,1)S(1)} %fusion.11), channel_id=1, source_target_pairs={{0,2},{1,3},{2,0},{3,1},{4,6},{5,7},{6,4},{7,5},{8,10},{9,11},{10,... | collective-permute-start | bytes 1572872 | tf_op jit(solution)/shard_map/ppermute | solution.py:763
  83.4 4.2 %collective-permute-start.6 = (bf16[2,256,1024]{2,1,0:T(8,128)(2,1)}, bf16[2,256,1024]{2,1,0:T(8,128)(2,1)}, u32[]{:S(2)}, u32[]{:S(2)}) collective-permute-start(bf16[2,256,1024]{2,1,0:T(8,128)(2,1)} %get-tuple-element.204), channel_id=1, source_target_pairs={{0,1},{1,0},{2,3},{3,2},{4,5},{5,4},{6,7},{7,6},{8,9},{9,8},{10,11... | collective-permute-start | bytes 3145736 | tf_op jit(solution)/shard_map/ppermute | solution.py:763
  83.5 6.3 %collective-permute-start.8 = (bf16[512,1024]{1,0:T(8,128)(2,1)S(1)}, bf16[512,1024]{1,0:T(8,128)(2,1)}, u32[]{:S(2)}, u32[]{:S(2)}) collective-permute-start(bf16[512,1024]{1,0:T(8,128)(2,1)S(1)} %copy-done.26), channel_id=1, source_target_pairs={{0,1},{1,0},{2,3},{3,2},{4,5},{5,4},{6,7},{7,6},{8,9},{9,8},{10,11... | collective-permute-start | bytes 3145736 | tf_op jit(solution)/shard_map/ppermute | solution.py:763
  87.0 2.8 collective-permute-start.7
  87.2 17.2 %collective-permute-start.9 = (bf16[256,1024]{1,0:T(8,128)(2,1)}, bf16[256,1024]{1,0:T(8,128)(2,1)S(1)}, u32[]{:S(2)}, u32[]{:S(2)}) collective-permute-start(bf16[256,1024]{1,0:T(8,128)(2,1)} %get-tuple-element.205.refs_0_), channel_id=1, source_target_pairs={{0,2},{1,3},{2,0},{3,1},{4,6},{5,7},{6,4},{7,5},{8,10},{9,11},{10,... | collective-permute-start | bytes 1572872 | tf_op jit(solution)/shard_map/ppermute | solution.py:763
  87.4 19.1 %collective-permute-start.11 = (bf16[512,1024]{1,0:T(8,128)(2,1)S(1)}, bf16[512,1024]{1,0:T(8,128)(2,1)S(1)}, u32[]{:S(2)}, u32[]{:S(2)}) collective-permute-start(bf16[512,1024]{1,0:T(8,128)(2,1)S(1)} %collective-permute-done.3.refs_2_), channel_id=1, source_target_pairs={{0,1},{1,0},{2,3},{3,2},{4,5},{5,4},{6,7},{7,6},{8,9},{9,8},{10,11... | collective-permute-start | bytes 3145736 | tf_op jit(solution)/shard_map/ppermute | solution.py:763
  104.4 2.2 collective-permute-start.10
  104.8 17.6 %collective-permute-start.12 = (bf16[256,1024]{1,0:T(8,128)(2,1)S(1)}, bf16[256,1024]{1,0:T(8,128)(2,1)}, u32[]{:S(2)}, u32[]{:S(2)}) collective-permute-start(bf16[256,1024]{1,0:T(8,128)(2,1)S(1)} %copy-done.52), channel_id=1, source_target_pairs={{0,2},{1,3},{2,0},{3,1},{4,6},{5,7},{6,4},{7,5},{8,10},{9,11},{10,... | collective-permute-start | bytes 1572872 | tf_op jit(solution)/shard_map/ppermute | solution.py:763
  125.0 2.1 collective-permute-start.13
  125.0 17.5 %collective-permute-start.14 = (bf16[256,1024]{1,0:T(8,128)(2,1)}, bf16[256,1024]{1,0:T(8,128)(2,1)S(1)}, u32[]{:S(2)}, u32[]{:S(2)}) collective-permute-start(bf16[256,1024]{1,0:T(8,128)(2,1)} %get-tuple-element.216.refs_0_), channel_id=1, source_target_pairs={{0,2},{1,3},{2,0},{3,1},{4,6},{5,7},{6,4},{7,5},{8,10},{9,11},{10,... | collective-permute-start | bytes 1572872 | tf_op jit(solution)/shard_map/ppermute | solution.py:763
  126.6 16.2 %collective-permute-start.15 = (bf16[256,1024]{1,0:T(8,128)(2,1)}, bf16[256,1024]{1,0:T(8,128)(2,1)S(1)}, u32[]{:S(2)}, u32[]{:S(2)}) collective-permute-start(bf16[256,1024]{1,0:T(8,128)(2,1)} %get-tuple-element.226), channel_id=1, source_target_pairs={{0,1},{1,0},{2,3},{3,2},{4,5},{5,4},{6,7},{7,6},{8,9},{9,8},{10,11... | collective-permute-start | bytes 1572872 | tf_op jit(solution)/shard_map/ppermute | solution.py:763
  142.5 2.0 collective-permute-start.16
  143.0 17.1 %collective-permute-start.17 = (bf16[256,1024]{1,0:T(8,128)(2,1)S(1)}, bf16[256,1024]{1,0:T(8,128)(2,1)S(1)}, u32[]{:S(2)}, u32[]{:S(2)}) collective-permute-start(bf16[256,1024]{1,0:T(8,128)(2,1)S(1)} %add_convert_fusion.6), channel_id=1, source_target_pairs={{0,2},{1,3},{2,0},{3,1},{4,6},{5,7},{6,4},{7,5},{8,10},{9,11},{10,... | collective-permute-start | bytes 1572872 | tf_op jit(solution)/shard_map/ppermute | solution.py:763
  144.4 16.2 %collective-permute-start.23 = (bf16[256,1024]{1,0:T(8,128)(2,1)S(1)}, bf16[256,1024]{1,0:T(8,128)(2,1)S(1)}, u32[]{:S(2)}, u32[]{:S(2)}) collective-permute-start(bf16[256,1024]{1,0:T(8,128)(2,1)S(1)} %copy-done.64), channel_id=1, source_target_pairs={{0,1},{1,0},{2,3},{3,2},{4,5},{5,4},{6,7},{7,6},{8,9},{9,8},{10,11... | collective-permute-start | bytes 1572872 | tf_op jit(solution)/shard_map/ppermute | solution.py:763
  160.1 5.3 %collective-permute-start.18 = (bf16[256,1024]{1,0:T(8,128)(2,1)}, bf16[256,1024]{1,0:T(8,128)(2,1)S(1)}, u32[]{:S(2)}, u32[]{:S(2)}) collective-permute-start(bf16[256,1024]{1,0:T(8,128)(2,1)} %get-tuple-element.236), channel_id=1, source_target_pairs={{0,1},{1,0},{2,3},{3,2},{4,5},{5,4},{6,7},{7,6},{8,9},{9,8},{10,11... | collective-permute-start | bytes 1572872 | tf_op jit(solution)/shard_map/ppermute | solution.py:763
  164.3 23.3 %collective-permute-start.24 = (bf16[256,1024]{1,0:T(8,128)(2,1)}, bf16[256,1024]{1,0:T(8,128)(2,1)}, u32[]{:S(2)}, u32[]{:S(2)}) collective-permute-start(bf16[256,1024]{1,0:T(8,128)(2,1)} %get-tuple-element.272.refs_17_.near_skip), channel_id=1, source_target_pairs={{0,2},{1,3},{2,0},{3,1},{4,6},{5,7},{6,4},{7,5},{8,10},{9,11},{10,... | collective-permute-start | bytes 1572872 | tf_op jit(solution)/shard_map/ppermute | solution.py:763
  166.7 23.0 %collective-permute-start.22 = (bf16[256,1024]{1,0:T(8,128)(2,1)S(1)}, bf16[256,1024]{1,0:T(8,128)(2,1)S(1)}, u32[]{:S(2)}, u32[]{:S(2)}) collective-permute-start(bf16[256,1024]{1,0:T(8,128)(2,1)S(1)} %add_convert_fusion.5), channel_id=1, source_target_pairs={{0,2},{1,3},{2,0},{3,1},{4,6},{5,7},{6,4},{7,5},{8,10},{9,11},{10,... | collective-permute-start | bytes 1572872 | tf_op jit(solution)/shard_map/ppermute | solution.py:763
  189.7 2.2 collective-permute-start.21
  189.8 22.3 %collective-permute-start.30 = (bf16[256,1024]{1,0:T(8,128)(2,1)S(1)}, bf16[256,1024]{1,0:T(8,128)(2,1)}, u32[]{:S(2)}, u32[]{:S(2)}) collective-permute-start(bf16[256,1024]{1,0:T(8,128)(2,1)S(1)} %copy-done.36), channel_id=1, source_target_pairs={{0,1},{1,0},{2,3},{3,2},{4,5},{5,4},{6,7},{7,6},{8,9},{9,8},{10,11... | collective-permute-start | bytes 1572872 | tf_op jit(solution)/shard_map/ppermute | solution.py:763
  190.3 15.8 %collective-permute-start.20 = (bf16[256,1024]{1,0:T(8,128)(2,1)}, bf16[256,1024]{1,0:T(8,128)(2,1)S(1)}, u32[]{:S(2)}, u32[]{:S(2)}) collective-permute-start(bf16[256,1024]{1,0:T(8,128)(2,1)} %get-tuple-element.240), channel_id=1, source_target_pairs={{0,1},{1,0},{2,3},{3,2},{4,5},{5,4},{6,7},{7,6},{8,9},{9,8},{10,11... | collective-permute-start | bytes 1572872 | tf_op jit(solution)/shard_map/ppermute | solution.py:763
  190.4 21.7 %collective-permute-start.28 = (bf16[256,1024]{1,0:T(8,128)(2,1)}, bf16[256,1024]{1,0:T(8,128)(2,1)}, u32[]{:S(2)}, u32[]{:S(2)}) collective-permute-start(bf16[256,1024]{1,0:T(8,128)(2,1)} %get-tuple-element.264), channel_id=1, source_target_pairs={{0,1},{1,0},{2,3},{3,2},{4,5},{5,4},{6,7},{7,6},{8,9},{9,8},{10,11... | collective-permute-start | bytes 1572872 | tf_op jit(solution)/shard_map/ppermute | solution.py:763
  190.8 25.1 %collective-permute-start.32 = (bf16[256,1024]{1,0:T(8,128)(2,1)}, bf16[256,1024]{1,0:T(8,128)(2,1)}, u32[]{:S(2)}, u32[]{:S(2)}) collective-permute-start(bf16[256,1024]{1,0:T(8,128)(2,1)} %collective-permute-done.24.refs_21_), channel_id=1, source_target_pairs={{0,1},{1,0},{2,3},{3,2},{4,5},{5,4},{6,7},{7,6},{8,9},{9,8},{10,11... | collective-permute-start | bytes 1572872 | tf_op jit(solution)/shard_map/ppermute | solution.py:763
  195.6 14.2 %collective-permute-start.25 = (bf16[256,1024]{1,0:T(8,128)(2,1)}, bf16[256,1024]{1,0:T(8,128)(2,1)S(1)}, u32[]{:S(2)}, u32[]{:S(2)}) collective-permute-start(bf16[256,1024]{1,0:T(8,128)(2,1)} %get-tuple-element.257.refs_18_.far_skip), channel_id=1, source_target_pairs={{0,2},{1,3},{2,0},{3,1},{4,6},{5,7},{6,4},{7,5},{8,10},{9,11},{10,... | collective-permute-start | bytes 1572872 | tf_op jit(solution)/shard_map/ppermute | solution.py:763
  206.2 10.9 %collective-permute-start.31 = (bf16[256,1024]{1,0:T(8,128)(2,1)S(1)}, bf16[256,1024]{1,0:T(8,128)(2,1)S(1)}, u32[]{:S(2)}, u32[]{:S(2)}) collective-permute-start(bf16[256,1024]{1,0:T(8,128)(2,1)S(1)} %copy-done.37), channel_id=1, source_target_pairs={{0,1},{1,0},{2,3},{3,2},{4,5},{5,4},{6,7},{7,6},{8,9},{9,8},{10,11... | collective-permute-start | bytes 1572872 | tf_op jit(solution)/shard_map/ppermute | solution.py:763
  209.9 8.1 %collective-permute-start.33 = (bf16[256,1024]{1,0:T(8,128)(2,1)S(1)}, bf16[256,1024]{1,0:T(8,128)(2,1)S(1)}, u32[]{:S(2)}, u32[]{:S(2)}) collective-permute-start(bf16[256,1024]{1,0:T(8,128)(2,1)S(1)} %collective-permute-done.25.refs_22_), channel_id=1, source_target_pairs={{0,1},{1,0},{2,3},{3,2},{4,5},{5,4},{6,7},{7,6},{8,9},{9,8},{10,11... | collective-permute-start | bytes 1572872 | tf_op jit(solution)/shard_map/ppermute | solution.py:763
  212.1 38.6 %collective-permute-start.34 = (bf16[4,128,1152]{2,1,0:T(8,128)(2,1)}, bf16[4,128,1152]{2,1,0:T(8,128)(2,1)S(1)}, u32[]{:S(2)}, u32[]{:S(2)}) collective-permute-start(bf16[4,128,1152]{2,1,0:T(8,128)(2,1)} %get-tuple-element.255), channel_id=1, source_target_pairs={{0,4},{4,0},{8,12},{12,8},{16,20},{20,16},{24,28},{28,24},{1,5},{5... | collective-permute-start | bytes 3538952 | tf_op jit(solution)/shard_map/ppermute | solution.py:763
  212.1 38.6 %collective-permute-start.35 = (bf16[4,128,1152]{2,1,0:T(8,128)(2,1)}, bf16[4,128,1152]{2,1,0:T(8,128)(2,1)}, u32[]{:S(2)}, u32[]{:S(2)}) collective-permute-start(bf16[4,128,1152]{2,1,0:T(8,128)(2,1)} %get-tuple-element.271), channel_id=1, source_target_pairs={{0,8},{4,12},{8,0},{12,4},{16,24},{20,28},{24,16},{28,20},{1,9},{5... | collective-permute-start | bytes 3538952 | tf_op jit(solution)/shard_map/ppermute | solution.py:763
  215.9 42.3 %collective-permute-start.26 = (bf16[256,1024]{1,0:T(8,128)(2,1)}, bf16[256,1024]{1,0:T(8,128)(2,1)}, u32[]{:S(2)}, u32[]{:S(2)}) collective-permute-start(bf16[256,1024]{1,0:T(8,128)(2,1)} %add_convert_fusion.4), channel_id=1, source_target_pairs={{0,2},{1,3},{2,0},{3,1},{4,6},{5,7},{6,4},{7,5},{8,10},{9,11},{10,... | collective-permute-start | bytes 1572872 | tf_op jit(solution)/shard_map/ppermute | solution.py:763
  217.1 41.1 %collective-permute-start.29 = (bf16[256,1024]{1,0:T(8,128)(2,1)}, bf16[256,1024]{1,0:T(8,128)(2,1)}, u32[]{:S(2)}, u32[]{:S(2)}) collective-permute-start(bf16[256,1024]{1,0:T(8,128)(2,1)} %add_convert_fusion.2), channel_id=1, source_target_pairs={{0,2},{1,3},{2,0},{3,1},{4,6},{5,7},{6,4},{7,5},{8,10},{9,11},{10,... | collective-permute-start | bytes 1572872 | tf_op jit(solution)/shard_map/ppermute | solution.py:763
  255.8 27.2 %collective-permute-start.36 = (bf16[2,128,1152]{2,1,0:T(8,128)(2,1)}, bf16[2,128,1152]{2,1,0:T(8,128)(2,1)S(1)}, u32[]{:S(2)}, u32[]{:S(2)}) collective-permute-start(bf16[2,128,1152]{2,1,0:T(8,128)(2,1)} %get-tuple-element.282), channel_id=1, source_target_pairs={{0,8},{4,12},{8,0},{12,4},{16,24},{20,28},{24,16},{28,20},{1,9},{5... | collective-permute-start | bytes 1769480 | tf_op jit(solution)/shard_map/ppermute | solution.py:763
  255.8 27.2 %collective-permute-start.37 = (bf16[2,128,1152]{2,1,0:T(8,128)(2,1)}, bf16[2,128,1152]{2,1,0:T(8,128)(2,1)S(1)}, u32[]{:S(2)}, u32[]{:S(2)}) collective-permute-start(bf16[2,128,1152]{2,1,0:T(8,128)(2,1)} %get-tuple-element.284), channel_id=1, source_target_pairs={{0,4},{4,0},{8,12},{12,8},{16,20},{20,16},{24,28},{28,24},{1,5},{5... | collective-permute-start | bytes 1769480 | tf_op jit(solution)/shard_map/ppermute | solution.py:763
  258.1 25.0 %copy-start.8 = (bf16[4,128,512]{2,1,0:T(8,128)(2,1)S(1)}, bf16[4,128,512]{2,1,0:T(8,128)(2,1)}, u32[]{:S(2)}) copy-start(bf16[4,128,512]{2,1,0:T(8,128)(2,1)} %copy-done.7) | copy-start | bytes 1572868
  258.1 24.9 %collective-permute-start.38 = (bf16[4,128,512]{2,1,0:T(8,128)(2,1)S(1)}, bf16[4,128,512]{2,1,0:T(8,128)(2,1)S(1)}, u32[]{:S(2)}, u32[]{:S(2)}) collective-permute-start(bf16[4,128,512]{2,1,0:T(8,128)(2,1)S(1)} %get-tuple-element.286), channel_id=1, source_target_pairs={{0,4},{4,0},{8,12},{12,8},{16,20},{20,16},{24,28},{28,24},{1,5},{5... | collective-permute-start | bytes 1572872 | tf_op jit(solution)/shard_map/ppermute | solution.py:763
  291.9 4.4 %collective-permute-start.39 = (bf16[2,512,1024]{2,1,0:T(8,128)(2,1)}, bf16[2,512,1024]{2,1,0:T(8,128)(2,1)S(1)}, u32[]{:S(2)}, u32[]{:S(2)}) collective-permute-start(bf16[2,512,1024]{2,1,0:T(8,128)(2,1)} %get-tuple-element.296), channel_id=1, source_target_pairs={{0,1},{1,0},{2,3},{3,2},{4,5},{5,4},{6,7},{7,6},{8,9},{9,8},{10,11... | collective-permute-start | bytes 6291464 | tf_op jit(solution)/shard_map/ppermute | solution.py:763
  291.9 13.0 %collective-permute-start.19 = (bf16[256,1024]{1,0:T(8,128)(2,1)}, bf16[256,1024]{1,0:T(8,128)(2,1)S(1)}, u32[]{:S(2)}, u32[]{:S(2)}) collective-permute-start(bf16[256,1024]{1,0:T(8,128)(2,1)} %get-tuple-element.238), channel_id=1, source_target_pairs={{0,1},{1,0},{2,3},{3,2},{4,5},{5,4},{6,7},{7,6},{8,9},{9,8},{10,11... | collective-permute-start | bytes 1572872 | tf_op jit(solution)/shard_map/ppermute | solution.py:763
  292.4 21.8 %collective-permute-start.27 = (bf16[256,1024]{1,0:T(8,128)(2,1)}, bf16[256,1024]{1,0:T(8,128)(2,1)S(1)}, u32[]{:S(2)}, u32[]{:S(2)}) collective-permute-start(bf16[256,1024]{1,0:T(8,128)(2,1)} %get-tuple-element.262), channel_id=1, source_target_pairs={{0,1},{1,0},{2,3},{3,2},{4,5},{5,4},{6,7},{7,6},{8,9},{9,8},{10,11... | collective-permute-start | bytes 1572872 | tf_op jit(solution)/shard_map/ppermute | solution.py:763
  292.5 14.9 %collective-permute-start.41 = (bf16[2,128,512]{2,1,0:T(8,128)(2,1)S(1)}, bf16[2,128,512]{2,1,0:T(8,128)(2,1)S(1)}, u32[]{:S(2)}, u32[]{:S(2)}) collective-permute-start(bf16[2,128,512]{2,1,0:T(8,128)(2,1)S(1)} %copy-done.25), channel_id=1, source_target_pairs={{0,8},{4,12},{8,0},{12,4},{16,24},{20,28},{24,16},{28,20},{1,9},{5... | collective-permute-start | bytes 786440 | tf_op jit(solution)/shard_map/ppermute | solution.py:763
  298.7 50.7 %collective-permute-start.40 = (bf16[512,1024]{1,0:T(8,128)(2,1)S(1)}, bf16[512,1024]{1,0:T(8,128)(2,1)S(1)}, u32[]{:S(2)}, u32[]{:S(2)}) collective-permute-start(bf16[512,1024]{1,0:T(8,128)(2,1)S(1)} %fusion.10), channel_id=1, source_target_pairs={{0,2},{1,3},{2,0},{3,1},{4,6},{5,7},{6,4},{7,5},{8,10},{9,11},{10,... | collective-permute-start | bytes 3145736 | tf_op jit(solution)/shard_map/ppermute | solution.py:763
  303.5 36.9 %copy-start.11 = (bf16[1,128,1152]{2,1,0:T(8,128)(2,1)S(1)}, bf16[1,128,1152]{2,1,0:T(8,128)(2,1)}, u32[]{:S(2)}) copy-start(bf16[1,128,1152]{2,1,0:T(8,128)(2,1)} %copy-done.10) | copy-start | bytes 884740
  304.0 8.1 %collective-permute-start.42 = (bf16[4,128,256]{2,1,0:T(8,128)(2,1)S(1)}, bf16[4,128,256]{2,1,0:T(8,128)(2,1)S(1)}, u32[]{:S(2)}, u32[]{:S(2)}) collective-permute-start(bf16[4,128,256]{2,1,0:T(8,128)(2,1)S(1)} %get-tuple-element.307), channel_id=1, source_target_pairs={{0,4},{4,0},{8,12},{12,8},{16,20},{20,16},{24,28},{28,24},{1,5},{5... | collective-permute-start | bytes 786440 | tf_op jit(solution)/shard_map/ppermute | solution.py:763
  306.3 37.8 %copy-start.9 = (bf16[128,1152]{1,0:T(8,128)(2,1)S(1)}, bf16[128,1152]{1,0:T(8,128)(2,1)}, u32[]{:S(2)}) copy-start(bf16[128,1152]{1,0:T(8,128)(2,1)} %reduce-scatter.2.cloned.1.call-done.refs_8_) | copy-start | bytes 884740
  306.3 37.7 %copy-start.16 = (f32[1,1024]{1,0:T(1,128)S(1)}, f32[1,1024]{1,0:T(1,128)}, u32[]{:S(2)}) copy-start(f32[1,1024]{1,0:T(1,128)} %get-tuple-element.298.refs_0_) | copy-start | bytes 12292
  306.3 37.7 %copy-start.17 = (f32[1,1024]{1,0:T(1,128)S(1)}, f32[1,1024]{1,0:T(1,128)}, u32[]{:S(2)}) copy-start(f32[1,1024]{1,0:T(1,128)} %get-tuple-element.299.refs_1_) | copy-start | bytes 12292
  306.3 37.7 %copy-start.18 = (f32[1,128]{1,0:T(1,128)S(1)}, f32[1,128]{1,0:T(1,128)}, u32[]{:S(2)}) copy-start(f32[1,128]{1,0:T(1,128)} %get-tuple-element.279.refs_2_) | copy-start | bytes 1540
  306.3 37.7 %copy-start.19 = (f32[1,128]{1,0:T(1,128)S(1)}, f32[1,128]{1,0:T(1,128)}, u32[]{:S(2)}) copy-start(f32[1,128]{1,0:T(1,128)} %get-tuple-element.300.refs_3_) | copy-start | bytes 1540
  306.3 25.6 %collective-permute-start.43 = (bf16[1,128,1152]{2,1,0:T(8,128)(2,1)S(1)}, bf16[1,128,1152]{2,1,0:T(8,128)(2,1)S(1)}, u32[]{:S(2)}, u32[]{:S(2)}) collective-permute-start(bf16[1,128,1152]{2,1,0:T(8,128)(2,1)S(1)} %copy-done.23), channel_id=1, source_target_pairs={{0,16},{4,20},{8,24},{12,28},{16,0},{20,4},{24,8},{28,12},{1,17},{... | collective-permute-start | bytes 884744 | tf_op jit(solution)/shard_map/ppermute | solution.py:763
  307.5 30.8 %collective-permute-start.44 = (bf16[1,128,1152]{2,1,0:T(8,128)(2,1)S(1)}, bf16[1,128,1152]{2,1,0:T(8,128)(2,1)S(1)}, u32[]{:S(2)}, u32[]{:S(2)}) collective-permute-start(bf16[1,128,1152]{2,1,0:T(8,128)(2,1)S(1)} %copy-done.21), channel_id=1, source_target_pairs={{0,16},{4,20},{8,24},{12,28},{16,0},{20,4},{24,8},{28,12},{1,17},{... | collective-permute-start | bytes 884744 | tf_op jit(solution)/shard_map/ppermute | solution.py:763
  312.6 27.7 %collective-permute-start.45 = (bf16[1,128,512]{2,1,0:T(8,128)(2,1)S(1)}, bf16[1,128,512]{2,1,0:T(8,128)(2,1)S(1)}, u32[]{:S(2)}, u32[]{:S(2)}) collective-permute-start(bf16[1,128,512]{2,1,0:T(8,128)(2,1)S(1)} %get-tuple-element.312), channel_id=1, source_target_pairs={{0,16},{4,20},{8,24},{12,28},{16,0},{20,4},{24,8},{28,12},{1,17},{... | collective-permute-start | bytes 393224 | tf_op jit(solution)/shard_map/ppermute | solution.py:763
  314.3 26.1 %collective-permute-start.46 = (bf16[2,128,256]{2,1,0:T(8,128)(2,1)S(1)}, bf16[2,128,256]{2,1,0:T(8,128)(2,1)S(1)}, u32[]{:S(2)}, u32[]{:S(2)}) collective-permute-start(bf16[2,128,256]{2,1,0:T(8,128)(2,1)S(1)} %get-tuple-element.314), channel_id=1, source_target_pairs={{0,8},{4,12},{8,0},{12,4},{16,24},{20,28},{24,16},{28,20},{1,9},{5... | collective-permute-start | bytes 393224 | tf_op jit(solution)/shard_map/ppermute | solution.py:763
  343.0 5.2 %collective-permute-start.47 = (bf16[1,128,256]{2,1,0:T(8,128)(2,1)S(1)}, bf16[1,128,256]{2,1,0:T(8,128)(2,1)S(1)}, u32[]{:S(2)}, u32[]{:S(2)}) collective-permute-start(bf16[1,128,256]{2,1,0:T(8,128)(2,1)S(1)} %get-tuple-element.318), channel_id=1, source_target_pairs={{0,16},{4,20},{8,24},{12,28},{16,0},{20,4},{24,8},{28,12},{1,17},{... | collective-permute-start | bytes 196616 | tf_op jit(solution)/shard_map/ppermute | solution.py:763
  355.3 3.3 collective-permute-start.50
  355.3 3.9 %collective-permute-start.49 = (f32[1,2304]{1,0:T(1,128)}, f32[1,2304]{1,0:T(1,128)S(1)}, u32[]{:S(2)}, u32[]{:S(2)}) collective-permute-start(f32[1,2304]{1,0:T(1,128)} %get-tuple-element.322), channel_id=1, source_target_pairs={{0,2},{1,3},{2,0},{3,1},{4,6},{5,7},{6,4},{7,5},{8,10},{9,11},{10,... | collective-permute-start | bytes 27656 | tf_op jit(solution)/shard_map/ppermute | solution.py:763
  356.4 2.8 collective-permute-start.48
  360.0 4.6 %collective-permute-start.53 = (f32[1,2304]{1,0:T(1,128)S(1)}, f32[1,2304]{1,0:T(1,128)S(1)}, u32[]{:S(2)}, u32[]{:S(2)}) collective-permute-start(f32[1,2304]{1,0:T(1,128)S(1)} %add_add_fusion.1), channel_id=1, source_target_pairs={{0,12},{4,8},{8,4},{12,0},{16,28},{20,24},{24,20},{28,16},{1,13},{... | collective-permute-start | bytes 27656 | tf_op jit(solution)/shard_map/ppermute | solution.py:763
  362.3 3.7 collective-permute-start.52
  362.7 3.7 collective-permute-start.51
  366.4 4.6 %collective-permute-start.54 = (f32[1,2304]{1,0:T(1,128)S(1)}, f32[1,2304]{1,0:T(1,128)S(1)}, u32[]{:S(2)}, u32[]{:S(2)}) collective-permute-start(f32[1,2304]{1,0:T(1,128)S(1)} %add_add_fusion), channel_id=1, source_target_pairs={{0,16},{4,20},{8,24},{12,28},{16,0},{20,4},{24,8},{28,12},{1,17},{... | collective-permute-start | bytes 27656 | tf_op jit(solution)/shard_map/ppermute | solution.py:763
  (57 other events, 347.9 us)
Sparse Core Ops, SparseCore 0:
  189.9 78.9 reduce-scatter.1

commit v2 on v0

--- a/solution.py
+++ b/solution.py
@@ -649,33 +649,26 @@
 
 
 def row_kernel(counts, *refs):
-    scatter_ref, row_ref, turned_ref = refs[-3:]
-    parts, heads, squares = refs[: counts[0]], refs[counts[0] : counts[1]], refs[counts[1] : -3]
+    row_ref = refs[-1]
+    parts, heads, squares = refs[: counts[0]], refs[counts[0] : counts[1]], refs[counts[1] : -1]
     width = parts[0].shape[1]
     total = lambda items: sum([item[...] for item in items[1:]], items[0][...])
     row_ref[:, :width] = jnp.zeros((1, width), jnp.float32)
     row_ref[:, width : 2 * width] = total(parts)
     row_ref[:, 2 * width : 2 * width + 2 * HD] = total(heads)
-    scattered = scatter_ref[...].astype(jnp.float32)
-    turned_ref[...] = scattered.T
-    over = jnp.sum(scattered * scattered, axis=0, keepdims=True)
-    square = jnp.sum(over, axis=1, keepdims=True) + total(squares)
     lane = lax.broadcasted_iota(jnp.int32, (1, 2 * HD), 1)
-    row_ref[:, 2 * width + 2 * HD :] = jnp.where(lane == 0, square, 0.0)
-
-
-def row_of(parts, heads, squares, scattered):
+    row_ref[:, 2 * width + 2 * HD :] = jnp.where(lane == 0, total(squares), 0.0)
+
+
+def row_of(parts, heads, squares):
     counts = (len(parts), len(parts) + len(heads))
     return pl.pallas_call(
         lambda *refs: row_kernel(counts, *refs),
-        out_shape=[
-            jax.ShapeDtypeStruct((1, 2 * parts[0].shape[1] + 4 * HD), jnp.float32),
-            jax.ShapeDtypeStruct(scattered.shape[::-1], jnp.float32),
-        ],
+        out_shape=jax.ShapeDtypeStruct((1, 2 * parts[0].shape[1] + 4 * HD), jnp.float32),
         compiler_params=params(24),
         cost_estimate=cost(0, MIB),
         name="row",
-    )(*parts, *heads, *squares, scattered)
+    )(*parts, *heads, *squares)
 
 
 def finish_kernel(
@@ -1041,25 +1034,22 @@
     first_dh = dh_of(0, keep, near, after(far, out_far[0]))
     passed = share_of(after(tuple(backs[1]), far))
     sums.append(across_of(passed))
-    sent = after(grad_full, passed[2], first_dh[0][0])
-    down_grad = contract_rows(sent, hidden).astype(jnp.bfloat16)
-    gate_grad = contract_rows(after(normed_two, down_grad), flat_low[:, :hidden_width])
+    normed_two = after(normed_two, passed[2], first_dh[0][0])
+    gate_grad = contract_rows(normed_two, flat_low[:, :hidden_width])
     gate = ScatterSum([gate_grad.astype(jnp.bfloat16)], [(hidden_width, False)])
     sent, square = advance(here, [gate])
     squares = [square]
+    up_grad = contract_rows(after(normed_two, sent[0]), flat_low[:, hidden_width:])
+    up = ScatterSum([up_grad.astype(jnp.bfloat16)], [(hidden_width, False)], True)
+    sent, _ = advance(here, [up])
     out_sums = [share_of(after(tuple(out), passed[2])) for out in outs]
     keep, near, far = sums[1]
-    far_late = after(far, sent[0], first_dh[0][2])
-    second_dh = dh_of(1, keep, near, far_late)
+    second_dh = dh_of(1, keep, near, after(far, sent[0], first_dh[0][2]))
     pieces_dh, ffn_parts = zip(first_dh, second_dh)
-    down_sum = lax.psum_scatter(
-        after(down_grad, far_late), "dp", scatter_dimension=0, tiled=True
-    )
-    normed_two = after(normed_two, pieces_dh[1][0])
-    up_grad = contract_rows(normed_two, flat_low[:, hidden_width:])
-    up = ScatterSum([up_grad.astype(jnp.bfloat16)], [(hidden_width, False)], True)
-    advance(here, [up], pieces_dh[1][2])
-    sent, _ = advance(here, [gate], up.sources[0])
+    down_grad = contract_rows(after(grad_full, pieces_dh[1][0]), hidden).astype(jnp.bfloat16)
+    down = ScatterSum([down_grad], [(hidden_width, True)])
+    sent, _ = advance(here, [down])
+    sent, _ = advance(here, [gate], sent[0])
 
     dh = [pieces_dh[half][r] for r in range(PIECES) for half in range(HALVES)]
     dh[0] = after(dh[0], *sent, *[item[2] for item in out_sums])
@@ -1084,11 +1074,11 @@
                 ],
                 [(context.shape[1], True), (joints[0].shape[1], False)],
             )
-            sent, _ = advance(here, [gate, up, early], outs_back[1])
+            sent, _ = advance(here, [gate, up, down, early], outs_back[1])
             dh = [after(dh_full, *sent, *out_fars)]
         else:
             dh = [dh_full]
-    sent, square = advance(here, [gate, up, early], joints[-1], down_sum)
+    sent, square = advance(here, [gate, up, down, early], joints[-1])
     squares.append(square)
     joints[0] = after(joints[0], *sent)
     send, keep = spread(place, joints, weight_rows)
@@ -1100,14 +1090,12 @@
     passed = (keep, near, added(keep[1], near[1]))
     keep, near, far = across_of(passed)
     late = ScatterSum(late, [(joints[0].shape[1] * (groups - 1), False)])
-    pending = [gate, up, early, late]
-    gates = [passed[2]]
-    while pending:
-        pending = [item for item in pending if item.total is None]
-        _, square = advance(here, pending, *gates)
+    advance(here, [late], passed[2])
+    pending = [item for item in (gate, up, down, early, late) if item.total is None]
+    while pending != [late]:
+        _, square = advance(here, pending)
         squares.append(square)
-        pending = [item for item in pending if item.total is None]
-        gates = []
+        pending = [item for item in (gate, up, down, early, late) if item.total is None]
 
     results = []
     for half in range(HALVES):
@@ -1117,15 +1105,19 @@
     result = jnp.concatenate(results, axis=0).astype(jnp.bfloat16)
 
     ffn_parts = [after(ffn_parts[0], result), *ffn_parts[1:]]
-    row, down_total = row_of(ffn_parts, head_parts, squares[1:-1], down_sum)
+    row = row_of(ffn_parts, head_parts, squares)
+    gates = [row]
+    while late.total is None:
+        _, square = advance(here, [late], *gates)
+        gates = []
     skips = [pieces[0] for pieces in pieces_dh]
-    input_grad, row = finish(tokens, skips, keep, near, far, attn_gain, row, squares[-1])
+    input_grad, row = finish(tokens, skips, keep, near, far, attn_gain, row, square)
     summed = sum_all(row)
     entries = gains.shape[0]
     out_fan = max(QH * HD * 16 // length, 16)
     out_rate = RATE_WEIGHT * (QH * HD / out_fan) ** 0.5
     updated = adam_all(
-        entries, summed, [*early.total, *late.total, *gate.total, *up.total, down_total],
+        entries, summed, [*early.total, *late.total, *gate.total, *up.total, *down.total],
         [
             (qkv_master, qkv_mean, qkv_square),
             (out_master, out_mean, out_square),

time: 406 us -> 385 us (0.948)
  between operations: 15.6 us -> 2.2 us
  waiting for transfers between devices: 59.4 us -> 46.2 us
  starting transfers between devices: 49.8 us -> 37.6 us
  Pallas kernels: 199 us -> 211 us
  local copies, waits for them, and re-layouts: 26.9 us -> 31.6 us
    ppermute x55 -> x58, waiting for transfers between devices: 59.3 us -> 46.2 us  [exchange(): return lax.ppermute(value, axis, [(i, i ^ bit) for i in range(size)])]
    ppermute x55 -> x58, starting transfers between devices: 49.8 us -> 37.6 us  [exchange(): return lax.ppermute(value, axis, [(i, i ^ bit) for i in range(size)])]
    unnamed x114 -> x142, local copies, waits for them, and re-layouts: 21.4 us -> 26.1 us
    pallas_call x2, Pallas kernels: 51.1 us -> 55.5 us  [attend_back(): pl.pallas_call(lambda *refs: attend_back_kernel(pieces, *refs), grid_spec...]
    pallas_call x9 -> x10, Pallas kernels: 7.68 us -> 11.7 us  [advance(): pl.pallas_call(lambda *refs: advance_kernel(plans, *refs), in_specs=[pl.B...]
  transfers between devices with their start and end apart: 56 -> 58, of which waited for: 21 -> 19; matrix products, arithmetic and copies ran while one was open for 16% -> 17% of each run, Pallas kernels for 43% -> 49%
where the time goes in v2:
time: 385 us; the launch traced here: 383 us
  Pallas kernels  211 us (55%)
  waiting for transfers between devices  46.2 us (12%)
  starting transfers between devices  37.6 us (10%)
  matrix products  33.2 us (9%)
  local copies, waits for them, and re-layouts  31.6 us (8%)
  other arithmetic  21.4 us (6%)
    pallas_call x4, Pallas kernels, feed(): pl.pallas_call(feed_kernel, grid=(1,), in_specs=[pl.BlockSpec((block, wid...  60.9 us
    pallas_call x2, Pallas kernels, attend_back(): pl.pallas_call(lambda *refs: attend_back_kernel(pieces, *refs), grid_spec...  55.5 us
    ppermute x58, waiting for transfers between devices, exchange(): return lax.ppermute(value, axis, [(i, i ^ bit) for i in range(size)])  46.2 us
    ppermute x58, starting transfers between devices, exchange(): return lax.ppermute(value, axis, [(i, i ^ bit) for i in range(size)])  37.6 us
    pallas_call x2, Pallas kernels, attend(): pl.pallas_call(lambda *refs: attend_kernel(half, *refs), grid_spec=pltpu....  34.8 us
    dot_general x6, matrix products, contract_rows(): lax.dot_general(left, right, (((0,), (0,)), ((), ())), preferred_element_...  33.2 us
    unnamed x142, local copies, waits for them, and re-layouts  26.1 us
    pallas_call x2, Pallas kernels, project(): pl.pallas_call(project_kernel, grid_spec=pltpu.PrefetchScalarGridSpec(num...  14.3 us
  transfers between devices with their start and end apart: 58, of which 19 were waited for; matrix products, arithmetic and copies ran while one was open for 17% of the time, Pallas kernels for 49%

profile of v2, /device:TPU:0, one launch (start us, length us, event | category | flops | bytes accessed | tf_op | source)
XLA Modules:
  0.0 382.9 jit_solution(16263579212057926718)
XLA Ops:
  1.2 2.6 collective-permute-start
  3.7 1.3 slice.66
  5.9 1.5 select_bitcast_fusion
  8.5 2.3 copy.69
  10.8 1.3 fusion.17
  12.2 1.8 multiply_sine_fusion
  15.0 7.1 %project.2 = (bf16[2048,1024]{1,0:T(8,128)(2,1)}, f32[8,64,2048]{2,1,0:T(8,128)}, bf16[8,64,2048]{2,1,0:T(8,128)(2,1)}, bf16[8,2048,64]{2,1,0:T(8,128)(2,1)}) custom-call(s32[1]{0:T(128)} %bitcast.2.place_ref.refs_2_.refs_0_, bf16[512,1024]{1,0:T(8,128)(2,1)} %x_ref.5, bf16[512,1024]{1,0:T(8,128)(2,1)} %copy-done.39, f32[1,1024]{1,0:T(1,128)} %bitcast.90, ...), custom_call_target="tpu_custom_call" | custom-call | flops 134217728 | bytes 1048576 | tf_op jit(solution)/shard_map/project/pallas_call | solution.py:139
  22.1 5.4 %copy.74 = bf16[128,8,2,1152]{3,1,2,0:T(8,128)(2,1)} copy(bf16[128,8,2,1152]{3,2,1,0:T(2,128)(2,1)} %bitcast.79) | data formatting | bytes 9437184
  27.7 1.8 collective-permute-start.3
  30.7 7.2 %project.3 = (bf16[2048,1024]{1,0:T(8,128)(2,1)}, f32[8,64,2048]{2,1,0:T(8,128)}, bf16[8,64,2048]{2,1,0:T(8,128)(2,1)}, bf16[8,2048,64]{2,1,0:T(8,128)(2,1)}) custom-call(s32[1]{0:T(128)} %bitcast.2.place_ref.refs_2_.refs_0_, bf16[512,1024]{1,0:T(8,128)(2,1)} %copy-done.38, ...), custom_call_target="tpu_custom_call", output_to_operand_aliasing={{0}: (8, {}), {1}: (9, {}), {2}: (10, {}), {3}: (11, {})} | custom-call | flops 134217728 | bytes 1048576 | tf_op jit(solution)/shard_map/project/pallas_call | solution.py:139
  37.9 15.2 %attend.2 = (bf16[2048,256]{1,0:T(8,128)(2,1)}, bf16[256,2048]{1,0:T(8,128)(2,1)}, f32[2,2,1,2048]{3,2,1,0:T(1,128)}, bf16[2,256,1024]{2,1,0:T(8,128)(2,1)}, bf16[2,256,1024]{2,1,0:T(8,128)(2,1)}) custom-call(s32[8]{0:T(128)} %slice.70.refs_0_, s32[8]{0:T(128)} %slice.71.refs_1_, s32[1]{0:T(128)} %bitcast.2.place_ref.refs_2_.refs_0_, ...), custom_call_target="tpu_custom_call" | custom-call | flops 536870912 | bytes 786432 | tf_op jit(solution)/shard_map/attend/pallas_call | solution.py:261
  53.3 2.9 collective-permute-done.4.near_ref
  56.2 1.6 fusion.11
  57.8 1.8 collective-permute-start.5
  59.6 19.6 %attend.3 = (bf16[2048,256]{1,0:T(8,128)(2,1)}, bf16[256,2048]{1,0:T(8,128)(2,1)}, f32[2,2,1,2048]{3,2,1,0:T(1,128)}, bf16[2,256,1024]{2,1,0:T(8,128)(2,1)}, bf16[2,256,1024]{2,1,0:T(8,128)(2,1)}) custom-call(s32[8]{0:T(128)} %slice.70.refs_0_, s32[8]{0:T(128)} %slice.71.refs_1_, ...), custom_call_target="tpu_custom_call", output_to_operand_aliasing={{0}: (8, {}), {1}: (9, {}), {2}: (10, {})} | custom-call | flops 536870912 | bytes 786432 | tf_op jit(solution)/shard_map/attend/pallas_call | solution.py:261
  79.7 2.8 norm.2
  83.1 2.2 fusion.12
  85.4 12.8 %feed.4 = (bf16[2048,1024]{1,0:T(8,128)(2,1)}, bf16[2048,1024]{1,0:T(8,128)(2,1)}, bf16[2048,1152]{1,0:T(8,128)(2,1)}, bf16[2048,2304]{1,0:T(8,128)(2,1)}, bf16[...) custom-call(bf16[256,1024]{1,0:T(8,128)(2,1)} %get-tuple-element.209.re, ...), custom_call_target="tpu_custom_call" | custom-call | flops 905969664 | bytes 2097152 | tf_op jit(solution)/shard_map/feed/pallas_call | solution.py:542
  98.5 1.7 collective-permute-start.12
  101.4 22.3 %feed.5 = (bf16[2048,1024]{1,0:T(8,128)(2,1)}, bf16[2048,1024]{1,0:T(8,128)(2,1)}, bf16[2048,1152]{1,0:T(8,128)(2,1)}, bf16[2048,2304]{1,0:T(8,128)(2,1)}, bf16[...) custom-call(bf16[256,1024]{1,0:T(8,128)(2,1)} %copy-done.47, ...), custom_call_target="tpu_custom_call", output_to_operand_aliasing={{0}: (6, {}), {1}: (7, {}), {2}: (8, {}), {3}: (9, {})} | custom-call | flops 905969664 | bytes 2097152 | tf_op jit(solution)/shard_map/feed/pallas_call | solution.py:542
  123.7 2.6 norm.3
  126.3 1.6 collective-permute-start.14
  129.2 12.8 %feed.6 = (bf16[2048,1024]{1,0:T(8,128)(2,1)}, bf16[2048,1024]{1,0:T(8,128)(2,1)}, bf16[2048,1152]{1,0:T(8,128)(2,1)}, bf16[2048,2304]{1,0:T(8,128)(2,1)}, bf16[...) custom-call(bf16[256,1024]{1,0:T(8,128)(2,1)} %get-tuple-element.220, ...), custom_call_target="tpu_custom_call", output_to_operand_aliasing={{0}: (6, {}), {1}: (7, {}), {2}: (8, {}), {3}: (9, {})} | custom-call | flops 905969664 | bytes 2097152 | tf_op jit(solution)/shard_map/feed/pallas_call | solution.py:542
  142.4 1.5 collective-permute-start.17
  144.7 13.1 %feed.7 = (bf16[2048,1024]{1,0:T(8,128)(2,1)}, bf16[2048,1024]{1,0:T(8,128)(2,1)}, bf16[2048,1152]{1,0:T(8,128)(2,1)}, bf16[2048,2304]{1,0:T(8,128)(2,1)}, bf16[...) custom-call(bf16[256,1024]{1,0:T(8,128)(2,1)} %copy-done.45, ...), custom_call_target="tpu_custom_call", output_to_operand_aliasing={{0}: (6, {}), {1}: (7, {}), {2}: (8, {}), {3}: (9, {})} | custom-call | flops 905969664 | bytes 2097152 | tf_op jit(solution)/shard_map/feed/pallas_call | solution.py:542
  159.2 2.9 norm_back.2
  163.4 1.4 add_convert_fusion.5
  165.8 9.0 %fusion.4 = bf16[1024,1152]{1,0:T(8,128)(2,1)S(1)} fusion(bf16[2048,1024]{1,0:T(8,128)(2,1)} %get-tuple-element.257, bf16[2048,2304]{1,0:T(8,128)(2,1)} %get-tuple-element.255), kind=kOutput, calls=%fused_computation.4 | convolution fusion | flops 4833017856 | bytes 11272192 | tf_op jit(solution)/shard_map/dot_general | solution.py:69
  176.1 6.0 %fusion.7 = bf16[1024,1152]{1,0:T(8,128)(2,1)S(1)} fusion(bf16[2048,1024]{1,0:T(8,128)(2,1)S(1)} %copy-done.27, bf16[2048,2304]{1,0:T(8,128)(2,1)S(1)} %bitcast.75), kind=kOutput, calls=%fused_computation.5 | convolution fusion | flops 4833017856 | bytes 11272192 | tf_op jit(solution)/shard_map/dot_general | solution.py:69
  182.1 1.2 advance.11
  183.3 4.5 %collective-permute-done.22.far_ref = bf16[256,1024]{1,0:T(8,128)(2,1)S(1)} collective-permute-done((bf16[256,1024]{1,0:T(8,128)(2,1)S(1)}, bf16[256,1024]{1,0:T(8,128)(2,1)S(1)}, u32[]{:S(2)}, u32[]{:S(2)}) %collective-permute-start.22) | collective-permute-done | bytes 524320 | tf_op jit(solution)/shard_map/ppermute | solution.py:730
  188.7 2.9 norm_back.3
  192.7 9.1 %convolution_convert_fusion = bf16[1024,1152]{1,0:T(8,128)(2,1)S(1)} fusion(bf16[2048,1024]{1,0:T(8,128)(2,1)} %get-tuple-element.274, bf16[2048,1152]{1,0:T(8,128)(2,1)} %get-tuple-element.275), kind=kOutput, calls=%fused_computation.6 | convolution fusion | flops 4833017856 | bytes 11272192 | tf_op jit(solution)/shard_map/dot_general | solution.py:69
  203.6 2.5 collective-permute-done.25.refs_22_
  206.2 2.2 add_convert_fusion.4
  208.4 3.1 collective-permute-start.37
  211.5 2.0 add_convert_fusion.2
  217.4 28.8 %attend_back.2 = (bf16[2048,256]{1,0:T(8,128)(2,1)}, f32[1,128]{1,0:T(1,128)}, bf16[2048,1024]{1,0:T(8,128)(2,1)}) custom-call(s32[8]{0:T(128)} %slice.70.refs_0_, s32[8]{0:T(128)} %slice.71.refs_1_, s32[1]{0:T(128)} %bitcast.2.place_ref.refs_2_.refs_0_, bf16[2,4,64,2048]{3,2,1,0:T(8,128)(2,1)} %bitcast.62, bf16[2,4,2048,64]{3,2,1,0:T(8,128)(2,1)} %bitcast.52, ...), custom_call_target="tpu_custom_call" | custom-call | flops 1342177280 | bytes 1572864 | tf_op jit(solution)/shard_map/attend_back/pallas_call | solution.py:424
  246.2 3.9 %convolution_convert_fusion.3 = bf16[1024,256]{1,0:T(8,128)(2,1)S(1)} fusion(bf16[2048,1024]{1,0:T(8,128)(2,1)} %get-tuple-element.297.refs_17_, bf16[2048,256]{1,0:T(8,128)(2,1)} %get-tuple-element.285), kind=kOutput, calls=%fused_computation.10 | convolution fusion | flops 1074003968 | bytes 5767168 | tf_op jit(solution)/shard_map/dot_general | solution.py:69
  250.2 1.3 convolution_convert_fusion.2
  251.6 3.1 advance.14
  256.2 1.3 collective-permute-start.40
  258.2 2.0 collective-permute-start.38
  260.1 26.7 %attend_back.3 = (bf16[2048,256]{1,0:T(8,128)(2,1)}, f32[1,128]{1,0:T(1,128)}) custom-call(s32[8]{0:T(128)} %slice.70.refs_0_, s32[8]{0:T(128)} %slice.71.refs_1_, s32[1]{0:T(128)} %bitcast.2.place_ref.refs_2_.refs_0_, bf16[2,4,64,2048]{3,2,1,0:T(8,128)(2,1)} %bitcast.64, bf16[2,4,2048,64]{3,2,1,0:T(8,128)(2,1)} %bitcast.55, ...), custom_call_target="tpu_custom_call" | custom-call | flops 1342177280 | bytes 1572864 | tf_op jit(solution)/shard_map/attend_back/pallas_call | solution.py:424
  289.5 1.3 advance.15
  294.5 5.5 %spread.1 = (bf16[2,512,1024]{2,1,0:T(8,128)(2,1)}, bf16[2,512,1024]{2,1,0:T(8,128)(2,1)}) custom-call(s32[1]{0:T(128)} %bitcast.2.place_ref.refs_2_.refs_0_, bf16[2048,256]{1,0:T(8,128)(2,1)} %get-tuple-element.303.refs_1_.refs_3_, bf16[2048,256]{1,0:T(8,128)(2,1)} %get-tuple-element.315.refs_2_.refs_4_, ...), custom_call_target="tpu_custom_call" | custom-call | flops 268435456 | bytes 786432 | tf_op jit(solution)/shard_map/spread/pallas_call | solution.py:489
  300.6 4.4 %collective-permute-done.42.near_ref = bf16[2,512,1024]{2,1,0:T(8,128)(2,1)S(1)} collective-permute-done((bf16[2,512,1024]{2,1,0:T(8,128)(2,1)}, bf16[2,512,1024]{2,1,0:T(8,128)(2,1)S(1)}, u32[]{:S(2)}, u32[]{:S(2)}) %collective-permute-start.42) | collective-permute-done | bytes 2097184 | tf_op jit(solution)/shard_map/ppermute | solution.py:730
  305.1 2.4 fusion.10
  308.7 3.8 convolution_convert_fusion.1
  313.4 1.4 add_convert_fusion.3
  314.8 9.2 %collective-permute-done.44.refs_2_ = bf16[1,128,1152]{2,1,0:T(8,128)(2,1)S(1)} collective-permute-done((bf16[1,128,1152]{2,1,0:T(8,128)(2,1)S(1)}, bf16[1,128,1152]{2,1,0:T(8,128)(2,1)S(1)}, u32[]{:S(2)}, u32[]{:S(2)}) %collective-permute-start.44) | collective-permute-done | bytes 294944 | tf_op jit(solution)/shard_map/ppermute | solution.py:730
  324.0 5.9 %collective-permute-done.45.refs_4_ = bf16[1,128,1152]{2,1,0:T(8,128)(2,1)S(1)} collective-permute-done((bf16[1,128,1152]{2,1,0:T(8,128)(2,1)S(1)}, bf16[1,128,1152]{2,1,0:T(8,128)(2,1)S(1)}, u32[]{:S(2)}, u32[]{:S(2)}) %collective-permute-start.45) | collective-permute-done | bytes 294944 | tf_op jit(solution)/shard_map/ppermute | solution.py:730
  332.5 1.9 collective-permute-start.49
  334.4 1.4 add_convert_fusion.1
  335.8 4.3 %collective-permute-done.48.refs_2_ = bf16[1,128,512]{2,1,0:T(8,128)(2,1)S(1)} collective-permute-done((bf16[1,128,512]{2,1,0:T(8,128)(2,1)S(1)}, bf16[1,128,512]{2,1,0:T(8,128)(2,1)S(1)}, u32[]{:S(2)}, u32[]{:S(2)}) %collective-permute-start.48) | collective-permute-done | bytes 131104 | tf_op jit(solution)/shard_map/ppermute | solution.py:730
  343.6 2.7 row.1.begin_ref
  346.2 1.9 collective-permute-done.50.refs_2_
  350.4 4.9 %finish.1 = (bf16[512,1024]{1,0:T(8,128)(2,1)}, f32[1,2304]{1,0:T(1,128)}) custom-call(bf16[512,1024]{1,0:T(8,128)(2,1)} %x_ref.5, bf16[256,1024]{1,0:T(8,128)(2,1)} %get-tuple-element.279.refs_17_.near_skip, bf16[256,1024]{1,0:T(8,128)(2,1)} %get-tuple-element.260.refs_18_.far_skip, bf16[2,512,1024]{2,1,0:T(8,128)(2,1)} %get-tuple-element.304.keep_ref, ...), custom_call_target="tpu_custom_call" | custom-call | bytes 786432 | tf_op jit(solution)/shard_map/finish/pallas_call | solution.py:703
  357.2 1.4 collective-permute-done.53
  360.1 1.7 collective-permute-start.56
  361.8 1.3 collective-permute-start.55
  365.5 1.3 collective-permute-done.54
  367.5 3.8 %collective-permute-done.57 = f32[1,2304]{1,0:T(1,128)S(1)} collective-permute-done((f32[1,2304]{1,0:T(1,128)S(1)}, f32[1,2304]{1,0:T(1,128)S(1)}, u32[]{:S(2)}, u32[]{:S(2)}) %collective-permute-start.57) | collective-permute-done | bytes 9248 | tf_op jit(solution)/shard_map/ppermute | solution.py:730
  372.0 9.3 %adam.1 = (f32[128,512]{1,0:T(8,128)}, bf16[128,512]{1,0:T(8,128)(2,1)}, f32[128,512]{1,0:T(8,128)}, f32[128,512]{1,0:T(8,128)}, f32[256,128]{1,0:T(8,128)}, /*i...) custom-call(f32[1,2304]{1,0:T(1,128)} %add.97.refs_0_, ...), custom_call_target="tpu_custom_call" | custom-call | bytes 2097152 | tf_op jit(solution)/shard_map/adam/pallas_call | solution.py:907
  (259 shorter events, 50.7 us)
Async XLA Ops:
  0.7 13.4 %collective-permute-start.1 = (bf16[512,1024]{1,0:T(8,128)(2,1)}, bf16[512,1024]{1,0:T(8,128)(2,1)S(1)}, u32[]{:S(2)}, u32[]{:S(2)}) collective-permute-start(bf16[512,1024]{1,0:T(8,128)(2,1)} %x_ref.5), channel_id=1, source_target_pairs={{0,1},{1,0},{2,3},{3,2},{4,5},{5,4},{6,7},{7,6},{8,9},{9,8},{10,11... | collective-permute-start | bytes 3145736 | tf_op jit(solution)/shard_map/ppermute | solution.py:730
  1.2 26.5 %collective-permute-start = (bf16[512,1024]{1,0:T(8,128)(2,1)}, bf16[512,1024]{1,0:T(8,128)(2,1)S(1)}, u32[]{:S(2)}, u32[]{:S(2)}) collective-permute-start(bf16[512,1024]{1,0:T(8,128)(2,1)} %x_ref.5), channel_id=1, source_target_pairs={{0,2},{1,3},{2,0},{3,1},{4,6},{5,7},{6,4},{7,5},{8,10},{9,11},{10,... | collective-permute-start | bytes 3145736 | tf_op jit(solution)/shard_map/ppermute | solution.py:730
  27.7 3.0 collective-permute-start.2
  27.7 25.6 %collective-permute-start.3 = (bf16[512,1024]{1,0:T(8,128)(2,1)S(1)}, bf16[512,1024]{1,0:T(8,128)(2,1)S(1)}, u32[]{:S(2)}, u32[]{:S(2)}) collective-permute-start(bf16[512,1024]{1,0:T(8,128)(2,1)S(1)} %copy-done.28), channel_id=1, source_target_pairs={{0,2},{1,3},{2,0},{3,1},{4,6},{5,7},{6,4},{7,5},{8,10},{9,11},{10,... | collective-permute-start | bytes 3145736 | tf_op jit(solution)/shard_map/ppermute | solution.py:730
  53.3 29.7 %copy-start.30 = (bf16[512,1024]{1,0:T(8,128)(2,1)}, bf16[512,1024]{1,0:T(8,128)(2,1)S(1)}, u32[]{:S(2)}) copy-start(bf16[512,1024]{1,0:T(8,128)(2,1)S(1)} %collective-permute-done.3.refs_2_) | copy-start | bytes 3145732
  53.3 2.9 collective-permute-start.4
  57.8 21.4 %collective-permute-start.5 = (bf16[256,1024]{1,0:T(8,128)(2,1)S(1)}, bf16[256,1024]{1,0:T(8,128)(2,1)}, u32[]{:S(2)}, u32[]{:S(2)}) collective-permute-start(bf16[256,1024]{1,0:T(8,128)(2,1)S(1)} %fusion.11), channel_id=1, source_target_pairs={{0,2},{1,3},{2,0},{3,1},{4,6},{5,7},{6,4},{7,5},{8,10},{9,11},{10,... | collective-permute-start | bytes 1572872 | tf_op jit(solution)/shard_map/ppermute | solution.py:730
  79.2 4.0 %collective-permute-start.6 = (bf16[2,256,1024]{2,1,0:T(8,128)(2,1)}, bf16[2,256,1024]{2,1,0:T(8,128)(2,1)}, u32[]{:S(2)}, u32[]{:S(2)}) collective-permute-start(bf16[2,256,1024]{2,1,0:T(8,128)(2,1)} %get-tuple-element.208), channel_id=1, source_target_pairs={{0,1},{1,0},{2,3},{3,2},{4,5},{5,4},{6,7},{7,6},{8,9},{9,8},{10,11... | collective-permute-start | bytes 3145736 | tf_op jit(solution)/shard_map/ppermute | solution.py:730
  79.3 6.1 %collective-permute-start.8 = (bf16[512,1024]{1,0:T(8,128)(2,1)S(1)}, bf16[512,1024]{1,0:T(8,128)(2,1)}, u32[]{:S(2)}, u32[]{:S(2)}) collective-permute-start(bf16[512,1024]{1,0:T(8,128)(2,1)S(1)} %copy-done.28), channel_id=1, source_target_pairs={{0,1},{1,0},{2,3},{3,2},{4,5},{5,4},{6,7},{7,6},{8,9},{9,8},{10,11... | collective-permute-start | bytes 3145736 | tf_op jit(solution)/shard_map/ppermute | solution.py:730
  82.5 2.8 collective-permute-start.7
  82.7 15.4 %collective-permute-start.9 = (bf16[256,1024]{1,0:T(8,128)(2,1)}, bf16[256,1024]{1,0:T(8,128)(2,1)S(1)}, u32[]{:S(2)}, u32[]{:S(2)}) collective-permute-start(bf16[256,1024]{1,0:T(8,128)(2,1)} %get-tuple-element.209.refs_0_), channel_id=1, source_target_pairs={{0,2},{1,3},{2,0},{3,1},{4,6},{5,7},{6,4},{7,5},{8,10},{9,11},{10,... | collective-permute-start | bytes 1572872 | tf_op jit(solution)/shard_map/ppermute | solution.py:730
  83.0 17.3 %collective-permute-start.11 = (bf16[512,1024]{1,0:T(8,128)(2,1)S(1)}, bf16[512,1024]{1,0:T(8,128)(2,1)S(1)}, u32[]{:S(2)}, u32[]{:S(2)}) collective-permute-start(bf16[512,1024]{1,0:T(8,128)(2,1)S(1)} %collective-permute-done.3.refs_2_), channel_id=1, source_target_pairs={{0,1},{1,0},{2,3},{3,2},{4,5},{5,4},{6,7},{7,6},{8,9},{9,8},{10,11... | collective-permute-start | bytes 3145736 | tf_op jit(solution)/shard_map/ppermute | solution.py:730
  98.1 2.2 collective-permute-start.10
  98.5 25.2 %collective-permute-start.12 = (bf16[256,1024]{1,0:T(8,128)(2,1)S(1)}, bf16[256,1024]{1,0:T(8,128)(2,1)}, u32[]{:S(2)}, u32[]{:S(2)}) collective-permute-start(bf16[256,1024]{1,0:T(8,128)(2,1)S(1)} %copy-done.54), channel_id=1, source_target_pairs={{0,2},{1,3},{2,0},{3,1},{4,6},{5,7},{6,4},{7,5},{8,10},{9,11},{10,... | collective-permute-start | bytes 1572872 | tf_op jit(solution)/shard_map/ppermute | solution.py:730
  126.3 2.1 collective-permute-start.13
  126.3 15.7 %collective-permute-start.14 = (bf16[256,1024]{1,0:T(8,128)(2,1)}, bf16[256,1024]{1,0:T(8,128)(2,1)S(1)}, u32[]{:S(2)}, u32[]{:S(2)}) collective-permute-start(bf16[256,1024]{1,0:T(8,128)(2,1)} %get-tuple-element.220.refs_0_), channel_id=1, source_target_pairs={{0,2},{1,3},{2,0},{3,1},{4,6},{5,7},{6,4},{7,5},{8,10},{9,11},{10,... | collective-permute-start | bytes 1572872 | tf_op jit(solution)/shard_map/ppermute | solution.py:730
  127.8 14.3 %collective-permute-start.15 = (bf16[256,1024]{1,0:T(8,128)(2,1)}, bf16[256,1024]{1,0:T(8,128)(2,1)S(1)}, u32[]{:S(2)}, u32[]{:S(2)}) collective-permute-start(bf16[256,1024]{1,0:T(8,128)(2,1)} %get-tuple-element.230), channel_id=1, source_target_pairs={{0,1},{1,0},{2,3},{3,2},{4,5},{5,4},{6,7},{7,6},{8,9},{9,8},{10,11... | collective-permute-start | bytes 1572872 | tf_op jit(solution)/shard_map/ppermute | solution.py:730
  142.0 2.0 collective-permute-start.16
  142.4 15.5 %collective-permute-start.17 = (bf16[256,1024]{1,0:T(8,128)(2,1)S(1)}, bf16[256,1024]{1,0:T(8,128)(2,1)S(1)}, u32[]{:S(2)}, u32[]{:S(2)}) collective-permute-start(bf16[256,1024]{1,0:T(8,128)(2,1)S(1)} %add_convert_fusion.6), channel_id=1, source_target_pairs={{0,2},{1,3},{2,0},{3,1},{4,6},{5,7},{6,4},{7,5},{8,10},{9,11},{10,... | collective-permute-start | bytes 1572872 | tf_op jit(solution)/shard_map/ppermute | solution.py:730
  143.9 14.5 %collective-permute-start.23 = (bf16[256,1024]{1,0:T(8,128)(2,1)S(1)}, bf16[256,1024]{1,0:T(8,128)(2,1)S(1)}, u32[]{:S(2)}, u32[]{:S(2)}) collective-permute-start(bf16[256,1024]{1,0:T(8,128)(2,1)S(1)} %copy-done.66), channel_id=1, source_target_pairs={{0,1},{1,0},{2,3},{3,2},{4,5},{5,4},{6,7},{7,6},{8,9},{9,8},{10,11... | collective-permute-start | bytes 1572872 | tf_op jit(solution)/shard_map/ppermute | solution.py:730
  157.9 5.6 %collective-permute-start.18 = (bf16[256,1024]{1,0:T(8,128)(2,1)}, bf16[256,1024]{1,0:T(8,128)(2,1)S(1)}, u32[]{:S(2)}, u32[]{:S(2)}) collective-permute-start(bf16[256,1024]{1,0:T(8,128)(2,1)} %get-tuple-element.240), channel_id=1, source_target_pairs={{0,1},{1,0},{2,3},{3,2},{4,5},{5,4},{6,7},{7,6},{8,9},{9,8},{10,11... | collective-permute-start | bytes 1572872 | tf_op jit(solution)/shard_map/ppermute | solution.py:730
  162.1 41.0 %collective-permute-start.31 = (bf16[256,1024]{1,0:T(8,128)(2,1)}, bf16[256,1024]{1,0:T(8,128)(2,1)S(1)}, u32[]{:S(2)}, u32[]{:S(2)}) collective-permute-start(bf16[256,1024]{1,0:T(8,128)(2,1)} %get-tuple-element.279.refs_17_.near_skip), channel_id=1, source_target_pairs={{0,1},{1,0},{2,3},{3,2},{4,5},{5,4},{6,7},{7,6},{8,9},{9,8},{10,11... | collective-permute-start | bytes 1572872 | tf_op jit(solution)/shard_map/ppermute | solution.py:730
  162.2 21.1 %collective-permute-start.24 = (bf16[256,1024]{1,0:T(8,128)(2,1)}, bf16[256,1024]{1,0:T(8,128)(2,1)}, u32[]{:S(2)}, u32[]{:S(2)}) collective-permute-start(bf16[256,1024]{1,0:T(8,128)(2,1)} %get-tuple-element.279.refs_17_.near_skip), channel_id=1, source_target_pairs={{0,2},{1,3},{2,0},{3,1},{4,6},{5,7},{6,4},{7,5},{8,10},{9,11},{10,... | collective-permute-start | bytes 1572872 | tf_op jit(solution)/shard_map/ppermute | solution.py:730
  163.4 25.3 %collective-permute-start.21 = (bf16[256,1024]{1,0:T(8,128)(2,1)}, bf16[256,1024]{1,0:T(8,128)(2,1)}, u32[]{:S(2)}, u32[]{:S(2)}) collective-permute-start(bf16[256,1024]{1,0:T(8,128)(2,1)} %get-tuple-element.247), channel_id=1, source_target_pairs={{0,1},{1,0},{2,3},{3,2},{4,5},{5,4},{6,7},{7,6},{8,9},{9,8},{10,11... | collective-permute-start | bytes 1572872 | tf_op jit(solution)/shard_map/ppermute | solution.py:730
  164.8 23.1 %collective-permute-start.22 = (bf16[256,1024]{1,0:T(8,128)(2,1)S(1)}, bf16[256,1024]{1,0:T(8,128)(2,1)S(1)}, u32[]{:S(2)}, u32[]{:S(2)}) collective-permute-start(bf16[256,1024]{1,0:T(8,128)(2,1)S(1)} %add_convert_fusion.5), channel_id=1, source_target_pairs={{0,2},{1,3},{2,0},{3,1},{4,6},{5,7},{6,4},{7,5},{8,10},{9,11},{10,... | collective-permute-start | bytes 1572872 | tf_op jit(solution)/shard_map/ppermute | solution.py:730
  176.0 32.3 %collective-permute-start.30 = (bf16[4,128,1152]{2,1,0:T(8,128)(2,1)}, bf16[4,128,1152]{2,1,0:T(8,128)(2,1)S(1)}, u32[]{:S(2)}, u32[]{:S(2)}) collective-permute-start(bf16[4,128,1152]{2,1,0:T(8,128)(2,1)} %get-tuple-element.256), channel_id=1, source_target_pairs={{0,4},{4,0},{8,12},{12,8},{16,20},{20,16},{24,28},{28,24},{1,5},{5... | collective-permute-start | bytes 3538952 | tf_op jit(solution)/shard_map/ppermute | solution.py:730
  183.3 20.1 %collective-permute-start.20 = (bf16[256,1024]{1,0:T(8,128)(2,1)}, bf16[256,1024]{1,0:T(8,128)(2,1)}, u32[]{:S(2)}, u32[]{:S(2)}) collective-permute-start(bf16[256,1024]{1,0:T(8,128)(2,1)} %get-tuple-element.244), channel_id=1, source_target_pairs={{0,1},{1,0},{2,3},{3,2},{4,5},{5,4},{6,7},{7,6},{8,9},{9,8},{10,11... | collective-permute-start | bytes 1572872 | tf_op jit(solution)/shard_map/ppermute | solution.py:730
  188.7 19.7 %collective-permute-start.28 = (bf16[256,1024]{1,0:T(8,128)(2,1)}, bf16[256,1024]{1,0:T(8,128)(2,1)}, u32[]{:S(2)}, u32[]{:S(2)}) collective-permute-start(bf16[256,1024]{1,0:T(8,128)(2,1)} %get-tuple-element.267), channel_id=1, source_target_pairs={{0,1},{1,0},{2,3},{3,2},{4,5},{5,4},{6,7},{7,6},{8,9},{9,8},{10,11... | collective-permute-start | bytes 1572872 | tf_op jit(solution)/shard_map/ppermute | solution.py:730
  191.6 14.5 %collective-permute-start.25 = (bf16[256,1024]{1,0:T(8,128)(2,1)}, bf16[256,1024]{1,0:T(8,128)(2,1)S(1)}, u32[]{:S(2)}, u32[]{:S(2)}) collective-permute-start(bf16[256,1024]{1,0:T(8,128)(2,1)} %get-tuple-element.260.refs_18_.far_skip), channel_id=1, source_target_pairs={{0,2},{1,3},{2,0},{3,1},{4,6},{5,7},{6,4},{7,5},{8,10},{9,11},{10,... | collective-permute-start | bytes 1572872 | tf_op jit(solution)/shard_map/ppermute | solution.py:730
  203.0 11.5 %collective-permute-start.33 = (bf16[256,1024]{1,0:T(8,128)(2,1)}, bf16[256,1024]{1,0:T(8,128)(2,1)S(1)}, u32[]{:S(2)}, u32[]{:S(2)}) collective-permute-start(bf16[256,1024]{1,0:T(8,128)(2,1)} %collective-permute-done.24.refs_21_), channel_id=1, source_target_pairs={{0,1},{1,0},{2,3},{3,2},{4,5},{5,4},{6,7},{7,6},{8,9},{9,8},{10,11... | collective-permute-start | bytes 1572872 | tf_op jit(solution)/shard_map/ppermute | solution.py:730
  203.3 12.3 %collective-permute-start.32 = (bf16[256,1024]{1,0:T(8,128)(2,1)S(1)}, bf16[256,1024]{1,0:T(8,128)(2,1)S(1)}, u32[]{:S(2)}, u32[]{:S(2)}) collective-permute-start(bf16[256,1024]{1,0:T(8,128)(2,1)S(1)} %copy-done.37), channel_id=1, source_target_pairs={{0,1},{1,0},{2,3},{3,2},{4,5},{5,4},{6,7},{7,6},{8,9},{9,8},{10,11... | collective-permute-start | bytes 1572872 | tf_op jit(solution)/shard_map/ppermute | solution.py:730
  206.1 10.4 %collective-permute-start.34 = (bf16[256,1024]{1,0:T(8,128)(2,1)S(1)}, bf16[256,1024]{1,0:T(8,128)(2,1)S(1)}, u32[]{:S(2)}, u32[]{:S(2)}) collective-permute-start(bf16[256,1024]{1,0:T(8,128)(2,1)S(1)} %collective-permute-done.25.refs_22_), channel_id=1, source_target_pairs={{0,1},{1,0},{2,3},{3,2},{4,5},{5,4},{6,7},{7,6},{8,9},{9,8},{10,11... | collective-permute-start | bytes 1572872 | tf_op jit(solution)/shard_map/ppermute | solution.py:730
  208.4 43.2 %collective-permute-start.36 = (bf16[4,128,1152]{2,1,0:T(8,128)(2,1)}, bf16[4,128,1152]{2,1,0:T(8,128)(2,1)}, u32[]{:S(2)}, u32[]{:S(2)}) collective-permute-start(bf16[4,128,1152]{2,1,0:T(8,128)(2,1)} %get-tuple-element.258), channel_id=1, source_target_pairs={{0,8},{4,12},{8,0},{12,4},{16,24},{20,28},{24,16},{28,20},{1,9},{5... | collective-permute-start | bytes 3538952 | tf_op jit(solution)/shard_map/ppermute | solution.py:730
  208.4 43.2 %collective-permute-start.37 = (bf16[4,128,1152]{2,1,0:T(8,128)(2,1)}, bf16[4,128,1152]{2,1,0:T(8,128)(2,1)}, u32[]{:S(2)}, u32[]{:S(2)}) collective-permute-start(bf16[4,128,1152]{2,1,0:T(8,128)(2,1)} %get-tuple-element.276), channel_id=1, source_target_pairs={{0,4},{4,0},{8,12},{12,8},{16,20},{20,16},{24,28},{28,24},{1,5},{5... | collective-permute-start | bytes 3538952 | tf_op jit(solution)/shard_map/ppermute | solution.py:730
  214.5 43.6 %collective-permute-start.26 = (bf16[256,1024]{1,0:T(8,128)(2,1)}, bf16[256,1024]{1,0:T(8,128)(2,1)}, u32[]{:S(2)}, u32[]{:S(2)}) collective-permute-start(bf16[256,1024]{1,0:T(8,128)(2,1)} %add_convert_fusion.4), channel_id=1, source_target_pairs={{0,2},{1,3},{2,0},{3,1},{4,6},{5,7},{6,4},{7,5},{8,10},{9,11},{10,... | collective-permute-start | bytes 1572872 | tf_op jit(solution)/shard_map/ppermute | solution.py:730
  215.7 44.5 %collective-permute-start.29 = (bf16[256,1024]{1,0:T(8,128)(2,1)}, bf16[256,1024]{1,0:T(8,128)(2,1)}, u32[]{:S(2)}, u32[]{:S(2)}) collective-permute-start(bf16[256,1024]{1,0:T(8,128)(2,1)} %add_convert_fusion.2), channel_id=1, source_target_pairs={{0,2},{1,3},{2,0},{3,1},{4,6},{5,7},{6,4},{7,5},{8,10},{9,11},{10,... | collective-permute-start | bytes 1572872 | tf_op jit(solution)/shard_map/ppermute | solution.py:730
  216.6 35.0 %collective-permute-start.35 = (bf16[2,128,1152]{2,1,0:T(8,128)(2,1)}, bf16[2,128,1152]{2,1,0:T(8,128)(2,1)S(1)}, u32[]{:S(2)}, u32[]{:S(2)}) collective-permute-start(bf16[2,128,1152]{2,1,0:T(8,128)(2,1)} %get-tuple-element.278), channel_id=1, source_target_pairs={{0,8},{4,12},{8,0},{12,4},{16,24},{20,28},{24,16},{28,20},{1,9},{5... | collective-permute-start | bytes 1769480 | tf_op jit(solution)/shard_map/ppermute | solution.py:730
  256.2 31.4 %collective-permute-start.39 = (bf16[2,128,1152]{2,1,0:T(8,128)(2,1)}, bf16[2,128,1152]{2,1,0:T(8,128)(2,1)S(1)}, u32[]{:S(2)}, u32[]{:S(2)}) collective-permute-start(bf16[2,128,1152]{2,1,0:T(8,128)(2,1)} %get-tuple-element.292), channel_id=1, source_target_pairs={{0,4},{4,0},{8,12},{12,8},{16,20},{20,16},{24,28},{28,24},{1,5},{5... | collective-permute-start | bytes 1769480 | tf_op jit(solution)/shard_map/ppermute | solution.py:730
  256.2 31.4 %collective-permute-start.40 = (bf16[2,128,1152]{2,1,0:T(8,128)(2,1)}, bf16[2,128,1152]{2,1,0:T(8,128)(2,1)S(1)}, u32[]{:S(2)}, u32[]{:S(2)}) collective-permute-start(bf16[2,128,1152]{2,1,0:T(8,128)(2,1)} %get-tuple-element.294), channel_id=1, source_target_pairs={{0,8},{4,12},{8,0},{12,4},{16,24},{20,28},{24,16},{28,20},{1,9},{5... | collective-permute-start | bytes 1769480 | tf_op jit(solution)/shard_map/ppermute | solution.py:730
  257.5 29.4 %collective-permute-start.41 = (bf16[4,128,512]{2,1,0:T(8,128)(2,1)}, bf16[4,128,512]{2,1,0:T(8,128)(2,1)S(1)}, u32[]{:S(2)}, u32[]{:S(2)}) collective-permute-start(bf16[4,128,512]{2,1,0:T(8,128)(2,1)} %get-tuple-element.296), channel_id=1, source_target_pairs={{0,4},{4,0},{8,12},{12,8},{16,20},{20,16},{24,28},{28,24},{1,5},{5... | collective-permute-start | bytes 1572872 | tf_op jit(solution)/shard_map/ppermute | solution.py:730
  258.2 29.4 %copy-start.6 = (bf16[4,128,512]{2,1,0:T(8,128)(2,1)S(1)}, bf16[4,128,512]{2,1,0:T(8,128)(2,1)}, u32[]{:S(2)}) copy-start(bf16[4,128,512]{2,1,0:T(8,128)(2,1)} %copy-done.5) | copy-start | bytes 1572868
  258.2 28.7 %collective-permute-start.38 = (bf16[1,128,1152]{2,1,0:T(8,128)(2,1)}, bf16[1,128,1152]{2,1,0:T(8,128)(2,1)S(1)}, u32[]{:S(2)}, u32[]{:S(2)}) collective-permute-start(bf16[1,128,1152]{2,1,0:T(8,128)(2,1)} %get-tuple-element.290), channel_id=1, source_target_pairs={{0,16},{4,20},{8,24},{12,28},{16,0},{20,4},{24,8},{28,12},{1,17},{... | collective-permute-start | bytes 884744 | tf_op jit(solution)/shard_map/ppermute | solution.py:730
  300.0 5.1 %collective-permute-start.42 = (bf16[2,512,1024]{2,1,0:T(8,128)(2,1)}, bf16[2,512,1024]{2,1,0:T(8,128)(2,1)S(1)}, u32[]{:S(2)}, u32[]{:S(2)}) collective-permute-start(bf16[2,512,1024]{2,1,0:T(8,128)(2,1)} %get-tuple-element.305), channel_id=1, source_target_pairs={{0,1},{1,0},{2,3},{3,2},{4,5},{5,4},{6,7},{7,6},{8,9},{9,8},{10,11... | collective-permute-start | bytes 6291464 | tf_op jit(solution)/shard_map/ppermute | solution.py:730
  300.0 13.1 %collective-permute-start.19 = (bf16[256,1024]{1,0:T(8,128)(2,1)S(1)}, bf16[256,1024]{1,0:T(8,128)(2,1)S(1)}, u32[]{:S(2)}, u32[]{:S(2)}) collective-permute-start(bf16[256,1024]{1,0:T(8,128)(2,1)S(1)} %copy-done.65), channel_id=1, source_target_pairs={{0,1},{1,0},{2,3},{3,2},{4,5},{5,4},{6,7},{7,6},{8,9},{9,8},{10,11... | collective-permute-start | bytes 1572872 | tf_op jit(solution)/shard_map/ppermute | solution.py:730
  300.5 34.0 %collective-permute-start.27 = (bf16[256,1024]{1,0:T(8,128)(2,1)}, bf16[256,1024]{1,0:T(8,128)(2,1)S(1)}, u32[]{:S(2)}, u32[]{:S(2)}) collective-permute-start(bf16[256,1024]{1,0:T(8,128)(2,1)} %get-tuple-element.265), channel_id=1, source_target_pairs={{0,1},{1,0},{2,3},{3,2},{4,5},{5,4},{6,7},{7,6},{8,9},{9,8},{10,11... | collective-permute-start | bytes 1572872 | tf_op jit(solution)/shard_map/ppermute | solution.py:730
  300.6 12.5 %collective-permute-start.46 = (bf16[2,128,512]{2,1,0:T(8,128)(2,1)S(1)}, bf16[2,128,512]{2,1,0:T(8,128)(2,1)S(1)}, u32[]{:S(2)}, u32[]{:S(2)}) collective-permute-start(bf16[2,128,512]{2,1,0:T(8,128)(2,1)S(1)} %copy-done.26), channel_id=1, source_target_pairs={{0,8},{4,12},{8,0},{12,4},{16,24},{20,28},{24,16},{28,20},{1,9},{5... | collective-permute-start | bytes 786440 | tf_op jit(solution)/shard_map/ppermute | solution.py:730
  300.6 23.5 %collective-permute-start.44 = (bf16[1,128,1152]{2,1,0:T(8,128)(2,1)S(1)}, bf16[1,128,1152]{2,1,0:T(8,128)(2,1)S(1)}, u32[]{:S(2)}, u32[]{:S(2)}) collective-permute-start(bf16[1,128,1152]{2,1,0:T(8,128)(2,1)S(1)} %copy-done.24), channel_id=1, source_target_pairs={{0,16},{4,20},{8,24},{12,28},{16,0},{20,4},{24,8},{28,12},{1,17},{... | collective-permute-start | bytes 884744 | tf_op jit(solution)/shard_map/ppermute | solution.py:730
  307.5 41.9 %collective-permute-start.43 = (bf16[512,1024]{1,0:T(8,128)(2,1)S(1)}, bf16[512,1024]{1,0:T(8,128)(2,1)S(1)}, u32[]{:S(2)}, u32[]{:S(2)}) collective-permute-start(bf16[512,1024]{1,0:T(8,128)(2,1)S(1)} %fusion.10), channel_id=1, source_target_pairs={{0,2},{1,3},{2,0},{3,1},{4,6},{5,7},{6,4},{7,5},{8,10},{9,11},{10,... | collective-permute-start | bytes 3145736 | tf_op jit(solution)/shard_map/ppermute | solution.py:730
  313.0 16.9 %collective-permute-start.45 = (bf16[1,128,1152]{2,1,0:T(8,128)(2,1)S(1)}, bf16[1,128,1152]{2,1,0:T(8,128)(2,1)S(1)}, u32[]{:S(2)}, u32[]{:S(2)}) collective-permute-start(bf16[1,128,1152]{2,1,0:T(8,128)(2,1)S(1)} %copy-done.22), channel_id=1, source_target_pairs={{0,16},{4,20},{8,24},{12,28},{16,0},{20,4},{24,8},{28,12},{1,17},{... | collective-permute-start | bytes 884744 | tf_op jit(solution)/shard_map/ppermute | solution.py:730
  313.1 16.8 %collective-permute-start.47 = (bf16[4,128,256]{2,1,0:T(8,128)(2,1)S(1)}, bf16[4,128,256]{2,1,0:T(8,128)(2,1)S(1)}, u32[]{:S(2)}, u32[]{:S(2)}) collective-permute-start(bf16[4,128,256]{2,1,0:T(8,128)(2,1)S(1)} %get-tuple-element.318), channel_id=1, source_target_pairs={{0,4},{4,0},{8,12},{12,8},{16,20},{20,16},{24,28},{28,24},{1,5},{5... | collective-permute-start | bytes 786440 | tf_op jit(solution)/shard_map/ppermute | solution.py:730
  314.8 28.8 %copy-start.17 = (f32[1,1024]{1,0:T(1,128)S(1)}, f32[1,1024]{1,0:T(1,128)}, u32[]{:S(2)}) copy-start(f32[1,1024]{1,0:T(1,128)} %get-tuple-element.307.refs_0_) | copy-start | bytes 12292
  314.8 28.8 %copy-start.18 = (f32[1,1024]{1,0:T(1,128)S(1)}, f32[1,1024]{1,0:T(1,128)}, u32[]{:S(2)}) copy-start(f32[1,1024]{1,0:T(1,128)} %get-tuple-element.308.refs_1_) | copy-start | bytes 12292
  314.8 28.8 %copy-start.19 = (f32[1,128]{1,0:T(1,128)S(1)}, f32[1,128]{1,0:T(1,128)}, u32[]{:S(2)}) copy-start(f32[1,128]{1,0:T(1,128)} %get-tuple-element.287.refs_2_) | copy-start | bytes 1540
  314.8 28.7 %copy-start.20 = (f32[1,128]{1,0:T(1,128)S(1)}, f32[1,128]{1,0:T(1,128)}, u32[]{:S(2)}) copy-start(f32[1,128]{1,0:T(1,128)} %get-tuple-element.309.refs_3_) | copy-start | bytes 1540
  332.5 7.6 %collective-permute-start.48 = (bf16[1,128,512]{2,1,0:T(8,128)(2,1)S(1)}, bf16[1,128,512]{2,1,0:T(8,128)(2,1)S(1)}, u32[]{:S(2)}, u32[]{:S(2)}) collective-permute-start(bf16[1,128,512]{2,1,0:T(8,128)(2,1)S(1)} %get-tuple-element.321), channel_id=1, source_target_pairs={{0,16},{4,20},{8,24},{12,28},{16,0},{20,4},{24,8},{28,12},{1,17},{... | collective-permute-start | bytes 393224 | tf_op jit(solution)/shard_map/ppermute | solution.py:730
  332.5 7.9 %collective-permute-start.49 = (bf16[2,128,256]{2,1,0:T(8,128)(2,1)S(1)}, bf16[2,128,256]{2,1,0:T(8,128)(2,1)S(1)}, u32[]{:S(2)}, u32[]{:S(2)}) collective-permute-start(bf16[2,128,256]{2,1,0:T(8,128)(2,1)S(1)} %get-tuple-element.323), channel_id=1, source_target_pairs={{0,8},{4,12},{8,0},{12,4},{16,24},{20,28},{24,16},{28,20},{1,9},{5... | collective-permute-start | bytes 393224 | tf_op jit(solution)/shard_map/ppermute | solution.py:730
  342.3 5.8 %collective-permute-start.50 = (bf16[1,128,256]{2,1,0:T(8,128)(2,1)S(1)}, bf16[1,128,256]{2,1,0:T(8,128)(2,1)S(1)}, u32[]{:S(2)}, u32[]{:S(2)}) collective-permute-start(bf16[1,128,256]{2,1,0:T(8,128)(2,1)S(1)} %get-tuple-element.326), channel_id=1, source_target_pairs={{0,16},{4,20},{8,24},{12,28},{16,0},{20,4},{24,8},{28,12},{1,17},{... | collective-permute-start | bytes 196616 | tf_op jit(solution)/shard_map/ppermute | solution.py:730
  355.3 3.3 collective-permute-start.53
  355.5 3.9 %collective-permute-start.52 = (f32[1,2304]{1,0:T(1,128)}, f32[1,2304]{1,0:T(1,128)S(1)}, u32[]{:S(2)}, u32[]{:S(2)}) collective-permute-start(f32[1,2304]{1,0:T(1,128)} %get-tuple-element.330), channel_id=1, source_target_pairs={{0,2},{1,3},{2,0},{3,1},{4,6},{5,7},{6,4},{7,5},{8,10},{9,11},{10,... | collective-permute-start | bytes 27656 | tf_op jit(solution)/shard_map/ppermute | solution.py:730
  356.5 2.9 collective-permute-start.51
  360.1 4.6 %collective-permute-start.56 = (f32[1,2304]{1,0:T(1,128)S(1)}, f32[1,2304]{1,0:T(1,128)S(1)}, u32[]{:S(2)}, u32[]{:S(2)}) collective-permute-start(f32[1,2304]{1,0:T(1,128)S(1)} %add_add_fusion.1), channel_id=1, source_target_pairs={{0,12},{4,8},{8,4},{12,0},{16,28},{20,24},{24,20},{28,16},{1,13},{... | collective-permute-start | bytes 27656 | tf_op jit(solution)/shard_map/ppermute | solution.py:730
  361.8 3.7 collective-permute-start.55
  363.1 3.7 collective-permute-start.54
  366.8 4.6 %collective-permute-start.57 = (f32[1,2304]{1,0:T(1,128)S(1)}, f32[1,2304]{1,0:T(1,128)S(1)}, u32[]{:S(2)}, u32[]{:S(2)}) collective-permute-start(f32[1,2304]{1,0:T(1,128)S(1)} %add_add_fusion), channel_id=1, source_target_pairs={{0,16},{4,20},{8,24},{12,28},{16,0},{20,4},{24,8},{28,12},{1,17},{... | collective-permute-start | bytes 27656 | tf_op jit(solution)/shard_map/ppermute | solution.py:730
  (64 other events, 382.1 us)

commit v3 on v2

--- a/solution.py
+++ b/solution.py
@@ -24,7 +24,7 @@
 
 KINDS = QH // KVH + 2
 RATIO = QH // KVH
-PARTS = 2
+PARTS = 1
 PIECES = 4
 HALVES = 2
 CORE = 1
@@ -739,13 +739,14 @@
 
 
 class ScatterSum:
-    def __init__(self, grads, flipped, second_first=False):
+    def __init__(self, grads, flipped, swapped=()):
         size = lax.axis_size("dp")
         rows = grads[0].shape[0] // size
         self.left = [1 << k for k in reversed(range(size.bit_length() - 1))]
         self.order = self.left[::-1]
-        if second_first:
-            self.order[:2] = self.order[1::-1]
+        if swapped and len(self.order) > max(swapped):
+            one, two = swapped
+            self.order[one], self.order[two] = self.order[two], self.order[one]
         self.flipped = flipped
         self.sources = [grad.reshape(size, rows, grad.shape[1]) for grad in grads]
         self.columns = sum(grad.shape[1] for grad in grads)
@@ -1036,18 +1037,18 @@
     sums.append(across_of(passed))
     normed_two = after(normed_two, passed[2], first_dh[0][0])
     gate_grad = contract_rows(normed_two, flat_low[:, :hidden_width])
-    gate = ScatterSum([gate_grad.astype(jnp.bfloat16)], [(hidden_width, False)])
+    gate = ScatterSum([gate_grad.astype(jnp.bfloat16)], [(hidden_width, False)], (1, 2))
     sent, square = advance(here, [gate])
     squares = [square]
     up_grad = contract_rows(after(normed_two, sent[0]), flat_low[:, hidden_width:])
-    up = ScatterSum([up_grad.astype(jnp.bfloat16)], [(hidden_width, False)], True)
+    up = ScatterSum([up_grad.astype(jnp.bfloat16)], [(hidden_width, False)], (0, 1))
     sent, _ = advance(here, [up])
     out_sums = [share_of(after(tuple(out), passed[2])) for out in outs]
     keep, near, far = sums[1]
     second_dh = dh_of(1, keep, near, after(far, sent[0], first_dh[0][2]))
     pieces_dh, ffn_parts = zip(first_dh, second_dh)
     down_grad = contract_rows(after(grad_full, pieces_dh[1][0]), hidden).astype(jnp.bfloat16)
-    down = ScatterSum([down_grad], [(hidden_width, True)])
+    down = ScatterSum([down_grad], [(hidden_width, True)], (1, 2))
     sent, _ = advance(here, [down])
     sent, _ = advance(here, [gate], sent[0])
 

time: 385 us -> 374 us (0.971)
  Pallas kernels: 211 us -> 185 us
  starting transfers between devices: 37.6 us -> 46.3 us
    pallas_call x2, Pallas kernels: 55.5 us -> 41.4 us  [attend_back(): pl.pallas_call(lambda *refs: attend_back_kernel(pieces, *refs), grid_spec...]
    pallas_call x2, Pallas kernels: 34.8 us -> 24.1 us  [attend(): pl.pallas_call(lambda *refs: attend_kernel(half, *refs), grid_spec=pltpu....]
    ppermute x58, starting transfers between devices: 37.6 us -> 46.3 us  [exchange(): return lax.ppermute(value, axis, [(i, i ^ bit) for i in range(size)])]
  transfers between devices with their start and end apart: 58 -> 58, of which waited for: 19 -> 23; matrix products, arithmetic and copies ran while one was open for 17% -> 17% of each run, Pallas kernels for 49% -> 44%
where the time goes in v3:
time: 374 us; the launch traced here: 368 us
  Pallas kernels  185 us (49%)
  waiting for transfers between devices  49.5 us (13%)
  starting transfers between devices  46.3 us (12%)
  matrix products  33.1 us (9%)
  local copies, waits for them, and re-layouts  30.7 us (8%)
  other arithmetic  21.4 us (6%)
    pallas_call x4, Pallas kernels, feed(): pl.pallas_call(feed_kernel, grid=(1,), in_specs=[pl.BlockSpec((block, wid...  60.9 us
    ppermute x58, waiting for transfers between devices, exchange(): return lax.ppermute(value, axis, [(i, i ^ bit) for i in range(size)])  49.5 us
    ppermute x58, starting transfers between devices, exchange(): return lax.ppermute(value, axis, [(i, i ^ bit) for i in range(size)])  46.3 us
    pallas_call x2, Pallas kernels, attend_back(): pl.pallas_call(lambda *refs: attend_back_kernel(pieces, *refs), grid_spec...  41.4 us
    dot_general x6, matrix products, contract_rows(): lax.dot_general(left, right, (((0,), (0,)), ((), ())), preferred_element_...  33.1 us
    unnamed x142, local copies, waits for them, and re-layouts  25.2 us
    pallas_call x2, Pallas kernels, attend(): pl.pallas_call(lambda *refs: attend_kernel(half, *refs), grid_spec=pltpu....  24.1 us
    pallas_call x2, Pallas kernels, project(): pl.pallas_call(project_kernel, grid_spec=pltpu.PrefetchScalarGridSpec(num...  13.5 us
  transfers between devices with their start and end apart: 58, of which 23 were waited for; matrix products, arithmetic and copies ran while one was open for 17% of the time, Pallas kernels for 44%

profile of v3, /device:TPU:0, one launch (start us, length us, event | category | flops | bytes accessed | tf_op | source)
XLA Modules:
  0.0 368.3 jit_solution(2516985557661093927)
XLA Ops:
  1.2 2.6 collective-permute-start
  5.9 1.5 select_bitcast_fusion
  8.5 2.3 copy.69
  12.2 1.8 multiply_sine_fusion
  15.0 6.7 %project.2 = (bf16[2048,1024]{1,0:T(8,128)(2,1)}, f32[8,64,2048]{2,1,0:T(8,128)}, bf16[8,64,2048]{2,1,0:T(8,128)(2,1)}, bf16[8,2048,64]{2,1,0:T(8,128)(2,1)}) custom-call(s32[1]{0:T(128)} %bitcast.2.place_ref.refs_2_.refs_0_, bf16[512,1024]{1,0:T(8,128)(2,1)} %x_ref.5, bf16[512,1024]{1,0:T(8,128)(2,1)} %copy-done.39, f32[1,1024]{1,0:T(1,128)} %bitcast.90, ...), custom_call_target="tpu_custom_call" | custom-call | flops 134217728 | bytes 1048576 | tf_op jit(solution)/shard_map/project/pallas_call | solution.py:139
  21.7 5.4 %copy.74 = bf16[128,8,2,1152]{3,1,2,0:T(8,128)(2,1)} copy(bf16[128,8,2,1152]{3,2,1,0:T(2,128)(2,1)} %bitcast.79) | data formatting | bytes 9437184
  27.7 1.8 collective-permute-start.3
  30.7 6.8 %project.3 = (bf16[2048,1024]{1,0:T(8,128)(2,1)}, f32[8,64,2048]{2,1,0:T(8,128)}, bf16[8,64,2048]{2,1,0:T(8,128)(2,1)}, bf16[8,2048,64]{2,1,0:T(8,128)(2,1)}) custom-call(s32[1]{0:T(128)} %bitcast.2.place_ref.refs_2_.refs_0_, bf16[512,1024]{1,0:T(8,128)(2,1)} %copy-done.38, ...), custom_call_target="tpu_custom_call", output_to_operand_aliasing={{0}: (8, {}), {1}: (9, {}), {2}: (10, {}), {3}: (11, {})} | custom-call | flops 134217728 | bytes 1048576 | tf_op jit(solution)/shard_map/project/pallas_call | solution.py:139
  37.5 11.7 %attend.2 = (bf16[2048,256]{1,0:T(8,128)(2,1)}, bf16[256,2048]{1,0:T(8,128)(2,1)}, f32[2,2,1,2048]{3,2,1,0:T(1,128)}, bf16[2,256,1024]{2,1,0:T(8,128)(2,1)}, bf16[2,256,1024]{2,1,0:T(8,128)(2,1)}) custom-call(s32[8]{0:T(128)} %slice.70.refs_0_, s32[8]{0:T(128)} %slice.71.refs_1_, s32[1]{0:T(128)} %bitcast.2.place_ref.refs_2_.refs_0_, ...), custom_call_target="tpu_custom_call" | custom-call | flops 536870912 | bytes 786432 | tf_op jit(solution)/shard_map/attend/pallas_call | solution.py:261
  49.2 4.1 %collective-permute-done.3.refs_2_ = bf16[512,1024]{1,0:T(8,128)(2,1)S(1)} collective-permute-done((bf16[512,1024]{1,0:T(8,128)(2,1)S(1)}, bf16[512,1024]{1,0:T(8,128)(2,1)S(1)}, u32[]{:S(2)}, u32[]{:S(2)}) %collective-permute-start.3) | collective-permute-done | bytes 1048608 | tf_op jit(solution)/shard_map/ppermute | solution.py:730
  53.3 2.9 collective-permute-done.4.near_ref
  56.2 1.6 fusion.11
  57.8 1.8 collective-permute-start.5
  59.6 12.4 %attend.3 = (bf16[2048,256]{1,0:T(8,128)(2,1)}, bf16[256,2048]{1,0:T(8,128)(2,1)}, f32[2,2,1,2048]{3,2,1,0:T(1,128)}, bf16[2,256,1024]{2,1,0:T(8,128)(2,1)}, bf16[2,256,1024]{2,1,0:T(8,128)(2,1)}) custom-call(s32[8]{0:T(128)} %slice.70.refs_0_, s32[8]{0:T(128)} %slice.71.refs_1_, ...), custom_call_target="tpu_custom_call", output_to_operand_aliasing={{0}: (8, {}), {1}: (9, {}), {2}: (10, {})} | custom-call | flops 536870912 | bytes 786432 | tf_op jit(solution)/shard_map/attend/pallas_call | solution.py:261
  72.6 2.8 norm.2
  75.5 1.6 collective-permute-start.9
  77.3 2.2 fusion.12
  79.5 12.8 %feed.4 = (bf16[2048,1024]{1,0:T(8,128)(2,1)}, bf16[2048,1024]{1,0:T(8,128)(2,1)}, bf16[2048,1152]{1,0:T(8,128)(2,1)}, bf16[2048,2304]{1,0:T(8,128)(2,1)}, bf16[...) custom-call(bf16[256,1024]{1,0:T(8,128)(2,1)} %get-tuple-element.209.re, ...), custom_call_target="tpu_custom_call" | custom-call | flops 905969664 | bytes 2097152 | tf_op jit(solution)/shard_map/feed/pallas_call | solution.py:542
  95.0 22.3 %feed.5 = (bf16[2048,1024]{1,0:T(8,128)(2,1)}, bf16[2048,1024]{1,0:T(8,128)(2,1)}, bf16[2048,1152]{1,0:T(8,128)(2,1)}, bf16[2048,2304]{1,0:T(8,128)(2,1)}, bf16[...) custom-call(bf16[256,1024]{1,0:T(8,128)(2,1)} %copy-done.47, ...), custom_call_target="tpu_custom_call", output_to_operand_aliasing={{0}: (6, {}), {1}: (7, {}), {2}: (8, {}), {3}: (9, {})} | custom-call | flops 905969664 | bytes 2097152 | tf_op jit(solution)/shard_map/feed/pallas_call | solution.py:542
  117.3 2.6 norm.3
  122.8 12.8 %feed.6 = (bf16[2048,1024]{1,0:T(8,128)(2,1)}, bf16[2048,1024]{1,0:T(8,128)(2,1)}, bf16[2048,1152]{1,0:T(8,128)(2,1)}, bf16[2048,2304]{1,0:T(8,128)(2,1)}, bf16[...) custom-call(bf16[256,1024]{1,0:T(8,128)(2,1)} %get-tuple-element.220, ...), custom_call_target="tpu_custom_call", output_to_operand_aliasing={{0}: (6, {}), {1}: (7, {}), {2}: (8, {}), {3}: (9, {})} | custom-call | flops 905969664 | bytes 2097152 | tf_op jit(solution)/shard_map/feed/pallas_call | solution.py:542
  138.3 13.1 %feed.7 = (bf16[2048,1024]{1,0:T(8,128)(2,1)}, bf16[2048,1024]{1,0:T(8,128)(2,1)}, bf16[2048,1152]{1,0:T(8,128)(2,1)}, bf16[2048,2304]{1,0:T(8,128)(2,1)}, bf16[...) custom-call(bf16[256,1024]{1,0:T(8,128)(2,1)} %copy-done.45, ...), custom_call_target="tpu_custom_call", output_to_operand_aliasing={{0}: (6, {}), {1}: (7, {}), {2}: (8, {}), {3}: (9, {})} | custom-call | flops 905969664 | bytes 2097152 | tf_op jit(solution)/shard_map/feed/pallas_call | solution.py:542
  152.7 2.9 norm_back.2
  156.7 1.4 add_convert_fusion.5
  159.3 9.0 %fusion.4 = bf16[1024,1152]{1,0:T(8,128)(2,1)S(1)} fusion(bf16[2048,1024]{1,0:T(8,128)(2,1)} %get-tuple-element.257, bf16[2048,2304]{1,0:T(8,128)(2,1)} %get-tuple-element.255), kind=kOutput, calls=%fused_computation.4 | convolution fusion | flops 4833017856 | bytes 11272192 | tf_op jit(solution)/shard_map/dot_general | solution.py:69
  169.5 4.0 %collective-permute-start.30 = (bf16[4,128,1152]{2,1,0:T(8,128)(2,1)}, bf16[4,128,1152]{2,1,0:T(8,128)(2,1)S(1)}, u32[]{:S(2)}, u32[]{:S(2)}) collective-permute-start(bf16[4,128,1152]{2,1,0:T(8,128)(2,1)} %get-tuple-element.256), channel_id=1, source_target_pairs={{0,4},{4,0},{8,12},{12,8},{16,20},{20,16},{24,28},{28,24},{1,5},{5... | collective-permute-start | bytes 3538952 | tf_op jit(solution)/shard_map/ppermute | solution.py:730
  173.5 6.0 %fusion.7 = bf16[1024,1152]{1,0:T(8,128)(2,1)S(1)} fusion(bf16[2048,1024]{1,0:T(8,128)(2,1)S(1)} %copy-done.27, bf16[2048,2304]{1,0:T(8,128)(2,1)S(1)} %bitcast.75), kind=kOutput, calls=%fused_computation.5 | convolution fusion | flops 4833017856 | bytes 11272192 | tf_op jit(solution)/shard_map/dot_general | solution.py:69
  182.2 2.9 norm_back.3
  186.0 9.1 %convolution_convert_fusion = bf16[1024,1152]{1,0:T(8,128)(2,1)S(1)} fusion(bf16[2048,1024]{1,0:T(8,128)(2,1)} %get-tuple-element.274, bf16[2048,1152]{1,0:T(8,128)(2,1)} %get-tuple-element.275), kind=kOutput, calls=%fused_computation.6 | convolution fusion | flops 4833017856 | bytes 11272192 | tf_op jit(solution)/shard_map/dot_general | solution.py:69
  196.9 2.7 collective-permute-done.25.refs_22_
  199.6 2.2 add_convert_fusion.4
  201.9 3.5 collective-permute-start.36
  205.9 2.0 add_convert_fusion.2
  211.0 1.7 collective-permute-start.35
  212.7 21.7 %attend_back.2 = (bf16[2048,256]{1,0:T(8,128)(2,1)}, f32[1,128]{1,0:T(1,128)}, bf16[2048,1024]{1,0:T(8,128)(2,1)}) custom-call(s32[8]{0:T(128)} %slice.70.refs_0_, s32[8]{0:T(128)} %slice.71.refs_1_, s32[1]{0:T(128)} %bitcast.2.place_ref.refs_2_.refs_0_, bf16[2,4,64,2048]{3,2,1,0:T(8,128)(2,1)} %bitcast.62, bf16[2,4,2048,64]{3,2,1,0:T(8,128)(2,1)} %bitcast.52, ...), custom_call_target="tpu_custom_call" | custom-call | flops 1342177280 | bytes 1572864 | tf_op jit(solution)/shard_map/attend_back/pallas_call | solution.py:424
  234.4 3.9 %convolution_convert_fusion.3 = bf16[1024,256]{1,0:T(8,128)(2,1)S(1)} fusion(bf16[2048,1024]{1,0:T(8,128)(2,1)} %get-tuple-element.297.refs_17_, bf16[2048,256]{1,0:T(8,128)(2,1)} %get-tuple-element.285), kind=kOutput, calls=%fused_computation.10 | convolution fusion | flops 1074003968 | bytes 5767168 | tf_op jit(solution)/shard_map/dot_general | solution.py:69
  238.5 1.3 convolution_convert_fusion.2
  239.8 4.9 %collective-permute-done.36.refs_4_ = bf16[4,128,1152]{2,1,0:T(8,128)(2,1)} collective-permute-done((bf16[4,128,1152]{2,1,0:T(8,128)(2,1)}, bf16[4,128,1152]{2,1,0:T(8,128)(2,1)}, u32[]{:S(2)}, u32[]{:S(2)}) %collective-permute-start.36) | collective-permute-done | bytes 1179680 | tf_op jit(solution)/shard_map/ppermute | solution.py:730
  244.7 3.1 advance.14
  249.3 2.2 collective-permute-start.39
  253.9 19.7 %attend_back.3 = (bf16[2048,256]{1,0:T(8,128)(2,1)}, f32[1,128]{1,0:T(1,128)}) custom-call(s32[8]{0:T(128)} %slice.70.refs_0_, s32[8]{0:T(128)} %slice.71.refs_1_, s32[1]{0:T(128)} %bitcast.2.place_ref.refs_2_.refs_0_, bf16[2,4,64,2048]{3,2,1,0:T(8,128)(2,1)} %bitcast.64, bf16[2,4,2048,64]{3,2,1,0:T(8,128)(2,1)} %bitcast.55, ...), custom_call_target="tpu_custom_call" | custom-call | flops 1342177280 | bytes 1572864 | tf_op jit(solution)/shard_map/attend_back/pallas_call | solution.py:424
  273.6 2.4 collective-permute-done.41.refs_8_
  276.7 2.5 collective-permute-done.40.refs_6_
  286.1 5.5 %spread.1 = (bf16[2,512,1024]{2,1,0:T(8,128)(2,1)}, bf16[2,512,1024]{2,1,0:T(8,128)(2,1)}) custom-call(s32[1]{0:T(128)} %bitcast.2.place_ref.refs_2_.refs_0_, bf16[2048,256]{1,0:T(8,128)(2,1)} %get-tuple-element.303.refs_1_.refs_3_, bf16[2048,256]{1,0:T(8,128)(2,1)} %get-tuple-element.315.refs_2_.refs_4_, ...), custom_call_target="tpu_custom_call" | custom-call | flops 268435456 | bytes 786432 | tf_op jit(solution)/shard_map/spread/pallas_call | solution.py:489
  292.2 2.3 collective-permute-start.44
  294.4 2.3 collective-permute-done.42.near_ref
  296.7 2.4 fusion.10
  300.1 3.8 %convolution_convert_fusion.1 = bf16[1024,256]{1,0:T(8,128)(2,1)S(1)} fusion(bf16[2048,1024]{1,0:T(8,128)(2,1)} %get-tuple-element.286, bf16[2048,256]{1,0:T(8,128)(2,1)} %get-tuple-element.315.refs_2_.refs_4_), kind=kOutput, calls=%fused_computation.8 | convolution fusion | flops 1074003968 | bytes 5767168 | tf_op jit(solution)/shard_map/dot_general | solution.py:69
  306.0 1.4 add_convert_fusion.3
  307.4 1.6 collective-permute-done.44.refs_2_
  309.0 5.9 %collective-permute-done.45.refs_4_ = bf16[1,128,1152]{2,1,0:T(8,128)(2,1)S(1)} collective-permute-done((bf16[1,128,1152]{2,1,0:T(8,128)(2,1)S(1)}, bf16[1,128,1152]{2,1,0:T(8,128)(2,1)S(1)}, u32[]{:S(2)}, u32[]{:S(2)}) %collective-permute-start.45) | collective-permute-done | bytes 294944 | tf_op jit(solution)/shard_map/ppermute | solution.py:730
  317.5 1.8 collective-permute-start.49
  319.4 1.4 add_convert_fusion.1
  320.7 4.7 %collective-permute-done.48.refs_2_ = bf16[1,128,512]{2,1,0:T(8,128)(2,1)S(1)} collective-permute-done((bf16[1,128,512]{2,1,0:T(8,128)(2,1)S(1)}, bf16[1,128,512]{2,1,0:T(8,128)(2,1)S(1)}, u32[]{:S(2)}, u32[]{:S(2)}) %collective-permute-start.48) | collective-permute-done | bytes 131104 | tf_op jit(solution)/shard_map/ppermute | solution.py:730
  328.9 2.7 row.1.begin_ref
  331.5 1.5 collective-permute-done.50.refs_2_
  335.3 4.9 %finish.1 = (bf16[512,1024]{1,0:T(8,128)(2,1)}, f32[1,2304]{1,0:T(1,128)}) custom-call(bf16[512,1024]{1,0:T(8,128)(2,1)} %x_ref.5, bf16[256,1024]{1,0:T(8,128)(2,1)} %get-tuple-element.279.refs_17_.near_skip, bf16[256,1024]{1,0:T(8,128)(2,1)} %get-tuple-element.260.refs_18_.far_skip, bf16[2,512,1024]{2,1,0:T(8,128)(2,1)} %get-tuple-element.304.keep_ref, ...), custom_call_target="tpu_custom_call" | custom-call | bytes 786432 | tf_op jit(solution)/shard_map/finish/pallas_call | solution.py:703
  340.2 1.4 collective-permute-start.52
  342.1 1.4 collective-permute-done.53
  344.9 1.4 collective-permute-start.56
  346.3 2.1 collective-permute-start.55
  350.1 1.9 collective-permute-done.54
  353.2 3.5 collective-permute-done.57
  357.3 9.3 %adam.1 = (f32[128,512]{1,0:T(8,128)}, bf16[128,512]{1,0:T(8,128)(2,1)}, f32[128,512]{1,0:T(8,128)}, f32[128,512]{1,0:T(8,128)}, f32[256,128]{1,0:T(8,128)}, /*i...) custom-call(f32[1,2304]{1,0:T(1,128)} %add.97.refs_0_, ...), custom_call_target="tpu_custom_call" | custom-call | bytes 2097152 | tf_op jit(solution)/shard_map/adam/pallas_call | solution.py:908
  (259 shorter events, 60.7 us)
Async XLA Ops:
  0.7 13.4 %collective-permute-start.1 = (bf16[512,1024]{1,0:T(8,128)(2,1)}, bf16[512,1024]{1,0:T(8,128)(2,1)S(1)}, u32[]{:S(2)}, u32[]{:S(2)}) collective-permute-start(bf16[512,1024]{1,0:T(8,128)(2,1)} %x_ref.5), channel_id=1, source_target_pairs={{0,1},{1,0},{2,3},{3,2},{4,5},{5,4},{6,7},{7,6},{8,9},{9,8},{10,11... | collective-permute-start | bytes 3145736 | tf_op jit(solution)/shard_map/ppermute | solution.py:730
  1.2 26.5 %collective-permute-start = (bf16[512,1024]{1,0:T(8,128)(2,1)}, bf16[512,1024]{1,0:T(8,128)(2,1)S(1)}, u32[]{:S(2)}, u32[]{:S(2)}) collective-permute-start(bf16[512,1024]{1,0:T(8,128)(2,1)} %x_ref.5), channel_id=1, source_target_pairs={{0,2},{1,3},{2,0},{3,1},{4,6},{5,7},{6,4},{7,5},{8,10},{9,11},{10,... | collective-permute-start | bytes 3145736 | tf_op jit(solution)/shard_map/ppermute | solution.py:730
  27.7 3.0 collective-permute-start.2
  27.7 25.6 %collective-permute-start.3 = (bf16[512,1024]{1,0:T(8,128)(2,1)S(1)}, bf16[512,1024]{1,0:T(8,128)(2,1)S(1)}, u32[]{:S(2)}, u32[]{:S(2)}) collective-permute-start(bf16[512,1024]{1,0:T(8,128)(2,1)S(1)} %copy-done.28), channel_id=1, source_target_pairs={{0,2},{1,3},{2,0},{3,1},{4,6},{5,7},{6,4},{7,5},{8,10},{9,11},{10,... | collective-permute-start | bytes 3145736 | tf_op jit(solution)/shard_map/ppermute | solution.py:730
  53.3 23.8 %copy-start.30 = (bf16[512,1024]{1,0:T(8,128)(2,1)}, bf16[512,1024]{1,0:T(8,128)(2,1)S(1)}, u32[]{:S(2)}) copy-start(bf16[512,1024]{1,0:T(8,128)(2,1)S(1)} %collective-permute-done.3.refs_2_) | copy-start | bytes 3145732
  53.3 2.9 collective-permute-start.4
  57.8 14.2 %collective-permute-start.5 = (bf16[256,1024]{1,0:T(8,128)(2,1)S(1)}, bf16[256,1024]{1,0:T(8,128)(2,1)}, u32[]{:S(2)}, u32[]{:S(2)}) collective-permute-start(bf16[256,1024]{1,0:T(8,128)(2,1)S(1)} %fusion.11), channel_id=1, source_target_pairs={{0,2},{1,3},{2,0},{3,1},{4,6},{5,7},{6,4},{7,5},{8,10},{9,11},{10,... | collective-permute-start | bytes 1572872 | tf_op jit(solution)/shard_map/ppermute | solution.py:730
  72.0 5.3 %collective-permute-start.6 = (bf16[2,256,1024]{2,1,0:T(8,128)(2,1)}, bf16[2,256,1024]{2,1,0:T(8,128)(2,1)}, u32[]{:S(2)}, u32[]{:S(2)}) collective-permute-start(bf16[2,256,1024]{2,1,0:T(8,128)(2,1)} %get-tuple-element.208), channel_id=1, source_target_pairs={{0,1},{1,0},{2,3},{3,2},{4,5},{5,4},{6,7},{7,6},{8,9},{9,8},{10,11... | collective-permute-start | bytes 3145736 | tf_op jit(solution)/shard_map/ppermute | solution.py:730
  72.1 7.4 %collective-permute-start.8 = (bf16[512,1024]{1,0:T(8,128)(2,1)S(1)}, bf16[512,1024]{1,0:T(8,128)(2,1)}, u32[]{:S(2)}, u32[]{:S(2)}) collective-permute-start(bf16[512,1024]{1,0:T(8,128)(2,1)S(1)} %copy-done.28), channel_id=1, source_target_pairs={{0,1},{1,0},{2,3},{3,2},{4,5},{5,4},{6,7},{7,6},{8,9},{9,8},{10,11... | collective-permute-start | bytes 3145736 | tf_op jit(solution)/shard_map/ppermute | solution.py:730
  75.4 4.1 %collective-permute-start.7 = (bf16[256,1024]{1,0:T(8,128)(2,1)}, bf16[256,1024]{1,0:T(8,128)(2,1)}, u32[]{:S(2)}, u32[]{:S(2)}) collective-permute-start(bf16[256,1024]{1,0:T(8,128)(2,1)} %get-tuple-element.209.refs_0_), channel_id=1, source_target_pairs={{0,1},{1,0},{2,3},{3,2},{4,5},{5,4},{6,7},{7,6},{8,9},{9,8},{10,11... | collective-permute-start | bytes 1572872 | tf_op jit(solution)/shard_map/ppermute | solution.py:730
  75.5 16.7 %collective-permute-start.9 = (bf16[256,1024]{1,0:T(8,128)(2,1)}, bf16[256,1024]{1,0:T(8,128)(2,1)S(1)}, u32[]{:S(2)}, u32[]{:S(2)}) collective-permute-start(bf16[256,1024]{1,0:T(8,128)(2,1)} %get-tuple-element.209.refs_0_), channel_id=1, source_target_pairs={{0,2},{1,3},{2,0},{3,1},{4,6},{5,7},{6,4},{7,5},{8,10},{9,11},{10,... | collective-permute-start | bytes 1572872 | tf_op jit(solution)/shard_map/ppermute | solution.py:730
  77.1 16.2 %collective-permute-start.11 = (bf16[512,1024]{1,0:T(8,128)(2,1)S(1)}, bf16[512,1024]{1,0:T(8,128)(2,1)S(1)}, u32[]{:S(2)}, u32[]{:S(2)}) collective-permute-start(bf16[512,1024]{1,0:T(8,128)(2,1)S(1)} %collective-permute-done.3.refs_2_), channel_id=1, source_target_pairs={{0,1},{1,0},{2,3},{3,2},{4,5},{5,4},{6,7},{7,6},{8,9},{9,8},{10,11... | collective-permute-start | bytes 3145736 | tf_op jit(solution)/shard_map/ppermute | solution.py:730
  92.2 2.0 collective-permute-start.10
  92.7 24.6 %collective-permute-start.12 = (bf16[256,1024]{1,0:T(8,128)(2,1)S(1)}, bf16[256,1024]{1,0:T(8,128)(2,1)}, u32[]{:S(2)}, u32[]{:S(2)}) collective-permute-start(bf16[256,1024]{1,0:T(8,128)(2,1)S(1)} %copy-done.54), channel_id=1, source_target_pairs={{0,2},{1,3},{2,0},{3,1},{4,6},{5,7},{6,4},{7,5},{8,10},{9,11},{10,... | collective-permute-start | bytes 1572872 | tf_op jit(solution)/shard_map/ppermute | solution.py:730
  119.9 2.1 collective-permute-start.13
  120.2 15.3 %collective-permute-start.14 = (bf16[256,1024]{1,0:T(8,128)(2,1)}, bf16[256,1024]{1,0:T(8,128)(2,1)S(1)}, u32[]{:S(2)}, u32[]{:S(2)}) collective-permute-start(bf16[256,1024]{1,0:T(8,128)(2,1)} %get-tuple-element.220.refs_0_), channel_id=1, source_target_pairs={{0,2},{1,3},{2,0},{3,1},{4,6},{5,7},{6,4},{7,5},{8,10},{9,11},{10,... | collective-permute-start | bytes 1572872 | tf_op jit(solution)/shard_map/ppermute | solution.py:730
  120.9 15.1 %collective-permute-start.15 = (bf16[256,1024]{1,0:T(8,128)(2,1)}, bf16[256,1024]{1,0:T(8,128)(2,1)S(1)}, u32[]{:S(2)}, u32[]{:S(2)}) collective-permute-start(bf16[256,1024]{1,0:T(8,128)(2,1)} %get-tuple-element.230), channel_id=1, source_target_pairs={{0,1},{1,0},{2,3},{3,2},{4,5},{5,4},{6,7},{7,6},{8,9},{9,8},{10,11... | collective-permute-start | bytes 1572872 | tf_op jit(solution)/shard_map/ppermute | solution.py:730
  135.6 2.0 collective-permute-start.16
  136.2 15.3 %collective-permute-start.17 = (bf16[256,1024]{1,0:T(8,128)(2,1)S(1)}, bf16[256,1024]{1,0:T(8,128)(2,1)S(1)}, u32[]{:S(2)}, u32[]{:S(2)}) collective-permute-start(bf16[256,1024]{1,0:T(8,128)(2,1)S(1)} %add_convert_fusion.6), channel_id=1, source_target_pairs={{0,2},{1,3},{2,0},{3,1},{4,6},{5,7},{6,4},{7,5},{8,10},{9,11},{10,... | collective-permute-start | bytes 1572872 | tf_op jit(solution)/shard_map/ppermute | solution.py:730
  136.9 15.0 %collective-permute-start.23 = (bf16[256,1024]{1,0:T(8,128)(2,1)S(1)}, bf16[256,1024]{1,0:T(8,128)(2,1)S(1)}, u32[]{:S(2)}, u32[]{:S(2)}) collective-permute-start(bf16[256,1024]{1,0:T(8,128)(2,1)S(1)} %copy-done.66), channel_id=1, source_target_pairs={{0,1},{1,0},{2,3},{3,2},{4,5},{5,4},{6,7},{7,6},{8,9},{9,8},{10,11... | collective-permute-start | bytes 1572872 | tf_op jit(solution)/shard_map/ppermute | solution.py:730
  151.5 5.3 %collective-permute-start.18 = (bf16[256,1024]{1,0:T(8,128)(2,1)}, bf16[256,1024]{1,0:T(8,128)(2,1)S(1)}, u32[]{:S(2)}, u32[]{:S(2)}) collective-permute-start(bf16[256,1024]{1,0:T(8,128)(2,1)} %get-tuple-element.240), channel_id=1, source_target_pairs={{0,1},{1,0},{2,3},{3,2},{4,5},{5,4},{6,7},{7,6},{8,9},{9,8},{10,11... | collective-permute-start | bytes 1572872 | tf_op jit(solution)/shard_map/ppermute | solution.py:730
  155.6 40.8 %collective-permute-start.31 = (bf16[256,1024]{1,0:T(8,128)(2,1)}, bf16[256,1024]{1,0:T(8,128)(2,1)S(1)}, u32[]{:S(2)}, u32[]{:S(2)}) collective-permute-start(bf16[256,1024]{1,0:T(8,128)(2,1)} %get-tuple-element.279.refs_17_.near_skip), channel_id=1, source_target_pairs={{0,1},{1,0},{2,3},{3,2},{4,5},{5,4},{6,7},{7,6},{8,9},{9,8},{10,11... | collective-permute-start | bytes 1572872 | tf_op jit(solution)/shard_map/ppermute | solution.py:730
  155.8 24.9 %collective-permute-start.24 = (bf16[256,1024]{1,0:T(8,128)(2,1)}, bf16[256,1024]{1,0:T(8,128)(2,1)}, u32[]{:S(2)}, u32[]{:S(2)}) collective-permute-start(bf16[256,1024]{1,0:T(8,128)(2,1)} %get-tuple-element.279.refs_17_.near_skip), channel_id=1, source_target_pairs={{0,2},{1,3},{2,0},{3,1},{4,6},{5,7},{6,4},{7,5},{8,10},{9,11},{10,... | collective-permute-start | bytes 1572872 | tf_op jit(solution)/shard_map/ppermute | solution.py:730
  156.6 25.6 %collective-permute-start.21 = (bf16[256,1024]{1,0:T(8,128)(2,1)}, bf16[256,1024]{1,0:T(8,128)(2,1)}, u32[]{:S(2)}, u32[]{:S(2)}) collective-permute-start(bf16[256,1024]{1,0:T(8,128)(2,1)} %get-tuple-element.247), channel_id=1, source_target_pairs={{0,1},{1,0},{2,3},{3,2},{4,5},{5,4},{6,7},{7,6},{8,9},{9,8},{10,11... | collective-permute-start | bytes 1572872 | tf_op jit(solution)/shard_map/ppermute | solution.py:730
  158.1 23.2 %collective-permute-start.22 = (bf16[256,1024]{1,0:T(8,128)(2,1)S(1)}, bf16[256,1024]{1,0:T(8,128)(2,1)S(1)}, u32[]{:S(2)}, u32[]{:S(2)}) collective-permute-start(bf16[256,1024]{1,0:T(8,128)(2,1)S(1)} %add_convert_fusion.5), channel_id=1, source_target_pairs={{0,2},{1,3},{2,0},{3,1},{4,6},{5,7},{6,4},{7,5},{8,10},{9,11},{10,... | collective-permute-start | bytes 1572872 | tf_op jit(solution)/shard_map/ppermute | solution.py:730
  169.5 35.8 %collective-permute-start.30 = (bf16[4,128,1152]{2,1,0:T(8,128)(2,1)}, bf16[4,128,1152]{2,1,0:T(8,128)(2,1)S(1)}, u32[]{:S(2)}, u32[]{:S(2)}) collective-permute-start(bf16[4,128,1152]{2,1,0:T(8,128)(2,1)} %get-tuple-element.256), channel_id=1, source_target_pairs={{0,4},{4,0},{8,12},{12,8},{16,20},{20,16},{24,28},{28,24},{1,5},{5... | collective-permute-start | bytes 3538952 | tf_op jit(solution)/shard_map/ppermute | solution.py:730
  180.7 15.9 %collective-permute-start.20 = (bf16[256,1024]{1,0:T(8,128)(2,1)}, bf16[256,1024]{1,0:T(8,128)(2,1)}, u32[]{:S(2)}, u32[]{:S(2)}) collective-permute-start(bf16[256,1024]{1,0:T(8,128)(2,1)} %get-tuple-element.244), channel_id=1, source_target_pairs={{0,1},{1,0},{2,3},{3,2},{4,5},{5,4},{6,7},{7,6},{8,9},{9,8},{10,11... | collective-permute-start | bytes 1572872 | tf_op jit(solution)/shard_map/ppermute | solution.py:730
  182.2 19.7 %collective-permute-start.28 = (bf16[256,1024]{1,0:T(8,128)(2,1)}, bf16[256,1024]{1,0:T(8,128)(2,1)}, u32[]{:S(2)}, u32[]{:S(2)}) collective-permute-start(bf16[256,1024]{1,0:T(8,128)(2,1)} %get-tuple-element.267), channel_id=1, source_target_pairs={{0,1},{1,0},{2,3},{3,2},{4,5},{5,4},{6,7},{7,6},{8,9},{9,8},{10,11... | collective-permute-start | bytes 1572872 | tf_op jit(solution)/shard_map/ppermute | solution.py:730
  185.1 14.5 %collective-permute-start.25 = (bf16[256,1024]{1,0:T(8,128)(2,1)}, bf16[256,1024]{1,0:T(8,128)(2,1)S(1)}, u32[]{:S(2)}, u32[]{:S(2)}) collective-permute-start(bf16[256,1024]{1,0:T(8,128)(2,1)} %get-tuple-element.260.refs_18_.far_skip), channel_id=1, source_target_pairs={{0,2},{1,3},{2,0},{3,1},{4,6},{5,7},{6,4},{7,5},{8,10},{9,11},{10,... | collective-permute-start | bytes 1572872 | tf_op jit(solution)/shard_map/ppermute | solution.py:730
  196.3 12.6 %collective-permute-start.33 = (bf16[256,1024]{1,0:T(8,128)(2,1)}, bf16[256,1024]{1,0:T(8,128)(2,1)S(1)}, u32[]{:S(2)}, u32[]{:S(2)}) collective-permute-start(bf16[256,1024]{1,0:T(8,128)(2,1)} %collective-permute-done.24.refs_21_), channel_id=1, source_target_pairs={{0,1},{1,0},{2,3},{3,2},{4,5},{5,4},{6,7},{7,6},{8,9},{9,8},{10,11... | collective-permute-start | bytes 1572872 | tf_op jit(solution)/shard_map/ppermute | solution.py:730
  196.6 13.4 %collective-permute-start.32 = (bf16[256,1024]{1,0:T(8,128)(2,1)S(1)}, bf16[256,1024]{1,0:T(8,128)(2,1)S(1)}, u32[]{:S(2)}, u32[]{:S(2)}) collective-permute-start(bf16[256,1024]{1,0:T(8,128)(2,1)S(1)} %copy-done.37), channel_id=1, source_target_pairs={{0,1},{1,0},{2,3},{3,2},{4,5},{5,4},{6,7},{7,6},{8,9},{9,8},{10,11... | collective-permute-start | bytes 1572872 | tf_op jit(solution)/shard_map/ppermute | solution.py:730
  199.6 11.4 %collective-permute-start.34 = (bf16[256,1024]{1,0:T(8,128)(2,1)S(1)}, bf16[256,1024]{1,0:T(8,128)(2,1)S(1)}, u32[]{:S(2)}, u32[]{:S(2)}) collective-permute-start(bf16[256,1024]{1,0:T(8,128)(2,1)S(1)} %collective-permute-done.25.refs_22_), channel_id=1, source_target_pairs={{0,1},{1,0},{2,3},{3,2},{4,5},{5,4},{6,7},{7,6},{8,9},{9,8},{10,11... | collective-permute-start | bytes 1572872 | tf_op jit(solution)/shard_map/ppermute | solution.py:730
  201.9 42.9 %collective-permute-start.36 = (bf16[4,128,1152]{2,1,0:T(8,128)(2,1)}, bf16[4,128,1152]{2,1,0:T(8,128)(2,1)}, u32[]{:S(2)}, u32[]{:S(2)}) collective-permute-start(bf16[4,128,1152]{2,1,0:T(8,128)(2,1)} %get-tuple-element.258), channel_id=1, source_target_pairs={{0,8},{4,12},{8,0},{12,4},{16,24},{20,28},{24,16},{28,20},{1,9},{5... | collective-permute-start | bytes 3538952 | tf_op jit(solution)/shard_map/ppermute | solution.py:730
  205.3 39.4 %collective-permute-start.37 = (bf16[4,128,1152]{2,1,0:T(8,128)(2,1)}, bf16[4,128,1152]{2,1,0:T(8,128)(2,1)}, u32[]{:S(2)}, u32[]{:S(2)}) collective-permute-start(bf16[4,128,1152]{2,1,0:T(8,128)(2,1)} %get-tuple-element.276), channel_id=1, source_target_pairs={{0,4},{4,0},{8,12},{12,8},{16,20},{20,16},{24,28},{28,24},{1,5},{5... | collective-permute-start | bytes 3538952 | tf_op jit(solution)/shard_map/ppermute | solution.py:730
  209.0 44.9 %collective-permute-start.26 = (bf16[256,1024]{1,0:T(8,128)(2,1)}, bf16[256,1024]{1,0:T(8,128)(2,1)}, u32[]{:S(2)}, u32[]{:S(2)}) collective-permute-start(bf16[256,1024]{1,0:T(8,128)(2,1)} %add_convert_fusion.4), channel_id=1, source_target_pairs={{0,2},{1,3},{2,0},{3,1},{4,6},{5,7},{6,4},{7,5},{8,10},{9,11},{10,... | collective-permute-start | bytes 1572872 | tf_op jit(solution)/shard_map/ppermute | solution.py:730
  210.1 43.8 %collective-permute-start.29 = (bf16[256,1024]{1,0:T(8,128)(2,1)}, bf16[256,1024]{1,0:T(8,128)(2,1)}, u32[]{:S(2)}, u32[]{:S(2)}) collective-permute-start(bf16[256,1024]{1,0:T(8,128)(2,1)} %add_convert_fusion.2), channel_id=1, source_target_pairs={{0,2},{1,3},{2,0},{3,1},{4,6},{5,7},{6,4},{7,5},{8,10},{9,11},{10,... | collective-permute-start | bytes 1572872 | tf_op jit(solution)/shard_map/ppermute | solution.py:730
  211.0 33.7 %collective-permute-start.35 = (bf16[2,128,1152]{2,1,0:T(8,128)(2,1)}, bf16[2,128,1152]{2,1,0:T(8,128)(2,1)S(1)}, u32[]{:S(2)}, u32[]{:S(2)}) collective-permute-start(bf16[2,128,1152]{2,1,0:T(8,128)(2,1)} %get-tuple-element.278), channel_id=1, source_target_pairs={{0,16},{4,20},{8,24},{12,28},{16,0},{20,4},{24,8},{28,12},{1,17},{... | collective-permute-start | bytes 1769480 | tf_op jit(solution)/shard_map/ppermute | solution.py:730
  249.3 27.4 %collective-permute-start.39 = (bf16[2,128,1152]{2,1,0:T(8,128)(2,1)}, bf16[2,128,1152]{2,1,0:T(8,128)(2,1)S(1)}, u32[]{:S(2)}, u32[]{:S(2)}) collective-permute-start(bf16[2,128,1152]{2,1,0:T(8,128)(2,1)} %get-tuple-element.292), channel_id=1, source_target_pairs={{0,4},{4,0},{8,12},{12,8},{16,20},{20,16},{24,28},{28,24},{1,5},{5... | collective-permute-start | bytes 1769480 | tf_op jit(solution)/shard_map/ppermute | solution.py:730
  251.5 27.7 %collective-permute-start.40 = (bf16[2,128,1152]{2,1,0:T(8,128)(2,1)}, bf16[2,128,1152]{2,1,0:T(8,128)(2,1)S(1)}, u32[]{:S(2)}, u32[]{:S(2)}) collective-permute-start(bf16[2,128,1152]{2,1,0:T(8,128)(2,1)} %get-tuple-element.294), channel_id=1, source_target_pairs={{0,16},{4,20},{8,24},{12,28},{16,0},{20,4},{24,8},{28,12},{1,17},{... | collective-permute-start | bytes 1769480 | tf_op jit(solution)/shard_map/ppermute | solution.py:730
  252.6 23.4 %collective-permute-start.41 = (bf16[4,128,512]{2,1,0:T(8,128)(2,1)}, bf16[4,128,512]{2,1,0:T(8,128)(2,1)S(1)}, u32[]{:S(2)}, u32[]{:S(2)}) collective-permute-start(bf16[4,128,512]{2,1,0:T(8,128)(2,1)} %get-tuple-element.296), channel_id=1, source_target_pairs={{0,4},{4,0},{8,12},{12,8},{16,20},{20,16},{24,28},{28,24},{1,5},{5... | collective-permute-start | bytes 1572872 | tf_op jit(solution)/shard_map/ppermute | solution.py:730
  253.8 25.4 %copy-start.6 = (bf16[4,128,512]{2,1,0:T(8,128)(2,1)S(1)}, bf16[4,128,512]{2,1,0:T(8,128)(2,1)}, u32[]{:S(2)}) copy-start(bf16[4,128,512]{2,1,0:T(8,128)(2,1)} %copy-done.5) | copy-start | bytes 1572868
  253.9 22.1 %collective-permute-start.38 = (bf16[1,128,1152]{2,1,0:T(8,128)(2,1)}, bf16[1,128,1152]{2,1,0:T(8,128)(2,1)S(1)}, u32[]{:S(2)}, u32[]{:S(2)}) collective-permute-start(bf16[1,128,1152]{2,1,0:T(8,128)(2,1)} %get-tuple-element.290), channel_id=1, source_target_pairs={{0,8},{4,12},{8,0},{12,4},{16,24},{20,28},{24,16},{28,20},{1,9},{5... | collective-permute-start | bytes 884744 | tf_op jit(solution)/shard_map/ppermute | solution.py:730
  291.6 5.1 %collective-permute-start.42 = (bf16[2,512,1024]{2,1,0:T(8,128)(2,1)}, bf16[2,512,1024]{2,1,0:T(8,128)(2,1)S(1)}, u32[]{:S(2)}, u32[]{:S(2)}) collective-permute-start(bf16[2,512,1024]{2,1,0:T(8,128)(2,1)} %get-tuple-element.305), channel_id=1, source_target_pairs={{0,1},{1,0},{2,3},{3,2},{4,5},{5,4},{6,7},{7,6},{8,9},{9,8},{10,11... | collective-permute-start | bytes 6291464 | tf_op jit(solution)/shard_map/ppermute | solution.py:730
  291.6 12.9 %collective-permute-start.19 = (bf16[256,1024]{1,0:T(8,128)(2,1)S(1)}, bf16[256,1024]{1,0:T(8,128)(2,1)S(1)}, u32[]{:S(2)}, u32[]{:S(2)}) collective-permute-start(bf16[256,1024]{1,0:T(8,128)(2,1)S(1)} %copy-done.65), channel_id=1, source_target_pairs={{0,1},{1,0},{2,3},{3,2},{4,5},{5,4},{6,7},{7,6},{8,9},{9,8},{10,11... | collective-permute-start | bytes 1572872 | tf_op jit(solution)/shard_map/ppermute | solution.py:730
  292.1 27.3 %collective-permute-start.27 = (bf16[256,1024]{1,0:T(8,128)(2,1)}, bf16[256,1024]{1,0:T(8,128)(2,1)S(1)}, u32[]{:S(2)}, u32[]{:S(2)}) collective-permute-start(bf16[256,1024]{1,0:T(8,128)(2,1)} %get-tuple-element.265), channel_id=1, source_target_pairs={{0,1},{1,0},{2,3},{3,2},{4,5},{5,4},{6,7},{7,6},{8,9},{9,8},{10,11... | collective-permute-start | bytes 1572872 | tf_op jit(solution)/shard_map/ppermute | solution.py:730
  292.2 13.3 %collective-permute-start.46 = (bf16[2,128,512]{2,1,0:T(8,128)(2,1)S(1)}, bf16[2,128,512]{2,1,0:T(8,128)(2,1)S(1)}, u32[]{:S(2)}, u32[]{:S(2)}) collective-permute-start(bf16[2,128,512]{2,1,0:T(8,128)(2,1)S(1)} %copy-done.26), channel_id=1, source_target_pairs={{0,8},{4,12},{8,0},{12,4},{16,24},{20,28},{24,16},{28,20},{1,9},{5... | collective-permute-start | bytes 786440 | tf_op jit(solution)/shard_map/ppermute | solution.py:730
  292.2 16.8 %collective-permute-start.44 = (bf16[1,128,1152]{2,1,0:T(8,128)(2,1)S(1)}, bf16[1,128,1152]{2,1,0:T(8,128)(2,1)S(1)}, u32[]{:S(2)}, u32[]{:S(2)}) collective-permute-start(bf16[1,128,1152]{2,1,0:T(8,128)(2,1)S(1)} %copy-done.24), channel_id=1, source_target_pairs={{0,16},{4,20},{8,24},{12,28},{16,0},{20,4},{24,8},{28,12},{1,17},{... | collective-permute-start | bytes 884744 | tf_op jit(solution)/shard_map/ppermute | solution.py:730
  299.1 35.2 %collective-permute-start.43 = (bf16[512,1024]{1,0:T(8,128)(2,1)S(1)}, bf16[512,1024]{1,0:T(8,128)(2,1)S(1)}, u32[]{:S(2)}, u32[]{:S(2)}) collective-permute-start(bf16[512,1024]{1,0:T(8,128)(2,1)S(1)} %fusion.10), channel_id=1, source_target_pairs={{0,2},{1,3},{2,0},{3,1},{4,6},{5,7},{6,4},{7,5},{8,10},{9,11},{10,... | collective-permute-start | bytes 3145736 | tf_op jit(solution)/shard_map/ppermute | solution.py:730
  304.5 10.4 %collective-permute-start.45 = (bf16[1,128,1152]{2,1,0:T(8,128)(2,1)S(1)}, bf16[1,128,1152]{2,1,0:T(8,128)(2,1)S(1)}, u32[]{:S(2)}, u32[]{:S(2)}) collective-permute-start(bf16[1,128,1152]{2,1,0:T(8,128)(2,1)S(1)} %copy-done.22), channel_id=1, source_target_pairs={{0,8},{4,12},{8,0},{12,4},{16,24},{20,28},{24,16},{28,20},{1,9},{5... | collective-permute-start | bytes 884744 | tf_op jit(solution)/shard_map/ppermute | solution.py:730
  305.5 9.4 %collective-permute-start.47 = (bf16[4,128,256]{2,1,0:T(8,128)(2,1)S(1)}, bf16[4,128,256]{2,1,0:T(8,128)(2,1)S(1)}, u32[]{:S(2)}, u32[]{:S(2)}) collective-permute-start(bf16[4,128,256]{2,1,0:T(8,128)(2,1)S(1)} %get-tuple-element.318), channel_id=1, source_target_pairs={{0,4},{4,0},{8,12},{12,8},{16,20},{20,16},{24,28},{28,24},{1,5},{5... | collective-permute-start | bytes 786440 | tf_op jit(solution)/shard_map/ppermute | solution.py:730
  307.3 21.5 %copy-start.17 = (f32[1,1024]{1,0:T(1,128)S(1)}, f32[1,1024]{1,0:T(1,128)}, u32[]{:S(2)}) copy-start(f32[1,1024]{1,0:T(1,128)} %get-tuple-element.307.refs_0_) | copy-start | bytes 12292
  307.4 21.5 %copy-start.18 = (f32[1,1024]{1,0:T(1,128)S(1)}, f32[1,1024]{1,0:T(1,128)}, u32[]{:S(2)}) copy-start(f32[1,1024]{1,0:T(1,128)} %get-tuple-element.308.refs_1_) | copy-start | bytes 12292
  307.4 21.5 %copy-start.19 = (f32[1,128]{1,0:T(1,128)S(1)}, f32[1,128]{1,0:T(1,128)}, u32[]{:S(2)}) copy-start(f32[1,128]{1,0:T(1,128)} %get-tuple-element.287.refs_2_) | copy-start | bytes 1540
  307.4 21.5 %copy-start.20 = (f32[1,128]{1,0:T(1,128)S(1)}, f32[1,128]{1,0:T(1,128)}, u32[]{:S(2)}) copy-start(f32[1,128]{1,0:T(1,128)} %get-tuple-element.309.refs_3_) | copy-start | bytes 1540
  317.5 7.9 %collective-permute-start.48 = (bf16[1,128,512]{2,1,0:T(8,128)(2,1)S(1)}, bf16[1,128,512]{2,1,0:T(8,128)(2,1)S(1)}, u32[]{:S(2)}, u32[]{:S(2)}) collective-permute-start(bf16[1,128,512]{2,1,0:T(8,128)(2,1)S(1)} %get-tuple-element.321), channel_id=1, source_target_pairs={{0,16},{4,20},{8,24},{12,28},{16,0},{20,4},{24,8},{28,12},{1,17},{... | collective-permute-start | bytes 393224 | tf_op jit(solution)/shard_map/ppermute | solution.py:730
  317.5 7.9 %collective-permute-start.49 = (bf16[2,128,256]{2,1,0:T(8,128)(2,1)S(1)}, bf16[2,128,256]{2,1,0:T(8,128)(2,1)S(1)}, u32[]{:S(2)}, u32[]{:S(2)}) collective-permute-start(bf16[2,128,256]{2,1,0:T(8,128)(2,1)S(1)} %get-tuple-element.323), channel_id=1, source_target_pairs={{0,8},{4,12},{8,0},{12,4},{16,24},{20,28},{24,16},{28,20},{1,9},{5... | collective-permute-start | bytes 393224 | tf_op jit(solution)/shard_map/ppermute | solution.py:730
  327.4 5.6 %collective-permute-start.50 = (bf16[1,128,256]{2,1,0:T(8,128)(2,1)S(1)}, bf16[1,128,256]{2,1,0:T(8,128)(2,1)S(1)}, u32[]{:S(2)}, u32[]{:S(2)}) collective-permute-start(bf16[1,128,256]{2,1,0:T(8,128)(2,1)S(1)} %get-tuple-element.326), channel_id=1, source_target_pairs={{0,16},{4,20},{8,24},{12,28},{16,0},{20,4},{24,8},{28,12},{1,17},{... | collective-permute-start | bytes 196616 | tf_op jit(solution)/shard_map/ppermute | solution.py:730
  340.2 3.3 collective-permute-start.53
  340.2 3.9 %collective-permute-start.52 = (f32[1,2304]{1,0:T(1,128)}, f32[1,2304]{1,0:T(1,128)S(1)}, u32[]{:S(2)}, u32[]{:S(2)}) collective-permute-start(f32[1,2304]{1,0:T(1,128)} %get-tuple-element.330), channel_id=1, source_target_pairs={{0,2},{1,3},{2,0},{3,1},{4,6},{5,7},{6,4},{7,5},{8,10},{9,11},{10,... | collective-permute-start | bytes 27656 | tf_op jit(solution)/shard_map/ppermute | solution.py:730
  341.6 2.6 collective-permute-start.51
  344.9 4.6 %collective-permute-start.56 = (f32[1,2304]{1,0:T(1,128)S(1)}, f32[1,2304]{1,0:T(1,128)S(1)}, u32[]{:S(2)}, u32[]{:S(2)}) collective-permute-start(f32[1,2304]{1,0:T(1,128)S(1)} %add_add_fusion.1), channel_id=1, source_target_pairs={{0,12},{4,8},{8,4},{12,0},{16,28},{20,24},{24,20},{28,16},{1,13},{... | collective-permute-start | bytes 27656 | tf_op jit(solution)/shard_map/ppermute | solution.py:730
  346.3 3.8 %collective-permute-start.55 = (f32[1,2304]{1,0:T(1,128)S(1)}, f32[1,2304]{1,0:T(1,128)S(1)}, u32[]{:S(2)}, u32[]{:S(2)}) collective-permute-start(f32[1,2304]{1,0:T(1,128)S(1)} %add_add_fusion.1), channel_id=1, source_target_pairs={{0,8},{4,12},{8,0},{12,4},{16,24},{20,28},{24,16},{28,20},{1,9},{5... | collective-permute-start | bytes 27656 | tf_op jit(solution)/shard_map/ppermute | solution.py:730
  348.4 3.7 collective-permute-start.54
  352.1 4.6 %collective-permute-start.57 = (f32[1,2304]{1,0:T(1,128)S(1)}, f32[1,2304]{1,0:T(1,128)S(1)}, u32[]{:S(2)}, u32[]{:S(2)}) collective-permute-start(f32[1,2304]{1,0:T(1,128)S(1)} %add_add_fusion), channel_id=1, source_target_pairs={{0,16},{4,20},{8,24},{12,28},{16,0},{20,4},{24,8},{28,12},{1,17},{... | collective-permute-start | bytes 27656 | tf_op jit(solution)/shard_map/ppermute | solution.py:730
  (64 other events, 386.4 us)
